TPU v7x, 32 devices: a whole 2x2x4 slice. The times are simulated.
32 devices in a mesh: dp: 2 (over x), seq: 4 (over y, core), tensor: 4 (over z).
Axes of the slice: x: 2, y: 2, z: 4, core: 2. Of those that a mesh axis runs over, the one named last changes fastest.
Arguments:
- tokens: bfloat16 [2, 2, 3072, 2048], P(None, 'dp', 'seq'), may hold values from -6 to 6
- cotangent: bfloat16 [2, 2, 3072, 2048], P(None, 'dp', 'seq'), may hold values from -6 to 6
- w_query: bfloat16 [2048, 2048], P(('dp', 'seq'), 'tensor'), may hold values from -0.125 to 0.125
- w_key: bfloat16 [2048, 2048], P(('dp', 'seq'), 'tensor'), may hold values from -0.125 to 0.125
- w_value: bfloat16 [2048, 2048], P(('dp', 'seq'), 'tensor'), may hold values from -0.125 to 0.125
- w_out: bfloat16 [2048, 2048], P('tensor', ('dp', 'seq')), may hold values from -0.125 to 0.125
- w_gate: bfloat16 [2048, 8192], P(('dp', 'seq'), 'tensor'), may hold values from -0.125 to 0.125
- w_up: bfloat16 [2048, 8192], P(('dp', 'seq'), 'tensor'), may hold values from -0.125 to 0.125
- w_down: bfloat16 [8192, 2048], P('tensor', ('dp', 'seq')), may hold values from -0.0625 to 0.0625
- query_gain: bfloat16 [16, 128], P('tensor', ('dp', 'seq')), may hold values from 0.25 to 1.75
- key_gain: bfloat16 [16, 128], P('tensor', ('dp', 'seq')), may hold values from 0.25 to 1.75
- attn_gain: bfloat16 [2048], P(('dp', 'seq')), may hold values from 0.25 to 1.75
- mlp_gain: bfloat16 [2048], P(('dp', 'seq')), may hold values from 0.25 to 1.75
- parent_of: int32 [2, 2, 10], P(None, 'dp'), may hold values from 0 to 3, as said below
- seg_length: int32 [2, 2, 10], P(None, 'dp'), may hold values from 128 to 768, as said below
Outputs:
- layer_out: bfloat16 [2, 2, 3072, 2048], P(None, 'dp', 'seq')
- input_grad: float32 [2, 2, 3072, 2048], P(None, 'dp', 'seq')
- g_query: float32 [2048, 2048], P(('dp', 'seq'), 'tensor')
- g_key: float32 [2048, 2048], P(('dp', 'seq'), 'tensor')
- g_value: float32 [2048, 2048], P(('dp', 'seq'), 'tensor')
- g_out: float32 [2048, 2048], P('tensor', ('dp', 'seq'))
- g_gate: float32 [2048, 8192], P(('dp', 'seq'), 'tensor')
- g_up: float32 [2048, 8192], P(('dp', 'seq'), 'tensor')
- g_down: float32 [8192, 2048], P('tensor', ('dp', 'seq'))
- g_query_gain: float32 [16, 128], P('tensor', ('dp', 'seq'))
- g_key_gain: float32 [16, 128], P('tensor', ('dp', 'seq'))
- g_attn_gain: float32 [2048], P(('dp', 'seq'))
- g_mlp_gain: float32 [2048], P(('dp', 'seq'))
Inputs may be any that keep to these rules, and one draw needn't show every extreme that they name: `parent_of`: segments 0 to 3 have parent 0; each of the segments 1 to 3 is the parent of exactly two of the segments 3 + 1 to 9. `seg_length`: the trunk (segment 0) has 384 valid positions or more, every other segment 256 / 2 or more and 256 at most.
All inputs are finite; a program needn't handle non-finite values.
Results may differ from a plain program's by a relative error of at most 0.02.
Values may be sent and summed in bfloat16 or wider, within the bound.
A program may use at most 384 MiB of HBM per device.

v0:
```python
import math

import jax
import jax.numpy as jnp
from jax import lax
from jax.sharding import PartitionSpec as P

NH = 16
HD = 128
BLOCK = 256


norm_eps = 1e-06
masked_score = -1e30


def matmul(left, right):
    return jnp.dot(left, right, preferred_element_type=jnp.float32)


def left_t(left, right):
    return lax.dot_general(
        left, right, (((0,), (0,)), ((), ())), preferred_element_type=jnp.float32
    )


def right_t(left, right):
    return lax.dot_general(
        left, right, (((1,), (1,)), ((), ())), preferred_element_type=jnp.float32
    )


def lookup_parent(segments, parents, seg_count):
    picked = segments[:, None] == jnp.arange(seg_count, dtype=jnp.int32)[None, :]
    return jnp.sum(jnp.where(picked, parents[None, :], 0), axis=1)


def tree_tables(parents, lengths, n_blocks, block_size):
    seg_count = parents.shape[0]
    branches = (seg_count - 1) // 3
    trunk_blocks = n_blocks - 3 * branches
    blocks = jnp.arange(n_blocks, dtype=jnp.int32)
    seg_of = jnp.maximum(blocks - trunk_blocks + 1, 0)
    seg_start = jnp.where(blocks < trunk_blocks, 0, blocks)
    seg_pick = seg_of[:, None] == jnp.arange(seg_count, dtype=jnp.int32)[None, :]
    seg_span = jnp.sum(jnp.where(seg_pick, lengths[None, :], 0), axis=1)
    offset = (blocks - seg_start)[:, None] * block_size + jnp.arange(block_size, dtype=jnp.int32)[
        None, :
    ]
    valid_keys = (offset < seg_span[:, None]).reshape(-1)
    parent_one = lookup_parent(seg_of, parents, seg_count)
    parent_two = lookup_parent(parent_one, parents, seg_count)
    key_seg = seg_of[None, :]
    vis_table = (
        (key_seg == seg_of[:, None])
        | (key_seg == parent_one[:, None])
        | (key_seg == parent_two[:, None])
    )
    return (vis_table, valid_keys)


def key_tables(vis_table, valid_keys, key_pos, key_ok):
    n_blocks = vis_table.shape[0]
    key_block = key_pos // BLOCK
    picked = key_block[None, None, :] == jnp.arange(n_blocks, dtype=jnp.int32)[None, :, None]
    key_table = jnp.any(vis_table[:, :, None] & picked, axis=1)
    key_valid = jnp.take(valid_keys, key_pos) & key_ok
    return (key_table, key_valid)


def block_view(key_table, key_valid, key_pos, query_first, q_block):
    row_blocks = q_block // BLOCK
    rows = lax.dynamic_slice_in_dim(key_table, query_first // BLOCK, row_blocks, 0)
    key_count = rows.shape[1]
    visible = jnp.broadcast_to(rows[:, None, :], (row_blocks, BLOCK, key_count)).reshape(
        q_block, key_count
    )
    query_pos = query_first + jnp.arange(q_block, dtype=jnp.int32)
    return visible & key_valid[None, :] & (key_pos[None, :] <= query_pos[:, None])


def head_scores(query_rows, key_heads, visible):
    raw_scores = jnp.einsum(
        "qhd,khd->hqk", query_rows, key_heads, preferred_element_type=jnp.float32
    ) * HD ** (-0.5)
    return jnp.where(visible[None], raw_scores, masked_score)


def attend_forward(
    query_heads, key_heads, value_heads, key_table, key_valid, key_pos, first_row, q_block
):
    n_rows = query_heads.shape[0]

    def one_block(block_index):
        start_row = block_index * q_block
        query_rows = lax.dynamic_slice_in_dim(query_heads, start_row, q_block, 0)
        visible = block_view(key_table, key_valid, key_pos, first_row + start_row, q_block)
        scores = head_scores(query_rows, key_heads, visible)
        top_score = jnp.max(scores, axis=-1, keepdims=True)
        exp_scores = jnp.exp(scores - top_score)
        exp_total = jnp.sum(exp_scores, axis=-1, keepdims=True)
        prob_low = (exp_scores / exp_total).astype(jnp.bfloat16)
        attended = jnp.einsum(
            "hqk,khd->qhd", prob_low, value_heads, preferred_element_type=jnp.float32
        )
        return (attended, (top_score + jnp.log(exp_total))[..., 0])

    attended, log_total = lax.map(one_block, jnp.arange(n_rows // q_block, dtype=jnp.int32))
    return (attended.reshape(n_rows, -1), log_total)


def attend_backward(
    query_heads,
    key_heads,
    value_heads,
    grad_heads,
    log_total,
    key_table,
    key_valid,
    key_pos,
    first_row,
    q_block,
):
    n_rows = query_heads.shape[0]
    score_scale = HD ** (-0.5)
    key_zero = jnp.zeros(key_heads.shape, jnp.float32)

    def one_block(carry, block_index):
        key_grad, value_grad = carry
        start_row = block_index * q_block
        query_rows = lax.dynamic_slice_in_dim(query_heads, start_row, q_block, 0)
        grad_rows = lax.dynamic_slice_in_dim(grad_heads, start_row, q_block, 0)
        visible = block_view(key_table, key_valid, key_pos, first_row + start_row, q_block)
        scores = head_scores(query_rows, key_heads, visible)
        prob_rows = jnp.exp(scores - log_total[block_index][..., None])
        prob_low = prob_rows.astype(jnp.bfloat16)
        prob_grad = jnp.einsum(
            "qhd,khd->hqk", grad_rows, value_heads, preferred_element_type=jnp.float32
        )
        row_inner = jnp.sum(prob_rows * prob_grad, axis=-1, keepdims=True)
        score_low = (prob_rows * (prob_grad - row_inner)).astype(jnp.bfloat16)
        query_grad = (
            jnp.einsum("hqk,khd->qhd", score_low, key_heads, preferred_element_type=jnp.float32)
            * score_scale
        )
        key_grad = (
            key_grad
            + jnp.einsum("hqk,qhd->khd", score_low, query_rows, preferred_element_type=jnp.float32)
            * score_scale
        )
        value_grad = value_grad + jnp.einsum(
            "hqk,qhd->khd", prob_low, grad_rows, preferred_element_type=jnp.float32
        )
        return ((key_grad, value_grad), query_grad)

    (key_grad, value_grad), query_grad = lax.scan(
        one_block, (key_zero, key_zero), jnp.arange(n_rows // q_block, dtype=jnp.int32)
    )
    return (query_grad.reshape(n_rows, -1), key_grad, value_grad)


def fetch_weights(owned):
    return (
        lax.all_gather(owned[0], ("dp", "seq"), axis=0, tiled=True),
        lax.all_gather(owned[1], ("dp", "seq"), axis=0, tiled=True),
        lax.all_gather(owned[2], ("dp", "seq"), axis=0, tiled=True),
        lax.all_gather(owned[3], ("dp", "seq"), axis=1, tiled=True),
        lax.all_gather(owned[4], ("dp", "seq"), axis=0, tiled=True),
        lax.all_gather(owned[5], ("dp", "seq"), axis=0, tiled=True),
        lax.all_gather(owned[6], ("dp", "seq"), axis=1, tiled=True),
        lax.all_gather(owned[7], ("dp", "seq"), axis=1, tiled=True),
        lax.all_gather(owned[8], ("dp", "seq"), axis=1, tiled=True),
        lax.all_gather(owned[9], ("dp", "seq"), axis=0, tiled=True),
        lax.all_gather(owned[10], ("dp", "seq"), axis=0, tiled=True),
    )


def share_grads(grads):
    return (
        lax.psum_scatter(
            grads[0].astype(jnp.bfloat16), ("dp", "seq"), scatter_dimension=0, tiled=True
        ).astype(jnp.float32),
        lax.psum_scatter(
            grads[1].astype(jnp.bfloat16), ("dp", "seq"), scatter_dimension=0, tiled=True
        ).astype(jnp.float32),
        lax.psum_scatter(
            grads[2].astype(jnp.bfloat16), ("dp", "seq"), scatter_dimension=0, tiled=True
        ).astype(jnp.float32),
        lax.psum_scatter(
            grads[3].astype(jnp.bfloat16), ("dp", "seq"), scatter_dimension=1, tiled=True
        ).astype(jnp.float32),
        lax.psum_scatter(
            grads[4].astype(jnp.bfloat16), ("dp", "seq"), scatter_dimension=0, tiled=True
        ).astype(jnp.float32),
        lax.psum_scatter(
            grads[5].astype(jnp.bfloat16), ("dp", "seq"), scatter_dimension=0, tiled=True
        ).astype(jnp.float32),
        lax.psum_scatter(
            grads[6].astype(jnp.bfloat16), ("dp", "seq"), scatter_dimension=1, tiled=True
        ).astype(jnp.float32),
        lax.psum_scatter(
            grads[7].astype(jnp.bfloat16), ("dp", "seq"), scatter_dimension=1, tiled=True
        ).astype(jnp.float32),
        lax.psum_scatter(
            grads[8].astype(jnp.bfloat16), ("dp", "seq"), scatter_dimension=1, tiled=True
        ).astype(jnp.float32),
        lax.psum_scatter(
            grads[9].astype(jnp.bfloat16), ("dp", "seq"), scatter_dimension=0, tiled=True
        ).astype(jnp.float32),
        lax.psum_scatter(
            grads[10].astype(jnp.bfloat16), ("dp", "seq"), scatter_dimension=0, tiled=True
        ).astype(jnp.float32),
    )


def per_device(
    tokens,
    cotangent,
    w_query,
    w_key,
    w_value,
    w_out,
    w_gate,
    w_up,
    w_down,
    query_gain,
    key_gain,
    attn_gain,
    mlp_gain,
    parent_of,
    seg_length,
):
    owned = (
        w_query,
        w_key,
        w_value,
        w_out,
        w_gate,
        w_up,
        w_down,
        query_gain,
        key_gain,
        attn_gain,
        mlp_gain,
    )
    tok_rows = tokens.shape[2]
    seq_count = lax.axis_size("seq")
    seq_place = lax.axis_index("seq")
    n_blocks = tok_rows // BLOCK * seq_count
    first_row = seq_place * tok_rows
    q_block = math.gcd(512, tok_rows)
    full_width = NH * HD
    heads_here = w_query.shape[1] // HD
    key_pos = jnp.arange(n_blocks * BLOCK, dtype=jnp.int32)
    key_ok = jnp.ones((n_blocks * BLOCK,), jnp.bool_)
    totals = tuple((jnp.zeros(item.shape, jnp.float32) for item in owned))
    out_rows = []
    grad_rows = []
    for micro_step in range(tokens.shape[0]):
        gathered = fetch_weights(owned)
        (
            wq_full,
            wk_full,
            wv_full,
            wo_full,
            wg_full,
            wu_full,
            wd_full,
            qg_full,
            kg_full,
            ga_full,
            gm_full,
        ) = gathered
        vis_table, valid_keys = tree_tables(
            parent_of[micro_step, 0], seg_length[micro_step, 0], n_blocks, BLOCK
        )
        key_table, key_valid = key_tables(vis_table, valid_keys, key_pos, key_ok)
        inputs = tokens[micro_step, 0]
        q_raw = matmul(inputs, wq_full)
        k_raw = matmul(inputs, wk_full)
        v_raw = matmul(inputs, wv_full)
        q_square, k_square = lax.psum(
            (jnp.sum(q_raw * q_raw, axis=1), jnp.sum(k_raw * k_raw, axis=1)), "tensor"
        )
        q_inv = lax.rsqrt(q_square / full_width + norm_eps)[:, None]
        k_inv = lax.rsqrt(k_square / full_width + norm_eps)[:, None]
        q_unit = q_raw * q_inv
        k_unit = k_raw * k_inv
        q_gain_row = qg_full.reshape(-1).astype(jnp.float32)
        k_gain_row = kg_full.reshape(-1).astype(jnp.float32)
        q_low = (q_unit * q_gain_row).astype(jnp.bfloat16)
        k_low = (k_unit * k_gain_row).astype(jnp.bfloat16)
        v_low = v_raw.astype(jnp.bfloat16)
        key_rows, value_rows = (
            lax.all_gather(k_low, "seq", axis=0, tiled=True),
            lax.all_gather(v_low, "seq", axis=0, tiled=True),
        )
        query_heads = q_low.reshape(tok_rows, heads_here, HD)
        key_heads = key_rows.reshape(-1, heads_here, HD)
        value_heads = value_rows.reshape(-1, heads_here, HD)
        attended, log_total = attend_forward(
            query_heads, key_heads, value_heads, key_table, key_valid, key_pos, first_row, q_block
        )
        attn_low = attended.astype(jnp.bfloat16)
        attn_proj = lax.psum(matmul(attn_low, wo_full), "tensor")
        attn_inv = lax.rsqrt(jnp.mean(attn_proj * attn_proj, axis=1, keepdims=True) + norm_eps)
        attn_unit = attn_proj * attn_inv
        ga_row = ga_full.astype(jnp.float32)
        hidden = inputs.astype(jnp.float32) + attn_unit * ga_row
        hidden_low = hidden.astype(jnp.bfloat16)
        gate_pre = matmul(hidden_low, wg_full)
        up_pre = matmul(hidden_low, wu_full)
        gate_sig = jax.nn.sigmoid(gate_pre)
        gate_act = gate_pre * gate_sig
        inner_low = (gate_act * up_pre).astype(jnp.bfloat16)
        mlp_proj = lax.psum(matmul(inner_low, wd_full), "tensor")
        mlp_inv = lax.rsqrt(jnp.mean(mlp_proj * mlp_proj, axis=1, keepdims=True) + norm_eps)
        mlp_unit = mlp_proj * mlp_inv
        gm_row = gm_full.astype(jnp.float32)
        out_rows.append((hidden + mlp_unit * gm_row).astype(jnp.bfloat16))
        gathered = fetch_weights(owned)
        (
            wq_full,
            wk_full,
            wv_full,
            wo_full,
            wg_full,
            wu_full,
            wd_full,
            qg_full,
            kg_full,
            ga_full,
            gm_full,
        ) = gathered
        out_grad = cotangent[micro_step, 0].astype(jnp.float32)
        gm_grad = jnp.sum(out_grad * mlp_unit, axis=0)
        unit_grad = out_grad * gm_row
        mlp_low = (
            mlp_inv * (unit_grad - mlp_unit * jnp.mean(unit_grad * mlp_unit, axis=1, keepdims=True))
        ).astype(jnp.bfloat16)
        wd_grad = left_t(inner_low, mlp_low)
        inner_grad = right_t(mlp_low, wd_full)
        gate_low = (inner_grad * up_pre * gate_sig * (1.0 + gate_pre * (1.0 - gate_sig))).astype(
            jnp.bfloat16
        )
        up_low = (inner_grad * gate_act).astype(jnp.bfloat16)
        wg_grad = left_t(hidden_low, gate_low)
        wu_grad = left_t(hidden_low, up_low)
        hidden_grad = out_grad + lax.psum(
            right_t(gate_low, wg_full) + right_t(up_low, wu_full), "tensor"
        )
        ga_grad = jnp.sum(hidden_grad * attn_unit, axis=0)
        unit_grad = hidden_grad * ga_row
        proj_low = (
            attn_inv
            * (unit_grad - attn_unit * jnp.mean(unit_grad * attn_unit, axis=1, keepdims=True))
        ).astype(jnp.bfloat16)
        wo_grad = left_t(attn_low, proj_low)
        attn_grad_low = right_t(proj_low, wo_full).astype(jnp.bfloat16)
        query_grad, key_grad, value_grad = attend_backward(
            query_heads,
            key_heads,
            value_heads,
            attn_grad_low.reshape(tok_rows, heads_here, HD),
            log_total,
            key_table,
            key_valid,
            key_pos,
            first_row,
            q_block,
        )
        key_flat = key_grad.reshape(-1, heads_here * HD)
        value_flat = value_grad.reshape(-1, heads_here * HD)
        key_share, value_share = (
            lax.psum_scatter(
                key_flat.astype(jnp.bfloat16), "seq", scatter_dimension=0, tiled=True
            ).astype(jnp.float32),
            lax.psum_scatter(
                value_flat.astype(jnp.bfloat16), "seq", scatter_dimension=0, tiled=True
            ).astype(jnp.float32),
        )
        qg_grad = jnp.sum(query_grad * q_unit, axis=0)
        kg_grad = jnp.sum(key_share * k_unit, axis=0)
        q_scaled = query_grad * q_gain_row
        k_scaled = key_share * k_gain_row
        q_inner, k_inner = lax.psum(
            (jnp.sum(q_scaled * q_unit, axis=1), jnp.sum(k_scaled * k_unit, axis=1)), "tensor"
        )
        qr_low = (q_inv * (q_scaled - q_unit * (q_inner / full_width)[:, None])).astype(
            jnp.bfloat16
        )
        kr_low = (k_inv * (k_scaled - k_unit * (k_inner / full_width)[:, None])).astype(
            jnp.bfloat16
        )
        vr_low = value_share.astype(jnp.bfloat16)
        wq_grad = left_t(inputs, qr_low)
        wk_grad = left_t(inputs, kr_low)
        wv_grad = left_t(inputs, vr_low)
        back_sum = right_t(qr_low, wq_full) + right_t(kr_low, wk_full) + right_t(vr_low, wv_full)
        grad_rows.append(
            hidden_grad + lax.psum(back_sum.astype(jnp.bfloat16), "tensor").astype(jnp.float32)
        )
        step_grads = (
            wq_grad,
            wk_grad,
            wv_grad,
            wo_grad,
            wg_grad,
            wu_grad,
            wd_grad,
            qg_grad.reshape(heads_here, HD),
            kg_grad.reshape(heads_here, HD),
            ga_grad,
            gm_grad,
        )
        shares = share_grads(step_grads)
        totals = tuple((left_sum + right_sum for left_sum, right_sum in zip(totals, shares)))
    layer_out = jnp.stack(out_rows)[:, None]
    input_grad = jnp.stack(grad_rows)[:, None]
    return (
        layer_out,
        input_grad,
        totals[0],
        totals[1],
        totals[2],
        totals[3],
        totals[4],
        totals[5],
        totals[6],
        totals[7],
        totals[8],
        totals[9],
        totals[10],
    )


def solution(mesh):
    return jax.shard_map(
        per_device,
        mesh=mesh,
        in_specs=(
            P(None, "dp", "seq", None),
            P(None, "dp", "seq", None),
            P(("dp", "seq"), "tensor"),
            P(("dp", "seq"), "tensor"),
            P(("dp", "seq"), "tensor"),
            P("tensor", ("dp", "seq")),
            P(("dp", "seq"), "tensor"),
            P(("dp", "seq"), "tensor"),
            P("tensor", ("dp", "seq")),
            P("tensor", ("dp", "seq")),
            P("tensor", ("dp", "seq")),
            P(("dp", "seq")),
            P(("dp", "seq")),
            P(None, "dp", None),
            P(None, "dp", None),
        ),
        out_specs=(
            P(None, "dp", "seq", None),
            P(None, "dp", "seq", None),
            P(("dp", "seq"), "tensor"),
            P(("dp", "seq"), "tensor"),
            P(("dp", "seq"), "tensor"),
            P("tensor", ("dp", "seq")),
            P(("dp", "seq"), "tensor"),
            P(("dp", "seq"), "tensor"),
            P("tensor", ("dp", "seq")),
            P("tensor", ("dp", "seq")),
            P("tensor", ("dp", "seq")),
            P(("dp", "seq")),
            P(("dp", "seq")),
        ),
        check_vma=False,
    )
```

profile of v0, /device:TPU:0, one launch (start us, length us, event | category | flops | bytes accessed | tf_op | source)
XLA Modules:
  0.0 3694.5 jit_solution(4877060356997893607)
XLA Ops:
  20.0 20.5 all-gather.16.cloned.1.call-done
  49.5 20.9 all-gather.18.cloned.1.call-done
  80.9 18.7 all-reduce.5
  125.4 19.4 gather_fusion
  144.8 19.4 gather_fusion.1
  181.6 46.5 %while.64 = (s32[]{:T(128)}, bf16[3,256,4,128]{3,1,2,0:T(8,128)(2,1)}, f32[3,4,256]{2,1,0:T(4,128)S(1)}, s32[3]{0:T(128)S(1)}, s32[]{:T(128)}, /*index=5*/pred[1...) while((s32[]{:T(128)}, ...), condition=%wide.region_11.13_spmd.clone, body=%wide.region_8.12_spmd.clone.sunk | while | flops 1649936640 | bytes 63755244 | solution.py:108
  238.0 46.1 %while.65 = (s32[]{:T(128)}, bf16[3,256,4,128]{3,1,2,0:T(8,128)(2,1)S(1)}, f32[3,4,256]{2,1,0:T(4,128)S(1)}, s32[3]{0:T(128)S(1)}, s32[]{:T(128)}, /*index=5*/pr...) while((s32[]{:T(128)}, ...), condition=%wide.region_27.29_spmd.clone, body=%wide.region_24.28_spmd.clone.sunk | while | flops 1649936640 | bytes 60608976 | solution.py:108
  307.5 414.3 %all-reduce.20.cloned.1.call-done = (f32[768,2048]{1,0:T(8,128)}, f32[768,2048]{1,0:T(8,128)}) async-done(((f32[768,2048]{1,0:T(8,128)}, f32[768,2048]{1,0:T(8,128)}), (f32[768,2048]{1,0:T(8,128)}, f32[768,2048]{1,0:T(8,128)})) %all-reduce.20.cloned.1.call-update) | async-done | bytes 12582928 | tf_op jit(solution)/shard_map/psum | solution.py:305
  734.2 42.8 %all-gather.28.cloned.1.call-done = bf16[2048,2048]{1,0:T(8,128)(2,1)} async-done(((bf16[256,2048]{1,0:T(8,128)(2,1)}), bf16[2048,2048]{1,0:T(8,128)(2,1)}) %all-gather.28.cloned.1.call-update) | async-done | bytes 8388624 | tf_op jit(solution)/shard_map/all_gather | solution.py:168
  797.4 35.8 all-gather.30.cloned.1.call-done
  833.3 14.3 multiply_convert_fusion.9
  857.0 34.0 all-gather.32.cloned.1.call-done
  921.2 417.5 %all-reduce.18.cloned.1.call-done = (f32[768,2048]{1,0:T(8,128)}, f32[768,2048]{1,0:T(8,128)}) async-done(((f32[768,2048]{1,0:T(8,128)}, f32[768,2048]{1,0:T(8,128)}), (f32[768,2048]{1,0:T(8,128)}, f32[768,2048]{1,0:T(8,128)})) %all-reduce.18.cloned.1.call-update) | async-done | bytes 12582928 | tf_op jit(solution)/shard_map/psum | solution.py:316
  1355.0 17.6 multiply_convert_fusion.6
  1384.5 15.3 multiply_convert_fusion.3
  1399.8 12.9 fusion.212
  1412.8 13.5 convolution_add_fusion.1
  1436.5 425.8 %all-reduce.16.cloned.1.call-done = (f32[768,2048]{1,0:T(8,128)}, f32[768,2048]{1,0:T(8,128)}) async-done(((f32[768,2048]{1,0:T(8,128)}, f32[768,2048]{1,0:T(8,128)}), (f32[768,2048]{1,0:T(8,128)}, f32[768,2048]{1,0:T(8,128)})) %all-reduce.16.cloned.1.call-update) | async-done | bytes 12582928 | tf_op jit(solution)/shard_map/psum | solution.py:349
  1862.3 21.0 fusion.92
  1900.2 228.6 %while.67 = (s32[]{:T(128)}, f32[3072,4,128]{0,2,1:T(8,128)}, f32[3072,4,128]{0,2,1:T(8,128)}, f32[3,256,4,128]{1,0,3,2:T(4,128)}, s32[3]{0:T(128)S(1)}, /*index...) while((s32[]{:T(128)}, f32[3072,4,128]{0,2,1:T(8,128)}, ...), condition=%wide.region_50.52_spmd.clone, body=%wide.region_48.51_spmd.clone.sunk | while | flops 4083288320 | bytes 201900672 | solution.py:156
  1987.8 12.6 multiply_reduce_fusion.21
  2038.1 13.3 bitcast_add_fusion.11
  2115.5 13.3 bitcast_add_fusion.11
  2140.9 229.4 %while.66 = (s32[]{:T(128)}, f32[3072,4,128]{0,2,1:T(8,128)}, f32[3072,4,128]{0,2,1:T(8,128)}, f32[3,256,4,128]{1,0,3,2:T(4,128)}, s32[3]{0:T(128)S(1)}, /*index...) while((s32[]{:T(128)}, f32[3072,4,128]{0,2,1:T(8,128)}, ...), condition=%wide.region_37.39_spmd.clone, body=%wide.region_35.38_spmd.clone.sunk | while | flops 4083288320 | bytes 201900672 | solution.py:156
  2155.0 12.7 multiply_reduce_fusion.20
  2228.9 12.6 multiply_reduce_fusion.20
  2279.3 13.4 bitcast_add_fusion.9
  2356.7 13.4 bitcast_add_fusion.9
  2498.6 18.7 all-reduce.4
  2568.8 22.6 all-reduce.9
  2597.9 45.0 %reduce-scatter.65.cloned.1.call-done = bf16[2048,256]{1,0:T(8,128)(2,1)} async-done(((bf16[2048,2048]{1,0:T(8,128)(2,1)}), bf16[2048,256]{1,0:T(8,128)(2,1)}) %reduce-scatter.65.cloned.1.call-update) | async-done | bytes 1048592 | tf_op jit(solution)/shard_map/reduce_scatter | solution.py:198
  2646.0 71.7 %reduce-scatter.59.cloned.1.call-done = bf16[256,2048]{1,0:T(8,128)(2,1)} async-done(((bf16[2048,2048]{1,0:T(8,128)(2,1)}), bf16[256,2048]{1,0:T(8,128)(2,1)}) %reduce-scatter.59.cloned.1.call-update) | async-done | bytes 1048592 | tf_op jit(solution)/shard_map/reduce_scatter | solution.py:195
  2717.7 75.1 %reduce-scatter.61.cloned.1.call-done = bf16[256,2048]{1,0:T(8,128)(2,1)} async-done(((bf16[2048,2048]{1,0:T(8,128)(2,1)}), bf16[256,2048]{1,0:T(8,128)(2,1)}) %reduce-scatter.61.cloned.1.call-update) | async-done | bytes 1048592 | tf_op jit(solution)/shard_map/reduce_scatter | solution.py:195
  2796.1 71.5 %reduce-scatter.55.cloned.1.call-done = bf16[256,2048]{1,0:T(8,128)(2,1)} async-done(((bf16[2048,2048]{1,0:T(8,128)(2,1)}), bf16[256,2048]{1,0:T(8,128)(2,1)}) %reduce-scatter.55.cloned.1.call-update) | async-done | bytes 1048592 | tf_op jit(solution)/shard_map/reduce_scatter | solution.py:192
  2867.6 75.6 %reduce-scatter.57.cloned.1.call-done = bf16[256,2048]{1,0:T(8,128)(2,1)} async-done(((bf16[2048,2048]{1,0:T(8,128)(2,1)}), bf16[256,2048]{1,0:T(8,128)(2,1)}) %reduce-scatter.57.cloned.1.call-update) | async-done | bytes 1048592 | tf_op jit(solution)/shard_map/reduce_scatter | solution.py:192
  2946.4 31.6 reduce-scatter.67.cloned.1.call-done
  2978.8 34.2 reduce-scatter.69.cloned.1.call-done
  3014.4 43.0 %reduce-scatter.51.cloned.1.call-done = bf16[512,256]{1,0:T(8,128)(2,1)} async-done(((bf16[512,2048]{1,0:T(8,128)(2,1)}), bf16[512,256]{1,0:T(8,128)(2,1)}) %reduce-scatter.51.cloned.1.call-update) | async-done | bytes 262160 | tf_op jit(solution)/shard_map/reduce_scatter | solution.py:189
  3057.4 44.9 %reduce-scatter.53.cloned.1.call-done = bf16[512,256]{1,0:T(8,128)(2,1)} async-done(((bf16[512,2048]{1,0:T(8,128)(2,1)}), bf16[512,256]{1,0:T(8,128)(2,1)}) %reduce-scatter.53.cloned.1.call-update) | async-done | bytes 262160 | tf_op jit(solution)/shard_map/reduce_scatter | solution.py:189
  3104.2 33.0 reduce-scatter.71.cloned.1.call-done
  3137.9 34.2 reduce-scatter.73.cloned.1.call-done
  3173.5 43.2 %reduce-scatter.49.cloned.1.call-done = bf16[256,512]{0,1:T(8,128)(2,1)} async-done(((bf16[2048,512]{0,1:T(8,128)(2,1)}), bf16[256,512]{0,1:T(8,128)(2,1)}) %reduce-scatter.49.cloned.1.call-update) | async-done | bytes 262160 | tf_op jit(solution)/shard_map/reduce_scatter | solution.py:186
  3216.7 44.9 %reduce-scatter.47.cloned.1.call-done = bf16[256,512]{0,1:T(8,128)(2,1)} async-done(((bf16[2048,512]{0,1:T(8,128)(2,1)}), bf16[256,512]{0,1:T(8,128)(2,1)}) %reduce-scatter.47.cloned.1.call-update) | async-done | bytes 262160 | tf_op jit(solution)/shard_map/reduce_scatter | solution.py:186
  3263.7 42.3 %reduce-scatter.43.cloned.1.call-done = bf16[256,512]{0,1:T(8,128)(2,1)} async-done(((bf16[2048,512]{0,1:T(8,128)(2,1)}), bf16[256,512]{0,1:T(8,128)(2,1)}) %reduce-scatter.43.cloned.1.call-update) | async-done | bytes 262160 | tf_op jit(solution)/shard_map/reduce_scatter | solution.py:183
  3305.9 44.9 %reduce-scatter.45.cloned.1.call-done = bf16[256,512]{0,1:T(8,128)(2,1)} async-done(((bf16[2048,512]{0,1:T(8,128)(2,1)}), bf16[256,512]{0,1:T(8,128)(2,1)}) %reduce-scatter.45.cloned.1.call-update) | async-done | bytes 262160 | tf_op jit(solution)/shard_map/reduce_scatter | solution.py:183
  3352.9 42.4 %reduce-scatter.39.cloned.1.call-done = bf16[256,512]{0,1:T(8,128)(2,1)} async-done(((bf16[2048,512]{0,1:T(8,128)(2,1)}), bf16[256,512]{0,1:T(8,128)(2,1)}) %reduce-scatter.39.cloned.1.call-update) | async-done | bytes 262160 | tf_op jit(solution)/shard_map/reduce_scatter | solution.py:180
  3395.4 44.7 %reduce-scatter.41.cloned.1.call-done = bf16[256,512]{0,1:T(8,128)(2,1)} async-done(((bf16[2048,512]{0,1:T(8,128)(2,1)}), bf16[256,512]{0,1:T(8,128)(2,1)}) %reduce-scatter.41.cloned.1.call-update) | async-done | bytes 262160 | tf_op jit(solution)/shard_map/reduce_scatter | solution.py:180
  3442.2 223.4 %all-reduce.22.cloned.1.call-done = (bf16[768,2048]{1,0:T(8,128)(2,1)}, bf16[768,2048]{1,0:T(8,128)(2,1)}) async-done(((bf16[768,2048]{1,0:T(8,128)(2,1)}, bf16[768,2048]{1,0:T(8,128)(2,1)}), (bf16[768,2048]{1,0:T(8,128)(2,1)}, bf16[768,2048]{1,0:T(8,128)(2,1)})) %all-reduce.22.cloned.1.call-update) | async-done | bytes 6291472 | tf_op jit(solution)/shard_map/psum | solution.py:401
  (610 shorter events, 914.6 us)
Async XLA Ops:
  7.2 33.4 all-gather.16.cloned.1.call-start
  7.9 62.4 %all-gather.18.cloned.1.call-start = ((), (), s32[]{:S(2)}) async-start(), calls=%async_computation.23 | async-start | bytes 2359296 | tf_op jit(solution)/shard_map/all_gather | solution.py:165
  8.7 94.5 %all-gather.22.cloned.1.call-start = ((), (), s32[]{:S(2)}) async-start(), calls=%async_computation.25 | async-start | bytes 2359296 | tf_op jit(solution)/shard_map/all_gather | solution.py:166
  9.4 163.6 %all-gather.20.cloned.1.call-start = ((), (), s32[]{:S(2)}) async-start(), calls=%async_computation.24 | async-start | bytes 3932160 | tf_op jit(solution)/shard_map/all_gather | solution.py:295
  20.0 79.7 %copy-start.61 = (f32[128,4]{0,1:T(4,128)}, f32[128,4]{0,1:T(4,128)S(1)}, u32[]{:S(2)}) copy-start(f32[128,4]{0,1:T(4,128)S(1)} %reshape.733) | copy-start | bytes 6148
  45.1 121.5 %copy-start.15 = (f32[768,512]{0,1:T(8,128)}, f32[768,512]{0,1:T(8,128)S(1)}, u32[]{:S(2)}) copy-start(f32[768,512]{0,1:T(8,128)S(1)} %get-tuple-element.1266) | copy-start | bytes 4718596
  49.5 117.2 %copy-start.16 = (f32[768,512]{0,1:T(8,128)}, f32[768,512]{0,1:T(8,128)S(1)}, u32[]{:S(2)}) copy-start(f32[768,512]{0,1:T(8,128)S(1)} %get-tuple-element.1270) | copy-start | bytes 4718596
  99.6 67.0 %copy-start.49 = (f32[768]{0:T(1024)}, f32[768]{0:T(1024)S(1)}, u32[]{:S(2)}) copy-start(f32[768]{0:T(1024)S(1)} %get-tuple-element.1280) | copy-start | bytes 9220
  99.7 67.0 %copy-start.51 = (f32[768]{0:T(1024)}, f32[768]{0:T(1024)S(1)}, u32[]{:S(2)}) copy-start(f32[768]{0:T(1024)S(1)} %get-tuple-element.1282) | copy-start | bytes 9220
  103.1 73.4 %all-gather.24.cloned.1.call-start = ((), (), s32[]{:S(2)}) async-start(), calls=%async_computation.26 | async-start | bytes 3932160 | tf_op jit(solution)/shard_map/all_gather | solution.py:296
  108.4 119.8 %all-gather.34.cloned.1.call-start = ((), (), s32[]{:S(2)}) async-start(), calls=%async_computation.31 | async-start | bytes 3932160 | tf_op jit(solution)/shard_map/all_gather | solution.py:295
  109.0 124.7 %all-gather.36.cloned.1.call-start = ((), (), s32[]{:S(2)}) async-start(), calls=%async_computation.32 | async-start | bytes 3932160 | tf_op jit(solution)/shard_map/all_gather | solution.py:296
  114.9 172.1 %all-gather.26.cloned.1.call-start = ((), (), s32[]{:S(2)}) async-start(), calls=%async_computation.27 | async-start | bytes 2359296 | tf_op jit(solution)/shard_map/all_gather | solution.py:167
  115.7 606.2 %all-reduce.20.cloned.1.call-start = ((), (), s32[]{:S(2)}) async-start(), calls=%async_computation.57 | async-start | bytes 25165824 | tf_op jit(solution)/shard_map/psum | solution.py:305
  298.0 478.9 %all-gather.28.cloned.1.call-start = ((), (), s32[]{:S(2)}) async-start(), calls=%async_computation.28 | async-start | bytes 9437184 | tf_op jit(solution)/shard_map/all_gather | solution.py:168
  298.6 534.6 %all-gather.30.cloned.1.call-start = ((), (), s32[]{:S(2)}) async-start(), calls=%async_computation.29 | async-start | bytes 9437184 | tf_op jit(solution)/shard_map/all_gather | solution.py:169
  299.3 591.6 %all-gather.32.cloned.1.call-start = ((), (), s32[]{:S(2)}) async-start(), calls=%async_computation.30 | async-start | bytes 9437184 | tf_op jit(solution)/shard_map/all_gather | solution.py:170
  299.9 1038.7 %all-reduce.18.cloned.1.call-start = ((), (), s32[]{:S(2)}) async-start(), calls=%async_computation.56 | async-start | bytes 25165824 | tf_op jit(solution)/shard_map/psum | solution.py:316
  307.5 419.5 %copy-start.45 = (f32[8,1,256]{2,1,0:T(1,128)}, f32[8,1,256]{2,1,0:T(1,128)S(1)}, u32[]{:S(2)}) copy-start(f32[8,1,256]{2,1,0:T(1,128)S(1)} %convert_element_type.496) | copy-start | bytes 24580
  734.2 113.4 %copy-start.37 = (bf16[768,2048]{1,0:T(8,128)(2,1)}, bf16[768,2048]{1,0:T(8,128)(2,1)S(1)}, u32[]{:S(2)}) copy-start(bf16[768,2048]{1,0:T(8,128)(2,1)S(1)} %get-tuple-element.1242) | copy-start | bytes 9437188
  911.7 950.6 %all-reduce.16.cloned.1.call-start = ((), (), s32[]{:S(2)}) async-start(), calls=%async_computation.55 | async-start | bytes 25165824 | tf_op jit(solution)/shard_map/psum | solution.py:349
  1436.4 426.0 %copy-start.46 = (f32[8,1,256]{2,1,0:T(1,128)S(1)}, f32[8,1,256]{2,1,0:T(1,128)}, u32[]{:S(2)}) copy-start(f32[8,1,256]{2,1,0:T(1,128)} %copy-done.45) | copy-start | bytes 24580
  1436.4 426.0 %copy-start.58 = (f32[768]{0:T(1024)S(1)}, f32[768]{0:T(1024)}, u32[]{:S(2)}) copy-start(f32[768]{0:T(1024)} %copy-done.57) | copy-start | bytes 9220
  1436.4 426.0 %copy-start.60 = (f32[768]{0:T(1024)S(1)}, f32[768]{0:T(1024)}, u32[]{:S(2)}) copy-start(f32[768]{0:T(1024)} %copy-done.59) | copy-start | bytes 9220
  1436.4 447.0 %slice-start.8 = ((s8[6291456]{0:T(1024)(128)(4,1)}), s8[2097152]{0:T(1024)(128)(4,1)S(1)}, s32[]{:S(2)}) async-start(s8[6291456]{0:T(1024)(128)(4,1)} %bitcast.401), calls=%async_computation.67 | async-start | bytes 4194304
  1436.4 1042.3 %reduce-scatter.35.cloned.1.call-start = ((), (), s32[]{:S(2)}) async-start(), calls=%async_computation.35 | async-start | bytes 3932160 | tf_op jit(solution)/shard_map/reduce_scatter | solution.py:375
  2133.7 345.0 %reduce-scatter.31.cloned.1.call-start = ((), (), s32[]{:S(2)}) async-start(), calls=%async_computation.33 | async-start | bytes 3932160 | tf_op jit(solution)/shard_map/reduce_scatter | solution.py:375
  2375.2 108.5 %reduce-scatter.37.cloned.1.call-start = ((), (), s32[]{:S(2)}) async-start(), calls=%async_computation.36 | async-start | bytes 3932160 | tf_op jit(solution)/shard_map/reduce_scatter | solution.py:378
  2380.2 113.0 %reduce-scatter.33.cloned.1.call-start = ((), (), s32[]{:S(2)}) async-start(), calls=%async_computation.34 | async-start | bytes 3932160 | tf_op jit(solution)/shard_map/reduce_scatter | solution.py:378
  2386.1 211.8 %reduce-scatter.63.cloned.1.call-start = ((), (), s32[]{:S(2)}) async-start(), calls=%async_computation.49 | async-start | bytes 9437184 | tf_op jit(solution)/shard_map/reduce_scatter | solution.py:198
  2397.1 245.9 %reduce-scatter.65.cloned.1.call-start = ((), (), s32[]{:S(2)}) async-start(), calls=%async_computation.50 | async-start | bytes 9437184 | tf_op jit(solution)/shard_map/reduce_scatter | solution.py:198
  2410.0 307.7 %reduce-scatter.59.cloned.1.call-start = ((), (), s32[]{:S(2)}) async-start(), calls=%async_computation.47 | async-start | bytes 9437184 | tf_op jit(solution)/shard_map/reduce_scatter | solution.py:195
  2422.9 370.0 %reduce-scatter.61.cloned.1.call-start = ((), (), s32[]{:S(2)}) async-start(), calls=%async_computation.48 | async-start | bytes 9437184 | tf_op jit(solution)/shard_map/reduce_scatter | solution.py:195
  2436.0 431.6 %reduce-scatter.55.cloned.1.call-start = ((), (), s32[]{:S(2)}) async-start(), calls=%async_computation.45 | async-start | bytes 9437184 | tf_op jit(solution)/shard_map/reduce_scatter | solution.py:192
  2447.6 495.6 %reduce-scatter.57.cloned.1.call-start = ((), (), s32[]{:S(2)}) async-start(), calls=%async_computation.46 | async-start | bytes 9437184 | tf_op jit(solution)/shard_map/reduce_scatter | solution.py:192
  2458.6 519.4 %reduce-scatter.67.cloned.1.call-start = ((), (), s32[]{:S(2)}) async-start(), calls=%async_computation.51 | async-start | bytes 36864
  2466.5 546.5 %reduce-scatter.69.cloned.1.call-start = ((), (), s32[]{:S(2)}) async-start(), calls=%async_computation.52 | async-start | bytes 36864
  2467.3 590.1 %reduce-scatter.51.cloned.1.call-start = ((), (), s32[]{:S(2)}) async-start(), calls=%async_computation.43 | async-start | bytes 2359296 | tf_op jit(solution)/shard_map/reduce_scatter | solution.py:189
  2473.2 629.1 %reduce-scatter.53.cloned.1.call-start = ((), (), s32[]{:S(2)}) async-start(), calls=%async_computation.44 | async-start | bytes 2359296 | tf_op jit(solution)/shard_map/reduce_scatter | solution.py:189
  2478.6 658.5 %reduce-scatter.71.cloned.1.call-start = ((), (), s32[]{:S(2)}) async-start(), calls=%async_computation.53 | async-start | bytes 36864
  2482.8 689.3 %reduce-scatter.73.cloned.1.call-start = ((), (), s32[]{:S(2)}) async-start(), calls=%async_computation.54 | async-start | bytes 36864
  2483.6 733.1 %reduce-scatter.49.cloned.1.call-start = ((), (), s32[]{:S(2)}) async-start(), calls=%async_computation.42 | async-start | bytes 2359296 | tf_op jit(solution)/shard_map/reduce_scatter | solution.py:186
  2489.0 772.5 %reduce-scatter.47.cloned.1.call-start = ((), (), s32[]{:S(2)}) async-start(), calls=%async_computation.41 | async-start | bytes 2359296 | tf_op jit(solution)/shard_map/reduce_scatter | solution.py:186
  2498.5 807.4 %reduce-scatter.43.cloned.1.call-start = ((), (), s32[]{:S(2)}) async-start(), calls=%async_computation.39 | async-start | bytes 2359296 | tf_op jit(solution)/shard_map/reduce_scatter | solution.py:183
  2527.1 823.7 %reduce-scatter.45.cloned.1.call-start = ((), (), s32[]{:S(2)}) async-start(), calls=%async_computation.40 | async-start | bytes 2359296 | tf_op jit(solution)/shard_map/reduce_scatter | solution.py:183
  2532.8 862.6 %reduce-scatter.39.cloned.1.call-start = ((), (), s32[]{:S(2)}) async-start(), calls=%async_computation.37 | async-start | bytes 2359296 | tf_op jit(solution)/shard_map/reduce_scatter | solution.py:180
  2542.7 897.4 %reduce-scatter.41.cloned.1.call-start = ((), (), s32[]{:S(2)}) async-start(), calls=%async_computation.38 | async-start | bytes 2359296 | tf_op jit(solution)/shard_map/reduce_scatter | solution.py:180
  2547.8 1117.9 %all-reduce.22.cloned.1.call-start = ((), (), s32[]{:S(2)}) async-start(), calls=%async_computation.58 | async-start | bytes 12582912 | tf_op jit(solution)/shard_map/psum | solution.py:401
  (108 other events, 967.0 us)
Sparse Core Ops, SparseCore 0:
  9.9 30.5 all-gather.15
  42.4 27.8 all-gather.17
  72.2 27.8 all-gather.21
  103.2 27.5 all-gather.19
  132.2 28.5 all-gather.23
  162.7 28.5 all-gather.33
  192.8 28.5 all-gather.35
  223.3 28.1 all-gather.25
  298.1 423.6 all-reduce.19
  723.6 53.3 all-gather.27
  778.8 54.3 all-gather.29
  835.0 55.9 all-gather.31
  911.8 426.7 all-reduce.17
  1436.5 425.7 all-reduce.15
  2133.8 36.9 reduce-scatter.34
  2375.3 36.8 reduce-scatter.30
  2414.6 37.9 reduce-scatter.36
  2455.2 37.9 reduce-scatter.32
  2496.6 71.2 reduce-scatter.62
  2571.7 71.2 reduce-scatter.64
  2646.4 71.2 reduce-scatter.58
  2721.6 71.2 reduce-scatter.60
  2796.3 71.2 reduce-scatter.54
  2871.9 71.2 reduce-scatter.56
  2946.7 31.2 reduce-scatter.66
  2981.7 31.2 reduce-scatter.68
  3016.1 41.2 reduce-scatter.50
  3061.0 41.2 reduce-scatter.52
  3105.9 31.2 reduce-scatter.70
  3140.8 31.2 reduce-scatter.72
  3175.4 41.2 reduce-scatter.48
  3220.3 41.2 reduce-scatter.46
  3264.7 41.2 reduce-scatter.42
  3309.6 41.2 reduce-scatter.44
  3354.1 41.2 reduce-scatter.38
  3398.9 41.2 reduce-scatter.40
  3442.4 223.2 all-reduce.21
where the time goes:
time: 3710 us; the launch traced here: 3690 us
  waiting for transfers between devices  2470 us (67%)
  matrix products  644 us (17%)
  other arithmetic  240 us (6%)
  local copies, waits for them, and re-layouts  208 us (6%)
  blocking collectives  95.8 us (3%)
    psum x1, waiting for transfers between devices, per_device(): lax.psum(right_t(gate_low, wg_full) + right_t(up_low, wu_full), 'tensor')  426 us
    psum x1, waiting for transfers between devices, per_device(): mlp_proj = lax.psum(matmul(inner_low, wd_full), 'tensor')  417 us
    psum x1, waiting for transfers between devices, per_device(): attn_proj = lax.psum(matmul(attn_low, wo_full), 'tensor')  414 us
    psum x1, waiting for transfers between devices, per_device(): lax.psum(back_sum.astype(jnp.bfloat16), 'tensor').astype(jnp.float32)  223 us
    reduce_scatter x2, waiting for transfers between devices, share_grads(): lax.psum_scatter(grads[4].astype(jnp.bfloat16), ('dp', 'seq'), scatter_di...  147 us
    reduce_scatter x2, waiting for transfers between devices, share_grads(): lax.psum_scatter(grads[5].astype(jnp.bfloat16), ('dp', 'seq'), scatter_di...  147 us
    unnamed x41, waiting for transfers between devices  139 us
    dot_general x14, matrix products, right_t(): lax.dot_general(left, right, (((1,), (1,)), ((), ())), preferred_element_...  111 us
  transfers between devices with their start and end apart: 37, of which 27 were waited for; matrix products, arithmetic and copies ran while one was open for 18% of the time, Pallas kernels for 0%

commit v1 on v0

v1 whole, which is shorter than its diff:
```python
import functools

import jax
import jax.numpy as jnp
from jax import lax
from jax.experimental import pallas as pl
from jax.experimental.pallas import tpu as pltpu
from jax.sharding import PartitionSpec as P

HD = 128
BLOCK = 256

norm_eps = 1e-06
masked_score = -1e30
f32 = jnp.float32
bf16 = jnp.bfloat16


def matmul(left, right):
    return jnp.dot(left, right, preferred_element_type=f32)


def left_t(left, right):
    return lax.dot_general(left, right, (((0,), (0,)), ((), ())), preferred_element_type=f32)


def right_t(left, right):
    return lax.dot_general(left, right, (((1,), (1,)), ((), ())), preferred_element_type=f32)


MESH = pl.DeviceIdType.MESH


class Line:
    def __init__(self, n, chunks, rows, part, out, s, land, res, sems):
        self.chunks, self.rows = chunks, rows
        self.part, self.out, self.s, self.land, self.res = part, out, s, land, res
        (
            self.load_sem,
            self.in_send,
            self.in_recv,
            self.out_send,
            self.out_recv,
            self.store_sem,
        ) = sems
        i = lax.axis_index("tensor")
        half = n // 2
        left = i < half
        self.inward = jnp.where(left, i + 1, i - 1)
        self.outward = jnp.where(left, i - 1, i + 1)
        self.relay = (i > 0) & (i < n - 1)
        self.mid = (i == half - 1) | (i == half)
        self.slot = jnp.where(self.mid, 1, 0)

    def at(self, c):
        return pl.ds(pl.multiple_of(c * self.rows, self.rows), self.rows)

    def load(self):
        return pltpu.make_async_copy(self.part, self.s, self.load_sem)

    def inward_copy(self, c, slot):
        return pltpu.make_async_remote_copy(
            src_ref=self.s.at[self.at(c)],
            dst_ref=self.land.at[slot, self.at(c)],
            send_sem=self.in_send.at[c],
            recv_sem=self.in_recv.at[slot, c],
            device_id={"tensor": self.inward},
            device_id_type=MESH,
        )

    def outward_copy(self, c):
        return pltpu.make_async_remote_copy(
            src_ref=self.res.at[self.at(c)],
            dst_ref=self.res.at[self.at(c)],
            send_sem=self.out_send.at[c],
            recv_sem=self.out_recv.at[c],
            device_id={"tensor": self.outward},
            device_id_type=MESH,
        )

    def store(self, c):
        return pltpu.make_async_copy(
            self.res.at[self.at(c)], self.out.at[self.at(c)], self.store_sem.at[c]
        )

    def begin(self):
        self.load().start()
        barrier = pltpu.get_barrier_semaphore()
        pl.semaphore_signal(
            barrier, inc=1, device_id={"tensor": self.inward}, device_id_type=MESH
        )

        @pl.when(self.relay)
        def _():
            pl.semaphore_signal(
                barrier, inc=1, device_id={"tensor": self.outward}, device_id_type=MESH
            )

        pl.semaphore_wait(barrier, jnp.where(self.relay, 2, 1))
        self.load().wait()

        @pl.when(~self.relay)
        def _():
            def one(c, carry):
                self.inward_copy(c, self.slot).start()
                return carry

            lax.fori_loop(0, self.chunks, one, 0)

    def reduce(self, c):
        @pl.when(self.relay)
        def _():
            self.inward_copy(c, 0).wait_recv()
            a = self.at(c)
            self.s[a, :] = (self.s[a, :].astype(f32) + self.land[0, a, :].astype(f32)).astype(bf16)
            self.inward_copy(c, self.slot).start()

    def spread(self, c):
        a = self.at(c)

        @pl.when(self.mid)
        def _():
            self.inward_copy(c, 1).wait_recv()
            self.res[a, :] = (
                self.s[a, :].astype(f32) + self.land[1, a, :].astype(f32)
            ).astype(bf16)

        @pl.when(~self.mid)
        def _():
            self.outward_copy(c).wait_recv()

        @pl.when(self.relay)
        def _():
            self.outward_copy(c).start()

        self.store(c).start()

    def end(self):
        def one(c, carry):
            self.inward_copy(c, self.slot).wait_send()

            @pl.when(self.relay)
            def _():
                self.outward_copy(c).wait_send()

            self.store(c).wait()
            return carry

        lax.fori_loop(0, self.chunks, one, 0)


def line_scratch(rows, width, chunks):
    dma = pltpu.SemaphoreType.DMA
    return [
        pltpu.VMEM((rows, width), bf16),
        pltpu.VMEM((2, rows, width), bf16),
        pltpu.VMEM((rows, width), bf16),
        dma(()),
        dma((chunks,)),
        dma((2, chunks)),
        dma((chunks,)),
        dma((chunks,)),
        dma((chunks,)),
    ]


def line_kernel(n, chunks, part, out, s, land, res, *sems):
    line = Line(n, chunks, part.shape[0] // chunks, part, out, s, land, res, sems)
    line.begin()

    def step(c, carry):
        line.reduce(c)

        @pl.when(c > 0)
        def _():
            line.spread(c - 1)

        return carry

    lax.fori_loop(0, chunks, step, 0)
    line.spread(chunks - 1)
    line.end()


def line_sum(part):
    rows, width = part.shape
    n = lax.axis_size("tensor")
    chunks = rows // 48
    return pl.pallas_call(
        functools.partial(line_kernel, n, chunks),
        in_specs=[pl.BlockSpec(memory_space=pl.ANY)],
        out_specs=pl.BlockSpec(memory_space=pl.ANY),
        out_shape=jax.ShapeDtypeStruct(part.shape, bf16),
        scratch_shapes=line_scratch(rows, width, chunks),
        compiler_params=pltpu.CompilerParams(
            collective_id=0, has_side_effects=True, vmem_limit_bytes=48 << 20
        ),
        name="line_sum",
    )(part)


def attn_scores(meta, i, trunk_rows, q, kt, kp, ko):
    scale = HD ** (-0.5)
    block = meta[i, 0]
    n_par = meta[i, 2]
    n_own = meta[i, 3]
    n_trunk = meta[i, 4]
    st = right_t(q, kt) * scale
    sp = right_t(q, kp) * scale
    so = right_t(q, ko) * scale
    row = lax.broadcasted_iota(jnp.int32, (BLOCK, trunk_rows), 0) + block * BLOCK
    col = lax.broadcasted_iota(jnp.int32, (BLOCK, trunk_rows), 1)
    st = jnp.where((col < n_trunk) & (col <= row), st, masked_score)
    row = lax.broadcasted_iota(jnp.int32, (BLOCK, BLOCK), 0)
    col = lax.broadcasted_iota(jnp.int32, (BLOCK, BLOCK), 1)
    sp = jnp.where(col < n_par, sp, masked_score)
    so = jnp.where((col < n_own) & (col <= row), so, masked_score)
    return st, sp, so


def attn_fwd_kernel(trunk_rows, meta, q, kt, vt, kp, vp, ko, vo, out, lse):
    i = pl.program_id(1)
    st, sp, so = attn_scores(meta, i, trunk_rows, q[...], kt[...], kp[...], ko[...])
    top = jnp.maximum(
        jnp.max(st, axis=1, keepdims=True),
        jnp.maximum(jnp.max(sp, axis=1, keepdims=True), jnp.max(so, axis=1, keepdims=True)),
    )
    et, ep, eo = jnp.exp(st - top), jnp.exp(sp - top), jnp.exp(so - top)
    total = (
        jnp.sum(et, axis=1, keepdims=True)
        + jnp.sum(ep, axis=1, keepdims=True)
        + jnp.sum(eo, axis=1, keepdims=True)
    )
    acc = matmul(et.astype(bf16), vt[...])
    acc += matmul(ep.astype(bf16), vp[...])
    acc += matmul(eo.astype(bf16), vo[...])
    out[...] = (acc / total).astype(bf16)
    lse[...] = jnp.broadcast_to(top + jnp.log(total), (BLOCK, HD))


def attn_bwd_kernel(
    trunk_rows, n_q, meta, q, do, lse, kt, vt, kp, vp, ko, vo,
    dq, dko, dvo, dkt, dvt, dkb, dvb, a_kt, a_vt, a_kb, a_vb,
):
    i = pl.program_id(1)

    @pl.when(i == 0)
    def _():
        for acc in (a_kt, a_vt, a_kb, a_vb):
            acc[...] = jnp.zeros_like(acc)

    scale = HD ** (-0.5)
    qv, dov = q[...], do[...]
    scores = attn_scores(meta, i, trunk_rows, qv, kt[...], kp[...], ko[...])
    top = lse[:, 0:1]
    probs = [jnp.exp(s - top) for s in scores]
    grads = [right_t(dov, v[...]) for v in (vt, vp, vo)]
    inner = sum(jnp.sum(p * g, axis=1, keepdims=True) for p, g in zip(probs, grads))
    low = [(p * (g - inner)).astype(bf16) for p, g in zip(probs, grads)]
    probs = [p.astype(bf16) for p in probs]
    dq[...] = scale * (
        matmul(low[0], kt[...]) + matmul(low[1], kp[...]) + matmul(low[2], ko[...])
    )
    a_kt[...] += left_t(low[0], qv)
    a_vt[...] += left_t(probs[0], dov)
    dko[...] = scale * left_t(low[2], qv)
    dvo[...] = left_t(probs[2], dov)
    at = pl.ds(pl.multiple_of(meta[i, 1] * BLOCK, BLOCK), BLOCK)
    a_kb[at, :] += left_t(low[1], qv)
    a_vb[at, :] += left_t(probs[1], dov)

    @pl.when(i == n_q - 1)
    def _():
        dkt[...] = (scale * a_kt[...]).astype(bf16)
        dvt[...] = a_vt[...].astype(bf16)
        dkb[...] = (scale * a_kb[...]).astype(bf16)
        dvb[...] = a_vb[...].astype(bf16)


def kv_specs(trunk_rows):
    trunk = pl.BlockSpec((trunk_rows, HD), lambda h, i, meta: (0, h))
    par = pl.BlockSpec((BLOCK, HD), lambda h, i, meta: (meta[i, 1], h))
    own = pl.BlockSpec((BLOCK, HD), lambda h, i, meta: (i, h))
    return [trunk, trunk, par, par, own, own]


def attend_forward(meta, q, kv):
    rows, width = q.shape
    trunk_rows = kv[0].shape[0]
    own = pl.BlockSpec((BLOCK, HD), lambda h, i, meta: (i, h))
    return pl.pallas_call(
        functools.partial(attn_fwd_kernel, trunk_rows),
        grid_spec=pltpu.PrefetchScalarGridSpec(
            num_scalar_prefetch=1,
            grid=(width // HD, rows // BLOCK),
            in_specs=[own] + kv_specs(trunk_rows),
            out_specs=[own, own],
        ),
        out_shape=[
            jax.ShapeDtypeStruct((rows, width), bf16),
            jax.ShapeDtypeStruct((rows, width), f32),
        ],
        compiler_params=pltpu.CompilerParams(vmem_limit_bytes=32 << 20),
        name="attend_forward",
    )(meta, q, *kv)


def attend_backward(meta, q, do, lse, kv):
    rows, width = q.shape
    trunk_rows = kv[0].shape[0]
    branch_rows = kv[2].shape[0]
    own = pl.BlockSpec((BLOCK, HD), lambda h, i, meta: (i, h))
    trunk = pl.BlockSpec((trunk_rows, HD), lambda h, i, meta: (0, h))
    branch = pl.BlockSpec((branch_rows, HD), lambda h, i, meta: (0, h))
    n_q = rows // BLOCK
    return pl.pallas_call(
        functools.partial(attn_bwd_kernel, trunk_rows, n_q),
        grid_spec=pltpu.PrefetchScalarGridSpec(
            num_scalar_prefetch=1,
            grid=(width // HD, n_q),
            in_specs=[own, own, own] + kv_specs(trunk_rows),
            out_specs=[own, own, own, trunk, trunk, branch, branch],
            scratch_shapes=[
                pltpu.VMEM((trunk_rows, HD), f32),
                pltpu.VMEM((trunk_rows, HD), f32),
                pltpu.VMEM((branch_rows, HD), f32),
                pltpu.VMEM((branch_rows, HD), f32),
            ],
        ),
        out_shape=[
            jax.ShapeDtypeStruct((rows, width), f32),
            jax.ShapeDtypeStruct((rows, width), f32),
            jax.ShapeDtypeStruct((rows, width), f32),
            jax.ShapeDtypeStruct((trunk_rows, width), bf16),
            jax.ShapeDtypeStruct((trunk_rows, width), bf16),
            jax.ShapeDtypeStruct((branch_rows, width), bf16),
            jax.ShapeDtypeStruct((branch_rows, width), bf16),
        ],
        compiler_params=pltpu.CompilerParams(vmem_limit_bytes=40 << 20),
        name="attend_backward",
    )(meta, q, do, lse, *kv)


def group_perm(n, k):
    half = n // 2
    return [(i, i // half * half + (i % half + k) % half) for i in range(n)]


def fetch_sources(block):
    n = lax.axis_size("seq")
    half = n // 2
    place = lax.axis_index("seq")
    spot = lax.rem(place, half)
    got = lax.ppermute(block, "seq", [(i, i + half) for i in range(half)])
    mine = jnp.where(place < half, block, got)
    parts = [mine] + [lax.ppermute(mine, "seq", group_perm(n, k)) for k in range(1, half)]
    out = []
    for source in range(half):
        pick = parts[0]
        for k in range(1, half):
            pick = jnp.where(lax.rem(spot - k + half, half) == source, parts[k], pick)
        out.append(pick)
    return jnp.concatenate(out, axis=0)


def return_to_sources(grads):
    n = lax.axis_size("seq")
    half = n // 2
    place = lax.axis_index("seq")
    spot = lax.rem(place, half)
    rows = grads.shape[0] // half
    pieces = [grads[s * rows : (s + 1) * rows] for s in range(half)]

    def piece(index):
        pick = pieces[0]
        for s in range(1, half):
            pick = jnp.where(index == s, pieces[s], pick)
        return pick

    total = piece(spot).astype(f32)
    for k in range(1, half):
        sent = piece(lax.rem(spot + k, half))
        total += lax.ppermute(sent, "seq", group_perm(n, k)).astype(f32)
    got = lax.ppermute(total.astype(bf16), "seq", [(i + half, i) for i in range(half)])
    return jnp.where(place < half, total + got.astype(f32), 0.0)


def gather_rows(item):
    return lax.all_gather(item, ("dp", "seq"), axis=0, tiled=True)


def gather_cols(item):
    return lax.all_gather(item, ("dp", "seq"), axis=1, tiled=True)


def scatter_rows(item):
    return lax.psum_scatter(
        item.astype(bf16), ("dp", "seq"), scatter_dimension=0, tiled=True
    ).astype(f32)


def scatter_cols(item):
    return lax.psum_scatter(
        item.astype(bf16), ("dp", "seq"), scatter_dimension=1, tiled=True
    ).astype(f32)


def all_reduce(parts):
    total = line_sum(jnp.concatenate([p.astype(bf16) for p in parts], axis=0)).astype(f32)
    rows = parts[0].shape[0]
    return [total[m * rows : (m + 1) * rows] for m in range(len(parts))]


def block_meta(parents, lengths, rows, n_blocks):
    seg_count = parents.shape[0]
    branches = (seg_count - 1) // 3
    trunk_blocks = n_blocks - 3 * branches
    blocks = lax.axis_index("seq") * (rows // BLOCK) + jnp.arange(rows // BLOCK, dtype=jnp.int32)
    seg = jnp.maximum(blocks - trunk_blocks + 1, 0)
    hit = seg[:, None] == jnp.arange(seg_count, dtype=jnp.int32)[None, :]
    parent = jnp.sum(jnp.where(hit, parents[None, :], 0), axis=1)
    own_len = jnp.sum(jnp.where(hit, lengths[None, :], 0), axis=1)
    hit = parent[:, None] == jnp.arange(seg_count, dtype=jnp.int32)[None, :]
    par_len = jnp.sum(jnp.where(hit, lengths[None, :], 0), axis=1)
    return jnp.stack(
        [
            blocks,
            jnp.maximum(parent - 1, 0),
            jnp.where(parent > 0, par_len, 0),
            jnp.where(blocks >= trunk_blocks, own_len, 0),
            jnp.broadcast_to(lengths[0], blocks.shape),
        ],
        axis=1,
    ).astype(jnp.int32)


def per_device(
    tokens, cotangent, w_query, w_key, w_value, w_out, w_gate, w_up, w_down,
    query_gain, key_gain, attn_gain, mlp_gain, parent_of, seg_length,
):
    micros, _, rows, width = tokens.shape
    n_blocks = rows // BLOCK * lax.axis_size("seq")
    heads = w_query.shape[1] // HD
    full_width = heads * HD * lax.axis_size("tensor")
    branches = (parent_of.shape[2] - 1) // 3
    trunk_rows = (n_blocks - 3 * branches) * BLOCK

    wq = gather_rows(w_query)
    wk = gather_rows(w_key)
    wv = gather_rows(w_value)
    q_gain = gather_cols(query_gain).reshape(-1).astype(f32)
    k_gain = gather_cols(key_gain).reshape(-1).astype(f32)
    wo = gather_cols(w_out)
    a_gain = gather_rows(attn_gain).astype(f32)
    m_gain = gather_rows(mlp_gain).astype(f32)
    wg = gather_rows(w_gate)
    wu = gather_rows(w_up)
    wd = gather_cols(w_down)

    saved = []
    for m in range(micros):
        x = tokens[m, 0]
        q_raw, k_raw, v_raw = matmul(x, wq), matmul(x, wk), matmul(x, wv)
        q_sq, k_sq = lax.psum(
            (jnp.sum(q_raw * q_raw, axis=1), jnp.sum(k_raw * k_raw, axis=1)), "tensor"
        )
        q_inv = lax.rsqrt(q_sq / full_width + norm_eps)[:, None]
        k_inv = lax.rsqrt(k_sq / full_width + norm_eps)[:, None]
        q_unit, k_unit = q_raw * q_inv, k_raw * k_inv
        q_low = (q_unit * q_gain).astype(bf16)
        k_low = (k_unit * k_gain).astype(bf16)
        v_low = v_raw.astype(bf16)
        sources = fetch_sources(jnp.concatenate([k_low, v_low], axis=1))
        cols = k_low.shape[1]
        kv = (
            sources[:trunk_rows, :cols],
            sources[:trunk_rows, cols:],
            sources[trunk_rows:, :cols],
            sources[trunk_rows:, cols:],
            k_low,
            v_low,
        )
        meta = block_meta(parent_of[m, 0], seg_length[m, 0], rows, n_blocks)
        attn_low, lse = attend_forward(meta, q_low, kv)
        saved.append(
            dict(x=x, q_inv=q_inv, k_inv=k_inv, q_unit=q_unit, k_unit=k_unit, q_low=q_low,
                 kv=kv, meta=meta, attn_low=attn_low, lse=lse)
        )

    outs = []
    projs = all_reduce([matmul(s["attn_low"], wo) for s in saved])
    for m in range(micros):
        s = saved[m]
        attn_proj = projs[m]
        attn_inv = lax.rsqrt(jnp.mean(attn_proj * attn_proj, axis=1, keepdims=True) + norm_eps)
        attn_unit = attn_proj * attn_inv
        hidden = s["x"].astype(f32) + attn_unit * a_gain
        hidden_low = hidden.astype(bf16)
        gate_pre = matmul(hidden_low, wg)
        up_pre = matmul(hidden_low, wu)
        sig = jax.nn.sigmoid(gate_pre)
        inner_low = (gate_pre * sig * up_pre).astype(bf16)
        s.update(attn_unit=attn_unit, attn_inv=attn_inv, hidden=hidden, hidden_low=hidden_low,
                 gate_pre=gate_pre.astype(bf16), up_pre=up_pre.astype(bf16), inner_low=inner_low)

    gm_grad = 0.0
    projs = all_reduce([matmul(s["inner_low"], wd) for s in saved])
    for m in range(micros):
        s = saved[m]
        mlp_proj = projs[m]
        mlp_inv = lax.rsqrt(jnp.mean(mlp_proj * mlp_proj, axis=1, keepdims=True) + norm_eps)
        mlp_unit = mlp_proj * mlp_inv
        outs.append((s["hidden"] + mlp_unit * m_gain).astype(bf16))
        c = cotangent[m, 0].astype(f32)
        gm_grad += jnp.sum(c * mlp_unit, axis=0)
        unit_grad = c * m_gain
        mlp_low = (
            mlp_inv * (unit_grad - mlp_unit * jnp.mean(unit_grad * mlp_unit, axis=1, keepdims=True))
        ).astype(bf16)
        inner_grad = right_t(mlp_low, wd)
        gate_pre, up_pre = s["gate_pre"].astype(f32), s["up_pre"].astype(f32)
        sig = jax.nn.sigmoid(gate_pre)
        gate_low = (inner_grad * up_pre * sig * (1.0 + gate_pre * (1.0 - sig))).astype(bf16)
        up_low = (inner_grad * gate_pre * sig).astype(bf16)
        s.update(c=c, mlp_low=mlp_low, gate_low=gate_low, up_low=up_low)

    def both(name):
        return jnp.concatenate([s[name] for s in saved], axis=0)

    g_down = scatter_cols(left_t(both("inner_low"), both("mlp_low")))
    hidden_low = both("hidden_low")
    g_gate = scatter_rows(left_t(hidden_low, both("gate_low")))
    g_up = scatter_rows(left_t(hidden_low, both("up_low")))

    ga_grad = 0.0
    backs = all_reduce([right_t(s["gate_low"], wg) + right_t(s["up_low"], wu) for s in saved])
    for m in range(micros):
        s = saved[m]
        hidden_grad = s["c"] + backs[m]
        ga_grad += jnp.sum(hidden_grad * s["attn_unit"], axis=0)
        unit_grad = hidden_grad * a_gain
        proj_low = (
            s["attn_inv"]
            * (unit_grad
               - s["attn_unit"] * jnp.mean(unit_grad * s["attn_unit"], axis=1, keepdims=True))
        ).astype(bf16)
        attn_grad = right_t(proj_low, wo).astype(bf16)
        dq, dko, dvo, dkt, dvt, dkb, dvb = attend_backward(
            s["meta"], s["q_low"], attn_grad, s["lse"], s["kv"]
        )
        returned = return_to_sources(
            jnp.concatenate(
                [jnp.concatenate([dkt, dvt], axis=1), jnp.concatenate([dkb, dvb], axis=1)], axis=0
            )
        )
        cols = dko.shape[1]
        dk = dko + returned[:, :cols]
        dv = dvo + returned[:, cols:]
        s.update(hidden_grad=hidden_grad, proj_low=proj_low, dq=dq, dk=dk, dv=dv)

    qg_grad = kg_grad = 0.0
    backs = []
    for m in range(micros):
        s = saved[m]
        q_unit, k_unit = s["q_unit"], s["k_unit"]
        qg_grad += jnp.sum(s["dq"] * q_unit, axis=0)
        kg_grad += jnp.sum(s["dk"] * k_unit, axis=0)
        q_scaled, k_scaled = s["dq"] * q_gain, s["dk"] * k_gain
        q_inner, k_inner = lax.psum(
            (jnp.sum(q_scaled * q_unit, axis=1), jnp.sum(k_scaled * k_unit, axis=1)), "tensor"
        )
        qr_low = (s["q_inv"] * (q_scaled - q_unit * (q_inner / full_width)[:, None])).astype(bf16)
        kr_low = (s["k_inv"] * (k_scaled - k_unit * (k_inner / full_width)[:, None])).astype(bf16)
        vr_low = s["dv"].astype(bf16)
        backs.append(right_t(qr_low, wq) + right_t(kr_low, wk) + right_t(vr_low, wv))
        s.update(qr_low=qr_low, kr_low=kr_low, vr_low=vr_low)

    grads = [s["hidden_grad"] + back for s, back in zip(saved, all_reduce(backs))]
    x = both("x")
    g_out = scatter_cols(left_t(both("attn_low"), both("proj_low")))
    g_query = scatter_rows(left_t(x, both("qr_low")))
    g_key = scatter_rows(left_t(x, both("kr_low")))
    g_value = scatter_rows(left_t(x, both("vr_low")))
    return (
        jnp.stack(outs)[:, None],
        jnp.stack(grads)[:, None],
        g_query,
        g_key,
        g_value,
        g_out,
        g_gate,
        g_up,
        g_down,
        scatter_cols(qg_grad.reshape(heads, HD)),
        scatter_cols(kg_grad.reshape(heads, HD)),
        scatter_rows(ga_grad),
        scatter_rows(gm_grad),
    )


def solution(mesh):
    rows = P(None, "dp", "seq", None)
    by_row = P(("dp", "seq"), "tensor")
    by_col = P("tensor", ("dp", "seq"))
    gain = P(("dp", "seq"))
    tree = P(None, "dp", None)
    weights = (by_row, by_row, by_row, by_col, by_row, by_row, by_col, by_col, by_col, gain, gain)
    return jax.shard_map(
        per_device,
        mesh=mesh,
        in_specs=(rows, rows) + weights + (tree, tree),
        out_specs=(rows, rows) + weights,
        check_vma=False,
    )
```

time: 3710 us -> 1550 us (0.42)
  waiting for transfers between devices: 2470 us -> 182 us
  Pallas kernels: 0 us -> 680 us
  matrix products: 644 us -> 273 us
  local copies, waits for them, and re-layouts: 208 us -> 44.3 us
  blocking collectives: 95.8 us -> 139 us
  other arithmetic: 240 us -> 197 us
    psum x4 -> x0, waiting for transfers between devices: 1480 us -> none  [the longest x1 426 us: per_device(): lax.psum(right_t(gate_low, wg_full) + right_t(up_low, wu_full), 'tensor')]
    pallas_call x0 -> x8, Pallas kernels: none -> 680 us  [the longest x4 611 us: line_sum(): pl.pallas_call(functools.partial(line_kernel, n, chunks), in_specs=[pl.Bl...]
    reduce_scatter x18 -> x7, waiting for transfers between devices: 694 us -> 51.5 us  [the longest x5 51.5 us: scatter_rows(): lax.psum_scatter(item.astype(bf16), ('dp', 'seq'), scatter_dimension=0, t...]
    dot_general x56 -> x14, matrix products: 425 us -> 95.7 us  [matmul(): return jnp.dot(left, right, preferred_element_type=f32)]
    unnamed x41 -> x18, waiting for transfers between devices: 139 us -> 3.8 us
    all_gather x11 -> x7, waiting for transfers between devices: 154 us -> 32 us  [the longest x5 32 us: gather_rows(): return lax.all_gather(item, ('dp', 'seq'), axis=0, tiled=True)]
    ppermute x0 -> x8, waiting for transfers between devices: none -> 94.4 us  [the longest x2 59.2 us: return_to_sources(): lax.ppermute(total.astype(bf16), 'seq', [(i + half, i) for i in range(hal...]
    dynamic_update_slice x12 -> x0, local copies, waits for them, and re-layouts: 85.6 us -> none  [attend_forward(): lax.map(one_block, jnp.arange(n_rows // q_block, dtype=jnp.int32))]
  transfers between devices with their start and end apart: 37 -> 24, of which waited for: 27 -> 6; matrix products, arithmetic and copies ran while one was open for 18% -> 21% of each run, Pallas kernels for 0% -> 23%
where the time goes in v1:
time: 1550 us; the launch traced here: 1540 us
  Pallas kernels  680 us (44%)
  matrix products  273 us (18%)
  other arithmetic  197 us (13%)
  waiting for transfers between devices  182 us (12%)
  blocking collectives  139 us (9%)
  local copies, waits for them, and re-layouts  44.3 us (3%)
  between operations  16.9 us (1%)
    pallas_call x4, Pallas kernels, line_sum(): pl.pallas_call(functools.partial(line_kernel, n, chunks), in_specs=[pl.Bl...  611 us
    dot_general x14, matrix products, right_t(): lax.dot_general(left, right, (((1,), (1,)), ((), ())), preferred_element_...  100 us
    dot_general x14, matrix products, matmul(): return jnp.dot(left, right, preferred_element_type=f32)  95.7 us
    dot_general x7, matrix products, left_t(): lax.dot_general(left, right, (((0,), (0,)), ((), ())), preferred_element_...  77.2 us
    all_gather x2, blocking collectives, gather_cols(): return lax.all_gather(item, ('dp', 'seq'), axis=1, tiled=True)  70.7 us
    ppermute x2, waiting for transfers between devices, return_to_sources(): lax.ppermute(total.astype(bf16), 'seq', [(i + half, i) for i in range(hal...  59.2 us
    reduce_scatter x5, waiting for transfers between devices, scatter_rows(): lax.psum_scatter(item.astype(bf16), ('dp', 'seq'), scatter_dimension=0, t...  51.5 us
    pallas_call x2, Pallas kernels, attend_backward(): pl.pallas_call(functools.partial(attn_bwd_kernel, trunk_rows, n_q), grid_...  44.3 us
  transfers between devices with their start and end apart: 24, of which 6 were waited for; matrix products, arithmetic and copies ran while one was open for 21% of the time, Pallas kernels for 23%

profile of v1, /device:TPU:0, one launch (start us, length us, event | category | flops | bytes accessed | tf_op | source)
XLA Modules:
  0.0 1544.3 jit_solution(3194295234677961815)
XLA Ops:
  11.2 10.3 all-gather.1
  21.6 18.9 %all-gather.14.cloned.1.call-done = bf16[2048,512]{1,0:T(8,128)(2,1)} async-done(((bf16[256,512]{1,0:T(8,128)(2,1)}), bf16[2048,512]{1,0:T(8,128)(2,1)}) %all-gather.14.cloned.1.call-update) | async-done | bytes 2097168 | tf_op jit(solution)/shard_map/all_gather | solution.py:389
  57.3 13.1 all-gather.12.cloned.1.call-done
  80.9 18.7 %all-reduce.3 = (f32[768]{0:T(1024)S(1)}, f32[768]{0:T(1024)S(1)}, f32[768]{0:T(1024)S(1)}, f32[768]{0:T(1024)S(1)}) all-reduce(f32[768]{0:T(1024)S(1)} %get-tuple-element.202, f32[768]{0:T(1024)S(1)} %get-tuple-element.204, f32[768]{0:T(1024)S(1)} %get-tuple-element.206, ...), channel_id=1, replica_groups=mesh['dp'=2,'seq'=4,'tensor'=4] {'tensor'}, use_global_device_ids=true, to_apply=%region_11.12 | all-reduce | flops 3072 | bytes 24576 | tf_op jit(solution)/shard_map/psum | solution.py:464
  121.2 35.2 %collective-permute-done = bf16[768,1024]{1,0:T(8,128)(2,1)} collective-permute-done((bf16[768,1024]{1,0:T(8,128)(2,1)}, bf16[768,1024]{1,0:T(8,128)(2,1)}, u32[]{:S(2)}, u32[]{:S(2)}) %collective-permute-start) | collective-permute-done | bytes 1572896 | tf_op jit(solution)/shard_map/ppermute | solution.py:354
  158.1 60.3 %all-gather = bf16[8,16,4]{1,2,0:T(4,128)(2,1)S(1)} all-gather(bf16[1,16,4]{1,2,0:T(4,128)(2,1)S(1)} %bitcast.193), channel_id=1, replica_groups=mesh['dp'=2,'seq'=4,'tensor'=4] {'dp','seq'}, dimensions={0}, use_global_device_ids=true | all-gather | bytes 1152 | tf_op jit(solution)/shard_map/all_gather | solution.py:393
  221.8 10.5 all-gather.2
  232.3 9.4 all-gather.3
  249.0 12.4 attend_forward.2
  265.7 12.4 attend_forward.3
  291.5 154.7 %line_sum.4 = bf16[1536,2048]{1,0:T(8,128)(2,1)} custom-call(bf16[1536,2048]{1,0:T(8,128)(2,1)} %pad_maximum_fusion.part), custom_call_target="tpu_custom_call" | custom-call | tf_op jit(solution)/shard_map/line_sum/pallas_call | solution.py:189
  455.0 5.8 fusion.46
  460.9 11.9 fusion.89
  472.7 8.5 fusion.90
  481.3 13.9 multiply_convert_fusion.3
  495.2 9.0 multiply_convert_fusion.2
  504.2 10.2 convolution_convert_fusion.4
  514.4 6.9 convolution_convert_fusion.3
  525.1 152.5 %line_sum.5 = bf16[1536,2048]{1,0:T(8,128)(2,1)} custom-call(bf16[1536,2048]{1,0:T(8,128)(2,1)} %pad_maximum_fusion.1.part), custom_call_target="tpu_custom_call" | custom-call | tf_op jit(solution)/shard_map/line_sum/pallas_call | solution.py:189
  677.6 9.1 convert_element_type.306
  692.0 9.6 fusion.7
  701.6 15.0 fusion.9
  716.6 16.4 %fusion.17 = (bf16[768,2048]{1,0:T(8,128)(2,1)}, bf16[768,2048]{1,0:T(8,128)(2,1)}) fusion(f32[768,2048]{1,0:T(8,128)} %fusion.89, bf16[768,2048]{1,0:T(8,128)(2,1)} %get-tuple-element.213, bf16[768,2048]{1,0:T(8,128)(2,1)S(1)} %get-tuple-element.154, bf16[2048,2048]{1,0:T(8,128)(2,1)} %all-gather.24.cloned.1.call-done), kind=kOutput, calls=%fused_computation.33 | convolution fusion | flops 6467616768 | bytes 27262976 | tf_op jit(solution)/shard_map/dot_general | solution.py:28
  733.0 12.1 fusion.91
  745.1 14.8 fusion.25
  759.9 11.9 fusion.92
  771.8 10.5 add_convert_fusion.3
  782.3 11.8 add_convert_fusion.2
  797.9 152.0 %line_sum.6 = bf16[1536,2048]{1,0:T(8,128)(2,1)} custom-call(bf16[1536,2048]{1,0:T(8,128)(2,1)} %pad_maximum_fusion.2.part), custom_call_target="tpu_custom_call" | custom-call | tf_op jit(solution)/shard_map/line_sum/pallas_call | solution.py:189
  949.9 9.2 convert_element_type.330
  959.2 8.4 multiply_reduce_fusion.3
  967.6 8.3 multiply_convert_fusion.1
  980.3 22.0 %attend_backward.3 = (f32[768,512]{1,0:T(8,128)S(1)}, f32[768,512]{1,0:T(8,128)S(1)}, f32[768,512]{1,0:T(8,128)S(1)}, bf16[768,512]{1,0:T(8,128)(2,1)S(1)}, bf16...) custom-call(s32[3,5]{1,0:T(4,128)S(1)} %stack.33.meta, ...), custom_call_target="tpu_custom_call" | custom-call | tf_op jit(solution)/shard_map/attend_backward/pallas_call | solution.py:316
  1008.2 22.2 %attend_backward.2 = (f32[768,512]{1,0:T(8,128)S(1)}, f32[768,512]{1,0:T(8,128)S(1)}, f32[768,512]{1,0:T(8,128)S(1)}, bf16[768,512]{1,0:T(8,128)(2,1)S(1)}, bf16...) custom-call(s32[3,5]{1,0:T(4,128)S(1)} %stack.32.meta, ...), custom_call_target="tpu_custom_call" | custom-call | tf_op jit(solution)/shard_map/attend_backward/pallas_call | solution.py:316
  1054.5 6.7 slice_bitcast_fusion.1
  1061.2 21.8 %collective-permute-done.7 = bf16[768,1024]{1,0:T(8,128)(2,1)} collective-permute-done((bf16[768,1024]{1,0:T(8,128)(2,1)}, bf16[768,1024]{1,0:T(8,128)(2,1)}, u32[]{:S(2)}, u32[]{:S(2)}) %collective-permute-start.7) | collective-permute-done | bytes 1572896 | tf_op jit(solution)/shard_map/ppermute | solution.py:384
  1086.6 37.4 %collective-permute-done.5 = bf16[768,1024]{1,0:T(8,128)(2,1)} collective-permute-done((bf16[768,1024]{1,0:T(8,128)(2,1)}, bf16[768,1024]{1,0:T(8,128)(2,1)}, u32[]{:S(2)}, u32[]{:S(2)}) %collective-permute-start.5) | collective-permute-done | bytes 1572896 | tf_op jit(solution)/shard_map/ppermute | solution.py:384
  1129.7 16.8 %all-reduce.2 = (f32[768]{0:T(1024)S(1)}, f32[768]{0:T(1024)S(1)}, f32[768]{0:T(1024)S(1)}, f32[768]{0:T(1024)S(1)}) all-reduce(f32[768]{0:T(1024)S(1)} %get-tuple-element.186, f32[768]{0:T(1024)S(1)} %get-tuple-element.184, f32[768]{0:T(1024)S(1)} %get-tuple-element.133, ...), channel_id=1, replica_groups=mesh['dp'=2,'seq'=4,'tensor'=4] {'tensor'}, use_global_device_ids=true, to_apply=%region_27.28 | all-reduce | flops 3072 | bytes 24576 | tf_op jit(solution)/shard_map/psum | solution.py:569
  1160.7 7.7 convolution_convert_fusion.8
  1179.0 18.5 %convolution_convert_fusion = bf16[2048,2048]{1,0:T(8,128)(2,1)} fusion(bf16[768,2048]{1,0:T(8,128)(2,1)} %get-tuple-element.210, bf16[768,2048]{1,0:T(8,128)(2,1)} %get-tuple-element.212, bf16[768,2048]{1,0:T(8,128)(2,1)} %get-tuple-element.155, bf16[768,2048]{1,0:T(8,128)(2,1)S(1)} %copy-done.65), kind=kOutput, calls=%fused_computation.13 | convolution fusion | flops 12914262016 | bytes 20971520 | tf_op jit(solution)/shard_map/dot_general | solution.py:24
  1199.4 18.5 %convolution_convert_fusion.1 = bf16[2048,2048]{1,0:T(8,128)(2,1)} fusion(bf16[768,2048]{1,0:T(8,128)(2,1)} %get-tuple-element.162, bf16[768,2048]{1,0:T(8,128)(2,1)} %get-tuple-element.160, bf16[768,2048]{1,0:T(8,128)(2,1)} %get-tuple-element.157, bf16[768,2048]{1,0:T(8,128)(2,1)S(1)} %copy-done.82), kind=kOutput, calls=%fused_computation.14 | convolution fusion | flops 12914262016 | bytes 20971520 | tf_op jit(solution)/shard_map/dot_general | solution.py:24
  1218.2 18.6 %convolution_convert_fusion.2 = bf16[2048,2048]{1,0:T(8,128)(2,1)} fusion(bf16[768,2048]{1,0:T(8,128)(2,1)} %get-tuple-element.163, bf16[768,2048]{1,0:T(8,128)(2,1)} %get-tuple-element.161, bf16[768,2048]{1,0:T(8,128)(2,1)} %get-tuple-element.157, bf16[768,2048]{1,0:T(8,128)(2,1)S(1)} %copy-done.82), kind=kOutput, calls=%fused_computation.15 | convolution fusion | flops 12914262016 | bytes 20971520 | tf_op jit(solution)/shard_map/dot_general | solution.py:24
  1238.7 12.7 all-reduce.4
  1285.8 151.7 %line_sum.7 = bf16[1536,2048]{1,0:T(8,128)(2,1)} custom-call(bf16[1536,2048]{1,0:T(8,128)(2,1)} %pad_maximum_fusion.3.part), custom_call_target="tpu_custom_call" | custom-call | tf_op jit(solution)/shard_map/line_sum/pallas_call | solution.py:189
  1437.5 9.4 convert_element_type.351
  1446.9 11.5 fusion.29
  1458.4 11.8 maximum_bitcast_fusion
  1482.9 51.5 %reduce-scatter.22.cloned.1.call-done = bf16[256,2048]{1,0:T(8,128)(2,1)} async-done(((bf16[2048,2048]{1,0:T(8,128)(2,1)}), bf16[256,2048]{1,0:T(8,128)(2,1)}) %reduce-scatter.22.cloned.1.call-update) | async-done | bytes 1048592 | tf_op jit(solution)/shard_map/reduce_scatter | solution.py:397
  (435 shorter events, 224.9 us)
Async XLA Ops:
  7.2 33.4 %all-gather.14.cloned.1.call-start = ((), (), s32[]{:S(2)}) async-start(), calls=%async_computation.10 | async-start | bytes 2359296 | tf_op jit(solution)/shard_map/all_gather | solution.py:389
  7.9 62.4 %all-gather.12.cloned.1.call-start = ((), (), s32[]{:S(2)}) async-start(), calls=%async_computation.9 | async-start | bytes 2359296 | tf_op jit(solution)/shard_map/all_gather | solution.py:389
  8.7 93.2 %all-gather.16.cloned.1.call-start = ((), (), s32[]{:S(2)}) async-start(), calls=%async_computation.11 | async-start | bytes 2359296 | tf_op jit(solution)/shard_map/all_gather | solution.py:389
  9.4 272.7 %all-gather.18.cloned.1.call-start = ((), (), s32[]{:S(2)}) async-start(), calls=%async_computation.12 | async-start | bytes 2359296 | tf_op jit(solution)/shard_map/all_gather | solution.py:393
  10.0 450.9 %all-gather.20.cloned.1.call-start = ((), (), s32[]{:S(2)}) async-start(), calls=%async_computation.13 | async-start | bytes 9437184 | tf_op jit(solution)/shard_map/all_gather | solution.py:389
  10.6 470.7 %all-gather.22.cloned.1.call-start = ((), (), s32[]{:S(2)}) async-start(), calls=%async_computation.14 | async-start | bytes 9437184 | tf_op jit(solution)/shard_map/all_gather | solution.py:389
  11.1 493.0 %all-gather.24.cloned.1.call-start = ((), (), s32[]{:S(2)}) async-start(), calls=%async_computation.15 | async-start | bytes 9437184 | tf_op jit(solution)/shard_map/all_gather | solution.py:393
  21.6 78.0 %copy-start.94 = (f32[128,4]{0,1:T(4,128)}, f32[128,4]{0,1:T(4,128)S(1)}, u32[]{:S(2)}) copy-start(f32[128,4]{0,1:T(4,128)S(1)} %reshape.233) | copy-start | bytes 6148
  99.6 144.2 %copy-start.90 = (f32[768]{0:T(1024)}, f32[768]{0:T(1024)S(1)}, u32[]{:S(2)}) copy-start(f32[768]{0:T(1024)S(1)} %get-tuple-element.219) | copy-start | bytes 9220
  99.6 144.2 %copy-start.92 = (f32[768]{0:T(1024)}, f32[768]{0:T(1024)S(1)}, u32[]{:S(2)}) copy-start(f32[768]{0:T(1024)S(1)} %get-tuple-element.221) | copy-start | bytes 9220
  107.6 48.8 %collective-permute-start = (bf16[768,1024]{1,0:T(8,128)(2,1)}, bf16[768,1024]{1,0:T(8,128)(2,1)}, u32[]{:S(2)}, u32[]{:S(2)}) collective-permute-start(bf16[768,1024]{1,0:T(8,128)(2,1)} %pad_maximum_fusion.11), channel_id=1, source_target_pairs={{0,8},{4,12},{1,9},{5,13},{2,10},{6,14},{3,11},{7,15},{16,24},{20,... | collective-permute-start | bytes 4718600 | tf_op jit(solution)/shard_map/ppermute | solution.py:354
  112.1 1145.8 %reduce-scatter.28.cloned.1.call-start = ((), (), s32[]{:S(2)}) async-start(), calls=%async_computation.23 | async-start | bytes 36864
  117.9 40.2 %copy-start.102 = (bf16[4,16]{1,0:T(4,128)(2,1)S(1)}, bf16[4,16]{1,0:T(4,128)(2,1)}, u32[]{:S(2)}) copy-start(bf16[4,16]{1,0:T(4,128)(2,1)} %param.24) | copy-start | bytes 388
  117.9 100.7 %collective-permute-start.2 = (bf16[768,1024]{1,0:T(8,128)(2,1)}, bf16[768,1024]{1,0:T(8,128)(2,1)}, u32[]{:S(2)}, u32[]{:S(2)}) collective-permute-start(bf16[768,1024]{1,0:T(8,128)(2,1)} %pad_maximum_fusion.12), channel_id=1, source_target_pairs={{0,8},{4,12},{1,9},{5,13},{2,10},{6,14},{3,11},{7,15},{16,24},{20,... | collective-permute-start | bytes 4718600 | tf_op jit(solution)/shard_map/ppermute | solution.py:354
  158.1 63.7 %copy-start.110 = (bf16[256]{0:T(256)(128)(2,1)S(1)}, bf16[256]{0:T(256)(128)(2,1)}, u32[]{:S(2)}) copy-start(bf16[256]{0:T(256)(128)(2,1)} %param.26) | copy-start | bytes 1540
  158.1 74.2 %copy-start.111 = (bf16[256]{0:T(256)(128)(2,1)S(1)}, bf16[256]{0:T(256)(128)(2,1)}, u32[]{:S(2)}) copy-start(bf16[256]{0:T(256)(128)(2,1)} %param.27) | copy-start | bytes 1540
  158.1 87.9 %collective-permute-start.1 = (bf16[768,1024]{1,0:T(8,128)(2,1)}, bf16[768,1024]{1,0:T(8,128)(2,1)}, u32[]{:S(2)}, u32[]{:S(2)}) collective-permute-start(bf16[768,1024]{1,0:T(8,128)(2,1)} %broadcast_select_fusion.7), channel_id=1, source_target_pairs={{0,4},{4,0},{8,12},{12,8},{1,5},{5,1},{9,13},{13,9},{2,6},{6,2},{1... | collective-permute-start | bytes 4718600 | tf_op jit(solution)/shard_map/ppermute | solution.py:356
  220.4 41.1 %collective-permute-start.3 = (bf16[768,1024]{1,0:T(8,128)(2,1)}, bf16[768,1024]{1,0:T(8,128)(2,1)}, u32[]{:S(2)}, u32[]{:S(2)}) collective-permute-start(bf16[768,1024]{1,0:T(8,128)(2,1)} %broadcast_select_fusion.6), channel_id=1, source_target_pairs={{0,4},{4,0},{8,12},{12,8},{1,5},{5,1},{9,13},{13,9},{2,6},{6,2},{1... | collective-permute-start | bytes 4718600 | tf_op jit(solution)/shard_map/ppermute | solution.py:356
  221.6 27.1 %copy-start.96 = (f32[128,4]{0,1:T(4,128)}, f32[128,4]{0,1:T(4,128)S(1)}, u32[]{:S(2)}) copy-start(f32[128,4]{0,1:T(4,128)S(1)} %reshape.232) | copy-start | bytes 6148
  246.0 18.7 %copy-start.18 = (bf16[768,512]{1,0:T(8,128)(2,1)}, bf16[768,512]{1,0:T(8,128)(2,1)S(1)}, u32[]{:S(2)}) copy-start(bf16[768,512]{1,0:T(8,128)(2,1)S(1)} %get-tuple-element.191.q) | copy-start | bytes 2359300
  797.9 161.3 %slice-start.3 = ((s8[12582912]{0:T(1024)(128)(4,1)}), s8[4194304]{0:T(1024)(128)(4,1)S(1)}, s32[]{:S(2)}) async-start(s8[12582912]{0:T(1024)(128)(4,1)} %bitcast.169), calls=%async_computation.28 | async-start | bytes 8388608
  797.9 161.3 %slice-start.4 = ((s8[12582912]{0:T(1024)(128)(4,1)}), s8[4194304]{0:T(1024)(128)(4,1)S(1)}, s32[]{:S(2)}) async-start(s8[12582912]{0:T(1024)(128)(4,1)} %bitcast.169), calls=%async_computation.29 | async-start | bytes 8388608
  975.9 29.9 %copy-start.67 = (bf16[768,2048]{1,0:T(8,128)(2,1)}, bf16[768,2048]{1,0:T(8,128)(2,1)S(1)}, u32[]{:S(2)}) copy-start(bf16[768,2048]{1,0:T(8,128)(2,1)S(1)} %get-tuple-element.150) | copy-start | bytes 9437188
  1005.9 32.9 %collective-permute-start.6 = (bf16[768,1024]{1,0:T(8,128)(2,1)}, bf16[768,1024]{1,0:T(8,128)(2,1)}, u32[]{:S(2)}, u32[]{:S(2)}) collective-permute-start(bf16[768,1024]{1,0:T(8,128)(2,1)} %broadcast_select_fusion.2), channel_id=1, source_target_pairs={{0,4},{4,0},{8,12},{12,8},{1,5},{5,1},{9,13},{13,9},{2,6},{6,2},{1... | collective-permute-start | bytes 4718600 | tf_op jit(solution)/shard_map/ppermute | solution.py:383
  1034.3 10.4 collective-permute-start.4
  1038.7 220.6 %reduce-scatter.20.cloned.1.call-start = ((), (), s32[]{:S(2)}) async-start(), calls=%async_computation.19 | async-start | bytes 2359296 | tf_op jit(solution)/shard_map/reduce_scatter | solution.py:403
  1043.1 39.9 %collective-permute-start.7 = (bf16[768,1024]{1,0:T(8,128)(2,1)}, bf16[768,1024]{1,0:T(8,128)(2,1)}, u32[]{:S(2)}, u32[]{:S(2)}) collective-permute-start(bf16[768,1024]{1,0:T(8,128)(2,1)} %fusion.54), channel_id=1, source_target_pairs={{8,0},{12,4},{9,1},{13,5},{10,2},{14,6},{11,3},{15,7},{24,16},{28,... | collective-permute-start | bytes 4718600 | tf_op jit(solution)/shard_map/ppermute | solution.py:384
  1048.4 75.5 %collective-permute-start.5 = (bf16[768,1024]{1,0:T(8,128)(2,1)}, bf16[768,1024]{1,0:T(8,128)(2,1)}, u32[]{:S(2)}, u32[]{:S(2)}) collective-permute-start(bf16[768,1024]{1,0:T(8,128)(2,1)} %fusion.53), channel_id=1, source_target_pairs={{8,0},{12,4},{9,1},{13,5},{10,2},{14,6},{11,3},{15,7},{24,16},{28,... | collective-permute-start | bytes 4718600 | tf_op jit(solution)/shard_map/ppermute | solution.py:384
  1054.4 415.8 %reduce-scatter.30.cloned.1.call-start = ((), (), s32[]{:S(2)}) async-start(), calls=%async_computation.24 | async-start | bytes 36864
  1054.5 28.5 %copy-start.51 = (bf16[768,1024]{1,0:T(8,128)(2,1)S(1)}, bf16[768,1024]{1,0:T(8,128)(2,1)}, u32[]{:S(2)}) copy-start(bf16[768,1024]{1,0:T(8,128)(2,1)} %copy-done.50) | copy-start | bytes 4718596
  1061.2 62.7 %copy-start.49 = (bf16[768,1024]{1,0:T(8,128)(2,1)S(1)}, bf16[768,1024]{1,0:T(8,128)(2,1)}, u32[]{:S(2)}) copy-start(bf16[768,1024]{1,0:T(8,128)(2,1)} %copy-done.47) | copy-start | bytes 4718596
  1061.2 62.7 %copy-start.54 = (bf16[768,1024]{1,0:T(8,128)(2,1)S(1)}, bf16[768,1024]{1,0:T(8,128)(2,1)}, u32[]{:S(2)}) copy-start(bf16[768,1024]{1,0:T(8,128)(2,1)} %copy-done.52) | copy-start | bytes 4718596
  1086.5 40.8 %copy-start.42 = (f32[768,1024]{1,0:T(8,128)}, f32[768,1024]{1,0:T(8,128)S(1)}, u32[]{:S(2)}) copy-start(f32[768,1024]{1,0:T(8,128)S(1)} %add_select_fusion) | copy-start | bytes 9437188
  1086.5 40.8 %copy-start.25 = (f32[768,512]{1,0:T(8,128)S(1)}, f32[768,512]{1,0:T(8,128)}, u32[]{:S(2)}) copy-start(f32[768,512]{1,0:T(8,128)} %copy-done.24) | copy-start | bytes 4718596
  1086.5 40.8 %copy-start.27 = (f32[768,512]{1,0:T(8,128)S(1)}, f32[768,512]{1,0:T(8,128)}, u32[]{:S(2)}) copy-start(f32[768,512]{1,0:T(8,128)} %copy-done.26) | copy-start | bytes 4718596
  1086.5 40.8 %copy-start.39 = (f32[768,512]{1,0:T(8,128)S(1)}, f32[768,512]{1,0:T(8,128)}, u32[]{:S(2)}) copy-start(f32[768,512]{1,0:T(8,128)} %copy.92) | copy-start | bytes 4718596
  1086.5 40.7 %copy-start.41 = (f32[768,512]{1,0:T(8,128)S(1)}, f32[768,512]{1,0:T(8,128)}, u32[]{:S(2)}) copy-start(f32[768,512]{1,0:T(8,128)} %copy.86) | copy-start | bytes 4718596
  1086.5 40.7 %copy-start.87 = (f32[768]{0:T(1024)S(1)}, f32[768]{0:T(1024)}, u32[]{:S(2)}) copy-start(f32[768]{0:T(1024)} %copy-done.86) | copy-start | bytes 9220
  1086.5 40.7 %copy-start.89 = (f32[768]{0:T(1024)S(1)}, f32[768]{0:T(1024)}, u32[]{:S(2)}) copy-start(f32[768]{0:T(1024)} %copy-done.88) | copy-start | bytes 9220
  1086.6 40.7 %copy-start.95 = (f32[128,4]{0,1:T(4,128)S(1)}, f32[128,4]{0,1:T(4,128)}, u32[]{:S(2)}) copy-start(f32[128,4]{0,1:T(4,128)} %copy-done.94) | copy-start | bytes 6148
  1146.6 325.1 %reduce-scatter.18.cloned.1.call-start = ((), (), s32[]{:S(2)}) async-start(), calls=%async_computation.18 | async-start | bytes 2359296 | tf_op jit(solution)/shard_map/reduce_scatter | solution.py:397
  1160.6 312.9 %reduce-scatter.16.cloned.1.call-start = ((), (), s32[]{:S(2)}) async-start(), calls=%async_computation.17 | async-start | bytes 2359296 | tf_op jit(solution)/shard_map/reduce_scatter | solution.py:397
  1168.4 307.0 %reduce-scatter.14.cloned.1.call-start = ((), (), s32[]{:S(2)}) async-start(), calls=%async_computation.16 | async-start | bytes 2359296 | tf_op jit(solution)/shard_map/reduce_scatter | solution.py:397
  1178.8 298.4 %reduce-scatter.26.cloned.1.call-start = ((), (), s32[]{:S(2)}) async-start(), calls=%async_computation.22 | async-start | bytes 9437184 | tf_op jit(solution)/shard_map/reduce_scatter | solution.py:403
  1197.5 282.6 %reduce-scatter.24.cloned.1.call-start = ((), (), s32[]{:S(2)}) async-start(), calls=%async_computation.21 | async-start | bytes 9437184 | tf_op jit(solution)/shard_map/reduce_scatter | solution.py:397
  1217.9 316.5 %reduce-scatter.22.cloned.1.call-start = ((), (), s32[]{:S(2)}) async-start(), calls=%async_computation.20 | async-start | bytes 9437184 | tf_op jit(solution)/shard_map/reduce_scatter | solution.py:397
  1285.8 161.1 %slice-start.6 = ((s8[12582912]{0:T(1024)(128)(4,1)}), s8[4194304]{0:T(1024)(128)(4,1)S(1)}, s32[]{:S(2)}) async-start(s8[12582912]{0:T(1024)(128)(4,1)} %bitcast.171), calls=%async_computation.31 | async-start | bytes 8388608
  1285.8 161.1 %slice-start.7 = ((s8[12582912]{0:T(1024)(128)(4,1)}), s8[4194304]{0:T(1024)(128)(4,1)S(1)}, s32[]{:S(2)}) async-start(s8[12582912]{0:T(1024)(128)(4,1)} %bitcast.171), calls=%async_computation.32 | async-start | bytes 8388608
  (102 other events, 529.1 us)
Sparse Core Ops, SparseCore 0:
  9.9 30.5 all-gather.13
  42.4 27.8 all-gather.11
  72.2 27.8 all-gather.15
  101.9 32.6 all-gather.17
  136.4 83.0 all-gather.19
  221.2 57.4 all-gather.21
  280.5 55.9 all-gather.23
  1038.9 30.4 reduce-scatter.27
  1073.0 49.7 reduce-scatter.19
  1146.7 27.5 reduce-scatter.29
  1178.5 41.2 reduce-scatter.17
  1223.5 41.2 reduce-scatter.15
  1269.0 41.2 reduce-scatter.13
  1313.5 71.2 reduce-scatter.25
  1388.6 71.2 reduce-scatter.23
  1463.1 71.2 reduce-scatter.21

commit v2 on v1

--- a/solution.py
+++ b/solution.py
@@ -1,4 +1,5 @@
 import functools
+import math
 
 import jax
 import jax.numpy as jnp
@@ -29,6 +30,22 @@
 
 
 MESH = pl.DeviceIdType.MESH
+
+
+def cost(us):
+    return pl.CostEstimate(flops=int(us * 1.1e9), bytes_accessed=0, transcendentals=0)
+
+
+def after(value, *earlier):
+    hbm = pl.BlockSpec(memory_space=pl.ANY)
+    return pl.pallas_call(
+        lambda *refs: None,
+        in_specs=[hbm] * (1 + len(earlier)),
+        out_specs=hbm,
+        out_shape=jax.ShapeDtypeStruct(value.shape, value.dtype),
+        input_output_aliases={0: 0},
+        name="after",
+    )(value, *earlier)
 
 
 class Line:
@@ -182,7 +199,7 @@
     line.end()
 
 
-def line_sum(part):
+def line_sum(part, collective_id):
     rows, width = part.shape
     n = lax.axis_size("tensor")
     chunks = rows // 48
@@ -193,10 +210,643 @@
         out_shape=jax.ShapeDtypeStruct(part.shape, bf16),
         scratch_shapes=line_scratch(rows, width, chunks),
         compiler_params=pltpu.CompilerParams(
-            collective_id=0, has_side_effects=True, vmem_limit_bytes=48 << 20
+            collective_id=collective_id, has_side_effects=True, vmem_limit_bytes=48 << 20
         ),
+        cost_estimate=cost(rows // 9),
         name="line_sum",
     )(part)
+
+
+def small_kernel(n, x, out, land, send, recv):
+    me = lax.axis_index("tensor")
+    barrier = pltpu.get_barrier_semaphore()
+    peers = [lax.rem(me + d, n) for d in range(1, n)]
+    for peer in peers:
+        pl.semaphore_signal(barrier, inc=1, device_id={"tensor": peer}, device_id_type=MESH)
+    land[me] = x[...]
+    pl.semaphore_wait(barrier, n - 1)
+    copies = [
+        pltpu.make_async_remote_copy(
+            src_ref=x,
+            dst_ref=land.at[me],
+            send_sem=send.at[d],
+            recv_sem=recv.at[me],
+            device_id={"tensor": peer},
+            device_id_type=MESH,
+        )
+        for d, peer in enumerate(peers)
+    ]
+    for copy in copies:
+        copy.start()
+    for d, peer in enumerate(peers):
+        pltpu.make_async_remote_copy(
+            src_ref=x,
+            dst_ref=land.at[peer],
+            send_sem=send.at[d],
+            recv_sem=recv.at[peer],
+            device_id={"tensor": peer},
+            device_id_type=MESH,
+        ).wait_recv()
+    total = land[0]
+    for place in range(1, n):
+        total += land[place]
+    out[...] = total
+    for copy in copies:
+        copy.wait_send()
+
+
+def small_sum(x, collective_id):
+    n = lax.axis_size("tensor")
+    flat = x.reshape(-1, 128)
+    dma = pltpu.SemaphoreType.DMA
+    vmem = pl.BlockSpec(memory_space=pltpu.VMEM)
+    return pl.pallas_call(
+        functools.partial(small_kernel, n),
+        in_specs=[vmem],
+        out_specs=vmem,
+        out_shape=jax.ShapeDtypeStruct(flat.shape, f32),
+        scratch_shapes=[pltpu.VMEM((n,) + flat.shape, f32), dma((n - 1,)), dma((n,))],
+        compiler_params=pltpu.CompilerParams(
+            collective_id=collective_id, has_side_effects=True
+        ),
+        cost_estimate=cost(7),
+        name="small_sum",
+    )(flat).reshape(x.shape)
+
+
+LINE_ROWS = 48
+LAG = 3
+TILE = 256
+NAMES = (
+    "part", "x", "cot", "w", "ga", "gm", "first", "proj", "hidden", "inner", "layer", "low",
+    "gu", "back", "pre", "grads", "gm_grad", "s", "land", "swap", "res", "acc", "h", "xin", "cin",
+    "wgt", "wut", "wdt", "gt", "ut", "it", "jt", "stage", "load_sem", "in_send", "in_recv", "swap_recv",
+    "out_send", "out_recv", "store_sem", "w_sem", "x_sem", "c_sem", "h_sem", "y_sem", "t_sem",
+    "r_sem", "g_sem",
+)
+
+
+class Mlp:
+    def __init__(self, n, micros, rows, *refs):
+        for name, ref in zip(NAMES, refs):
+            setattr(self, name, ref)
+        self.micros, self.rows = micros, rows
+        self.chunks = rows // LINE_ROWS
+        self.hidden_units = self.w.shape[1] // 3
+        self.tiles = self.hidden_units // TILE
+        i = lax.axis_index("tensor")
+        half = n // 2
+        left = i < half
+        self.inward = jnp.where(left, i + 1, i - 1)
+        self.outward = jnp.where(left, i - 1, i + 1)
+        self.relay = (i > 0) & (i < n - 1)
+        self.mid = (i == half - 1) | (i == half)
+
+    def at(self, m, c):
+        start = pl.multiple_of((m * self.chunks + c) * LINE_ROWS, LINE_ROWS)
+        return pl.ds(start, LINE_ROWS)
+
+    def micro(self, m):
+        return pl.ds(pl.multiple_of(m * self.rows, self.rows), self.rows)
+
+    def move_in(self, m, c):
+        return pltpu.make_async_remote_copy(
+            src_ref=self.s.at[self.at(m, c)],
+            dst_ref=self.land.at[self.at(m, c)],
+            send_sem=self.in_send.at[m, c],
+            recv_sem=self.in_recv.at[m, c],
+            device_id={"tensor": self.inward},
+            device_id_type=MESH,
+        )
+
+    def move_swap(self, m, c):
+        return pltpu.make_async_remote_copy(
+            src_ref=self.s.at[self.at(m, c)],
+            dst_ref=self.swap.at[self.at(m, c)],
+            send_sem=self.in_send.at[m, c],
+            recv_sem=self.swap_recv.at[m, c],
+            device_id={"tensor": self.inward},
+            device_id_type=MESH,
+        )
+
+    def move_out(self, m, c):
+        return pltpu.make_async_remote_copy(
+            src_ref=self.res.at[self.at(m, c)],
+            dst_ref=self.res.at[self.at(m, c)],
+            send_sem=self.out_send.at[m, c],
+            recv_sem=self.out_recv.at[m, c],
+            device_id={"tensor": self.outward},
+            device_id_type=MESH,
+        )
+
+    def send_in(self, m, c):
+        @pl.when(self.mid)
+        def _():
+            self.move_swap(m, c).start()
+
+        @pl.when(~self.mid)
+        def _():
+            self.move_in(m, c).start()
+
+    def each_chunk(self, body):
+        def one(c, carry):
+            body(c)
+            return carry
+
+        lax.fori_loop(0, self.chunks, one, 0)
+
+    def launch(self, m):
+        @pl.when(~self.relay)
+        def _():
+            self.each_chunk(lambda c: self.send_in(m, c))
+
+    def settle(self, m):
+        def one(c):
+            self.move_in(m, c).wait_send()
+
+            @pl.when(self.relay)
+            def _():
+                self.move_out(m, c).wait_send()
+
+        self.each_chunk(one)
+
+    def begin(self):
+        load = pltpu.make_async_copy(self.part, self.s, self.load_sem)
+        load.start()
+        rest = self.micro(0)
+        done = pltpu.make_async_copy(self.first, self.res.at[rest], self.y_sem)
+        done.start()
+        self.load_x(0, self.x).start()
+        for copy in self.load_w(0, 0):
+            copy.start()
+        barrier = pltpu.get_barrier_semaphore()
+        pl.semaphore_signal(
+            barrier, inc=1, device_id={"tensor": self.inward}, device_id_type=MESH
+        )
+
+        @pl.when(self.relay)
+        def _():
+            pl.semaphore_signal(
+                barrier, inc=1, device_id={"tensor": self.outward}, device_id_type=MESH
+            )
+
+        pl.semaphore_wait(barrier, jnp.where(self.relay, 2, 1))
+        load.wait()
+        done.wait()
+        for m in range(1, self.micros):
+            self.launch(m)
+        self.gm_grad[...] = jnp.zeros_like(self.gm_grad)
+
+    def reduce(self, m, c):
+        @pl.when(self.relay)
+        def _():
+            self.move_in(m, c).wait_recv()
+            a = self.at(m, c)
+            self.s[a, :] = (self.s[a, :].astype(f32) + self.land[a, :].astype(f32)).astype(bf16)
+            self.send_in(m, c)
+
+    def store(self, m, c, to):
+        a = self.at(m, c)
+        return pltpu.make_async_copy(self.res.at[a], to.at[a], self.store_sem.at[m, c])
+
+    def spread(self, which, m, c):
+        a = self.at(m, c)
+
+        @pl.when(self.mid)
+        def _():
+            self.move_swap(m, c).wait_recv()
+            self.res[a, :] = (self.s[a, :].astype(f32) + self.swap[a, :].astype(f32)).astype(bf16)
+
+        @pl.when(~self.mid)
+        def _():
+            self.move_out(m, c).wait_recv()
+
+        @pl.when(self.relay)
+        def _():
+            self.move_out(m, c).start()
+
+        @pl.when(which == 0)
+        def _():
+            self.store(m, c, self.proj).start()
+
+        @pl.when(which == 2)
+        def _():
+            self.store(m, c, self.back).start()
+
+    def load_x(self, m, source):
+        return pltpu.make_async_copy(source.at[self.micro(m)], self.xin, self.x_sem)
+
+    def load_c(self, m):
+        return pltpu.make_async_copy(self.cot.at[self.micro(m)], self.cin, self.c_sem)
+
+    def store_h(self, m, to):
+        return pltpu.make_async_copy(self.h, to.at[self.micro(m)], self.h_sem)
+
+    def store_layer(self, m):
+        return pltpu.make_async_copy(self.xin, self.layer.at[self.micro(m)], self.y_sem)
+
+    def cols(self, t, which=0):
+        return pl.ds(pl.multiple_of(which * self.hidden_units + t * TILE, TILE), TILE)
+
+    def load_w(self, t, slot):
+        return [
+            pltpu.make_async_copy(
+                self.w.at[:, self.cols(t, which)], to.at[slot], self.w_sem.at[which, slot]
+            )
+            for which, to in enumerate((self.wgt, self.wut, self.wdt))
+        ]
+
+    def load_pre(self, m, t, slot):
+        return [
+            pltpu.make_async_copy(
+                self.pre.at[self.micro(m), self.cols(t, which)],
+                to.at[slot],
+                self.r_sem.at[which, slot],
+            )
+            for which, to in enumerate((self.gt, self.ut))
+        ]
+
+    def store_tile(self, which, source, to, m, at, slot):
+        return pltpu.make_async_copy(
+            source.at[slot], to.at[self.micro(m), at], self.t_sem.at[which, slot]
+        )
+
+    def store_pre(self, m, t, slot):
+        return (
+            self.store_tile(0, self.gt, self.pre, m, self.cols(t, 0), slot),
+            self.store_tile(1, self.ut, self.pre, m, self.cols(t, 1), slot),
+            self.store_tile(2, self.it, self.inner, m, self.cols(t), slot),
+        )
+
+    def store_low(self, m, t, slot):
+        return (
+            self.store_tile(2, self.it, self.gu, m, self.cols(t, 0), slot),
+            self.store_tile(3, self.jt, self.gu, m, self.cols(t, 1), slot),
+        )
+
+    def row_groups(self, body):
+        step = 16
+
+        def one(r, carry):
+            body(pl.ds(pl.multiple_of(r * step, step), step), r * step)
+            return carry
+
+        lax.fori_loop(0, self.rows // step, one, 0)
+
+    def forward_start(self, m):
+        @pl.when(m > 0)
+        def _():
+            self.each_chunk(lambda c: self.store(m, c, self.proj).wait())
+
+        self.load_x(m, self.x).wait()
+        base = m * self.rows
+        gain = self.ga[...]
+
+        def one(at, r):
+            total = self.res[pl.ds(pl.multiple_of(base + r, 16), 16), :].astype(f32)
+            inv = lax.rsqrt(jnp.mean(total * total, axis=1, keepdims=True) + norm_eps)
+            self.h[at, :] = (self.xin[at, :].astype(f32) + total * inv * gain).astype(bf16)
+
+        self.row_groups(one)
+        self.store_h(m, self.hidden).start()
+
+    def backward_start(self, m):
+        for copy in self.load_pre(m, 0, 0):
+            copy.start()
+        self.load_x(m, self.hidden).wait()
+        self.load_c(m).wait()
+        base = m * self.rows
+        gain = self.gm[...]
+
+        def one(at, r):
+            total = self.res[pl.ds(pl.multiple_of(base + r, 16), 16), :].astype(f32)
+            inv = lax.rsqrt(jnp.mean(total * total, axis=1, keepdims=True) + norm_eps)
+            unit = total * inv
+            c = self.cin[at, :].astype(f32)
+            self.xin[at, :] = (self.xin[at, :].astype(f32) + unit * gain).astype(bf16)
+            hit = c * unit
+            self.gm_grad[...] += hit[0:8, :] + hit[8:16, :]
+            dy = c * gain
+            inner = jnp.mean(hit * gain, axis=1, keepdims=True)
+            self.h[at, :] = (inv * (dy - unit * inner)).astype(bf16)
+
+        self.row_groups(one)
+        self.store_layer(m).start()
+        self.store_h(m, self.low).start()
+
+    def tile_weights(self, t, slot, last):
+        for copy in self.load_w(t, slot):
+            copy.wait()
+
+        @pl.when(jnp.logical_not(last))
+        def _():
+            for copy in self.load_w(lax.rem(t + 1, self.tiles), 1 - slot):
+                copy.start()
+
+    def add(self, t, at, value):
+        @pl.when(t == 0)
+        def _():
+            self.acc[:, at] = value
+
+        @pl.when(t > 0)
+        def _():
+            self.acc[:, at] += value
+
+    def forward_tile(self, m, t):
+        slot = lax.rem(t, 2)
+        self.tile_weights(t, slot, False)
+
+        @pl.when(t >= 2)
+        def _():
+            for copy in self.store_pre(m, t - 2, slot):
+                copy.wait()
+
+        gate = matmul(self.h[...], self.wgt[slot])
+        up = matmul(self.h[...], self.wut[slot])
+        self.gt[slot] = gate.astype(bf16)
+        self.ut[slot] = up.astype(bf16)
+        self.it[slot] = (gate * jax.nn.sigmoid(gate) * up).astype(bf16)
+        for copy in self.store_pre(m, t, slot):
+            copy.start()
+        wide = self.acc.shape[1]
+        step = math.gcd(wide, 512)
+        for k in range(0, wide, step):
+            self.add(t, slice(k, k + step), right_t(self.it[slot], self.wdt[slot, k : k + step, :]))
+
+        @pl.when(t == self.tiles - 1)
+        def _():
+            for back in range(min(2, self.tiles)):
+                at = self.tiles - 1 - back
+                for copy in self.store_pre(m, at, at % 2):
+                    copy.wait()
+            self.store_h(m, self.hidden).wait()
+            self.finish(m, m > 0)
+
+    def backward_tile(self, m, t, last):
+        slot = lax.rem(t, 2)
+        self.tile_weights(t, slot, last & (t == self.tiles - 1))
+        for copy in self.load_pre(m, t, slot):
+            copy.wait()
+
+        @pl.when(t < self.tiles - 1)
+        def _():
+            for copy in self.load_pre(m, t + 1, 1 - slot):
+                copy.start()
+
+        @pl.when(t >= 2)
+        def _():
+            for copy in self.store_low(m, t - 2, slot):
+                copy.wait()
+
+        grad = matmul(self.h[...], self.wdt[slot])
+        gate = self.gt[slot].astype(f32)
+        sig = jax.nn.sigmoid(gate)
+        act = grad * sig
+        self.jt[slot] = (act * gate).astype(bf16)
+        self.it[slot] = (
+            act * self.ut[slot].astype(f32) * (1.0 + gate * (1.0 - sig))
+        ).astype(bf16)
+        for copy in self.store_low(m, t, slot):
+            copy.start()
+        wide = self.acc.shape[1]
+        step = math.gcd(wide, 512)
+        for k in range(0, wide, step):
+            self.add(
+                t,
+                slice(k, k + step),
+                right_t(self.it[slot], self.wgt[slot, k : k + step, :])
+                + right_t(self.jt[slot], self.wut[slot, k : k + step, :]),
+            )
+
+        @pl.when(t == self.tiles - 1)
+        def _():
+            for back in range(min(2, self.tiles)):
+                at = self.tiles - 1 - back
+                for copy in self.store_low(m, at, at % 2):
+                    copy.wait()
+            self.store_h(m, self.low).wait()
+            self.store_layer(m).wait()
+            self.finish(m, True)
+
+    def load_bigs(self, source):
+        return (
+            pltpu.make_async_copy(source.at[self.micro(0)], self.xin, self.x_sem),
+            pltpu.make_async_copy(source.at[self.micro(1)], self.cin, self.c_sem),
+        )
+
+    def load_units(self, source, w, slot):
+        return [
+            pltpu.make_async_copy(
+                source.at[self.micro(m), self.cols(w)], to.at[slot], self.r_sem.at[m, slot]
+            )
+            for m, to in enumerate((self.gt, self.ut))
+        ]
+
+    def start_units(self, w, slot):
+        split = 2 * self.tiles
+
+        @pl.when(w < split)
+        def _():
+            for copy in self.load_units(self.gu, w, slot):
+                copy.start()
+
+        @pl.when((w >= split) & (w < 3 * self.tiles))
+        def _():
+            for copy in self.load_units(self.inner, w - split, slot):
+                copy.start()
+
+    def store_grads(self, w, slot):
+        return pltpu.make_async_copy(
+            self.stage.at[slot], self.grads.at[:, self.cols(w), :], self.g_sem.at[slot]
+        )
+
+    def grad_tile(self, w):
+        slot = lax.rem(w, 2)
+        split = 2 * self.tiles
+
+        @pl.when((w == 0) | (w == split))
+        def _():
+            for copy in self.load_bigs(self.hidden):
+                copy.wait()
+
+        for copy in self.load_units(self.gu, 0, slot):
+            copy.wait()
+        self.start_units(w + 1, 1 - slot)
+
+        @pl.when(w >= 2)
+        def _():
+            self.store_grads(w - 2, slot).wait()
+
+        value = left_t(self.gt[slot], self.xin[...]) + left_t(self.ut[slot], self.cin[...])
+        owners, _, wide = self.stage.shape[1:]
+        for owner in range(owners):
+            self.stage[slot, owner] = value[:, owner * wide : (owner + 1) * wide].astype(bf16)
+        self.store_grads(w, slot).start()
+
+        @pl.when(w == split - 1)
+        def _():
+            for copy in self.load_bigs(self.low):
+                copy.start()
+
+        @pl.when(w == 3 * self.tiles - 1)
+        def _():
+            self.store_grads(w - 1, 1 - slot).wait()
+            self.store_grads(w, slot).wait()
+
+    def finish(self, m, sent):
+        @pl.when(sent)
+        def _():
+            self.settle(m)
+
+        base = m * self.rows
+
+        def one(at, r):
+            self.s[pl.ds(pl.multiple_of(base + r, 16), 16), :] = self.acc[at, :].astype(bf16)
+
+        self.row_groups(one)
+        self.launch(m)
+
+    def job(self, index, step):
+        micros = self.micros
+        m = lax.rem(index, micros)
+        forward = index < micros
+        last = index == 2 * micros - 1
+
+        @pl.when(forward & (step == 0))
+        def _():
+            self.forward_start(m)
+
+        @pl.when(jnp.logical_not(forward) & (step == 0))
+        def _():
+            self.backward_start(m)
+
+        tiled = (step >= 1) & (step <= self.tiles)
+
+        @pl.when(forward & tiled)
+        def _():
+            self.forward_tile(m, step - 1)
+
+        @pl.when(jnp.logical_not(forward) & tiled)
+        def _():
+            self.backward_tile(m, step - 1, last)
+
+        done = step == self.tiles
+
+        @pl.when(done & (index < micros - 1))
+        def _():
+            self.load_x(index + 1, self.x).start()
+
+        @pl.when(done & (index >= micros - 1) & jnp.logical_not(last))
+        def _():
+            self.load_x(index + 1 - micros, self.hidden).start()
+            self.load_c(index + 1 - micros).start()
+
+        @pl.when(done & last)
+        def _():
+            for copy in self.load_bigs(self.hidden):
+                copy.start()
+            self.start_units(0, 0)
+
+    def run(self):
+        n, micros = self.chunks, self.micros
+        total = 3 * micros * n
+        self.begin()
+
+        def clock(k, carry):
+            @pl.when(k < total)
+            def _():
+                self.reduce(lax.rem(k // n, micros), lax.rem(k, n))
+
+            back = k - LAG
+
+            @pl.when((back >= n) & (back < total))
+            def _():
+                sum_index = back // n
+                self.spread(sum_index // micros, lax.rem(sum_index, micros), lax.rem(back, n))
+
+            turn = back - n
+
+            @pl.when((turn >= 0) & (turn < 2 * micros * n))
+            def _():
+                self.job(turn // n, lax.rem(turn, n))
+
+            turn = turn - 2 * micros * n + n - self.tiles - 1
+
+            @pl.when((turn >= 0) & (turn < 3 * self.tiles))
+            def _():
+                self.grad_tile(turn)
+
+            return carry
+
+        grads_at = 2 * micros * n + LAG + self.tiles + 1
+        lax.fori_loop(n, max(total + LAG, grads_at + 3 * self.tiles), clock, 0)
+        for m in range(micros):
+            self.settle(m)
+            self.each_chunk(lambda c: self.store(m, c, self.back).wait())
+
+
+def mlp_kernel(n, micros, rows, *refs):
+    Mlp(n, micros, rows, *refs).run()
+
+
+def feed_forward(part, x, cot, w, ga, gm, first, micros, owners):
+    assert micros == 2
+    both, width = x.shape
+    hidden = w.shape[1] // 3
+    rows = both // micros
+    chunks = rows // LINE_ROWS
+    dma = pltpu.SemaphoreType.DMA
+    hbm = pl.BlockSpec(memory_space=pl.ANY)
+    vmem = pl.BlockSpec(memory_space=pltpu.VMEM)
+    wide = jax.ShapeDtypeStruct((both, width), bf16)
+    unit = jax.ShapeDtypeStruct((both, hidden), bf16)
+    two = jax.ShapeDtypeStruct((both, 2 * hidden), bf16)
+    return pl.pallas_call(
+        functools.partial(mlp_kernel, lax.axis_size("tensor"), micros, rows),
+        in_specs=[hbm] * 4 + [vmem] * 2 + [hbm],
+        out_specs=[hbm] * 9 + [vmem],
+        out_shape=[wide, wide, unit, wide, wide, two, wide, two]
+        + [jax.ShapeDtypeStruct((owners, 3 * hidden, width // owners), bf16)]
+        + [jax.ShapeDtypeStruct((8, width), f32)],
+        scratch_shapes=[
+            pltpu.VMEM((both, width), bf16),
+            pltpu.VMEM((both, width), bf16),
+            pltpu.VMEM((both, width), bf16),
+            pltpu.VMEM((both, width), bf16),
+            pltpu.VMEM((rows, width), f32),
+            pltpu.VMEM((rows, width), bf16),
+            pltpu.VMEM((rows, width), bf16),
+            pltpu.VMEM((rows, width), bf16),
+            pltpu.VMEM((2, width, TILE), bf16),
+            pltpu.VMEM((2, width, TILE), bf16),
+            pltpu.VMEM((2, width, TILE), bf16),
+            pltpu.VMEM((2, rows, TILE), bf16),
+            pltpu.VMEM((2, rows, TILE), bf16),
+            pltpu.VMEM((2, rows, TILE), bf16),
+            pltpu.VMEM((2, rows, TILE), bf16),
+            pltpu.VMEM((2, owners, TILE, width // owners), bf16),
+            dma(()),
+            dma((micros, chunks)),
+            dma((micros, chunks)),
+            dma((micros, chunks)),
+            dma((micros, chunks)),
+            dma((micros, chunks)),
+            dma((micros, chunks)),
+            dma((3, 2)),
+            dma(()),
+            dma(()),
+            dma(()),
+            dma(()),
+            dma((4, 2)),
+            dma((2, 2)),
+            dma((2,)),
+        ],
+        compiler_params=pltpu.CompilerParams(
+            collective_id=1, has_side_effects=True, vmem_limit_bytes=60 << 20
+        ),
+        cost_estimate=cost(both // 4),
+        name="feed_forward",
+    )(part, x, cot, w, ga, gm, first)
 
 
 def attn_scores(meta, i, trunk_rows, q, kt, kp, ko):
@@ -301,6 +951,7 @@
             jax.ShapeDtypeStruct((rows, width), f32),
         ],
         compiler_params=pltpu.CompilerParams(vmem_limit_bytes=32 << 20),
+        cost_estimate=cost(12),
         name="attend_forward",
     )(meta, q, *kv)
 
@@ -337,6 +988,7 @@
             jax.ShapeDtypeStruct((branch_rows, width), bf16),
         ],
         compiler_params=pltpu.CompilerParams(vmem_limit_bytes=40 << 20),
+        cost_estimate=cost(22),
         name="attend_backward",
     )(meta, q, do, lse, *kv)
 
@@ -346,13 +998,13 @@
     return [(i, i // half * half + (i % half + k) % half) for i in range(n)]
 
 
-def fetch_sources(block):
+def fetch_sources(block, hold):
     n = lax.axis_size("seq")
     half = n // 2
     place = lax.axis_index("seq")
     spot = lax.rem(place, half)
     got = lax.ppermute(block, "seq", [(i, i + half) for i in range(half)])
-    mine = jnp.where(place < half, block, got)
+    mine = jnp.where(place < half, block, got if hold is None else after(got, hold))
     parts = [mine] + [lax.ppermute(mine, "seq", group_perm(n, k)) for k in range(1, half)]
     out = []
     for source in range(half):
@@ -363,11 +1015,10 @@
     return jnp.concatenate(out, axis=0)
 
 
-def return_to_sources(grads):
+def sum_over_group(grads):
     n = lax.axis_size("seq")
     half = n // 2
-    place = lax.axis_index("seq")
-    spot = lax.rem(place, half)
+    spot = lax.rem(lax.axis_index("seq"), half)
     rows = grads.shape[0] // half
     pieces = [grads[s * rows : (s + 1) * rows] for s in range(half)]
 
@@ -381,34 +1032,25 @@
     for k in range(1, half):
         sent = piece(lax.rem(spot + k, half))
         total += lax.ppermute(sent, "seq", group_perm(n, k)).astype(f32)
-    got = lax.ppermute(total.astype(bf16), "seq", [(i + half, i) for i in range(half)])
-    return jnp.where(place < half, total + got.astype(f32), 0.0)
+    return total.astype(bf16)
+
+
+def return_to_sources(total):
+    n = lax.axis_size("seq")
+    half = n // 2
+    got = lax.ppermute(total, "seq", [(i + half, i) for i in range(half)])
+    both = total.astype(f32) + got.astype(f32)
+    return jnp.where(lax.axis_index("seq") < half, both, 0.0)
 
 
 def gather_rows(item):
     return lax.all_gather(item, ("dp", "seq"), axis=0, tiled=True)
-
-
-def gather_cols(item):
-    return lax.all_gather(item, ("dp", "seq"), axis=1, tiled=True)
 
 
 def scatter_rows(item):
     return lax.psum_scatter(
         item.astype(bf16), ("dp", "seq"), scatter_dimension=0, tiled=True
     ).astype(f32)
-
-
-def scatter_cols(item):
-    return lax.psum_scatter(
-        item.astype(bf16), ("dp", "seq"), scatter_dimension=1, tiled=True
-    ).astype(f32)
-
-
-def all_reduce(parts):
-    total = line_sum(jnp.concatenate([p.astype(bf16) for p in parts], axis=0)).astype(f32)
-    rows = parts[0].shape[0]
-    return [total[m * rows : (m + 1) * rows] for m in range(len(parts))]
 
 
 def block_meta(parents, lengths, rows, n_blocks):
@@ -445,156 +1087,167 @@
     branches = (parent_of.shape[2] - 1) // 3
     trunk_rows = (n_blocks - 3 * branches) * BLOCK
 
-    wq = gather_rows(w_query)
-    wk = gather_rows(w_key)
-    wv = gather_rows(w_value)
-    q_gain = gather_cols(query_gain).reshape(-1).astype(f32)
-    k_gain = gather_cols(key_gain).reshape(-1).astype(f32)
-    wo = gather_cols(w_out)
-    a_gain = gather_rows(attn_gain).astype(f32)
-    m_gain = gather_rows(mlp_gain).astype(f32)
-    wg = gather_rows(w_gate)
-    wu = gather_rows(w_up)
-    wd = gather_cols(w_down)
-
-    saved = []
+    cols = w_query.shape[1]
+    owners = lax.axis_size("dp") * lax.axis_size("seq")
+    w_attn = gather_rows(jnp.concatenate([w_query, w_key, w_value, w_out.T], axis=1))
+    gains = [query_gain.reshape(-1), key_gain.reshape(-1), attn_gain, mlp_gain]
+    gains = lax.all_gather(jnp.concatenate(gains), ("dp", "seq"), axis=0, tiled=False)
+    own = query_gain.size
+
+    def head_gain(block):
+        block = block.reshape(owners, heads, HD // owners)
+        return jnp.swapaxes(block, 0, 1).reshape(-1).astype(f32)
+
+    q_gain = head_gain(gains[:, :own])
+    k_gain = head_gain(gains[:, own : 2 * own])
+    a_gain = gains[:, 2 * own : 2 * own + attn_gain.size].reshape(-1).astype(f32)
+    m_gain = gains[:, 2 * own + attn_gain.size :].reshape(-1).astype(f32)
+    wq, wk, wv = (w_attn[:, k * cols : (k + 1) * cols] for k in range(3))
+    wo_t = w_attn[:, 3 * cols :]
+
+    def part_of(array, m):
+        return array[m * rows : (m + 1) * rows]
+
+    x = tokens.reshape(micros * rows, width)
+    cot = cotangent.reshape(micros * rows, width)
+    q_raw, k_raw, v_raw = matmul(x, wq), matmul(x, wk), matmul(x, wv)
+    q_sq, k_sq = small_sum(
+        jnp.stack([jnp.sum(q_raw * q_raw, axis=1), jnp.sum(k_raw * k_raw, axis=1)]), 2
+    )
+    q_inv = lax.rsqrt(q_sq / full_width + norm_eps)[:, None]
+    k_inv = lax.rsqrt(k_sq / full_width + norm_eps)[:, None]
+    q_unit, k_unit = q_raw * q_inv, k_raw * k_inv
+    q_low = (q_unit * q_gain).astype(bf16)
+    k_low = (k_unit * k_gain).astype(bf16)
+    v_low = v_raw.astype(bf16)
+
+    kvs, metas, attn_lows, lses, parts, first = [], [], [], [], [], None
     for m in range(micros):
-        x = tokens[m, 0]
-        q_raw, k_raw, v_raw = matmul(x, wq), matmul(x, wk), matmul(x, wv)
-        q_sq, k_sq = lax.psum(
-            (jnp.sum(q_raw * q_raw, axis=1), jnp.sum(k_raw * k_raw, axis=1)), "tensor"
-        )
-        q_inv = lax.rsqrt(q_sq / full_width + norm_eps)[:, None]
-        k_inv = lax.rsqrt(k_sq / full_width + norm_eps)[:, None]
-        q_unit, k_unit = q_raw * q_inv, k_raw * k_inv
-        q_low = (q_unit * q_gain).astype(bf16)
-        k_low = (k_unit * k_gain).astype(bf16)
-        v_low = v_raw.astype(bf16)
-        sources = fetch_sources(jnp.concatenate([k_low, v_low], axis=1))
-        cols = k_low.shape[1]
-        kv = (
-            sources[:trunk_rows, :cols],
-            sources[:trunk_rows, cols:],
-            sources[trunk_rows:, :cols],
-            sources[trunk_rows:, cols:],
-            k_low,
-            v_low,
-        )
-        meta = block_meta(parent_of[m, 0], seg_length[m, 0], rows, n_blocks)
-        attn_low, lse = attend_forward(meta, q_low, kv)
-        saved.append(
-            dict(x=x, q_inv=q_inv, k_inv=k_inv, q_unit=q_unit, k_unit=k_unit, q_low=q_low,
-                 kv=kv, meta=meta, attn_low=attn_low, lse=lse)
-        )
-
-    outs = []
-    projs = all_reduce([matmul(s["attn_low"], wo) for s in saved])
+        k_own, v_own = part_of(k_low, m), part_of(v_low, m)
+        sources = fetch_sources(jnp.concatenate([k_own, v_own], axis=1), first)
+        kvs.append(
+            (
+                sources[:trunk_rows, :cols],
+                sources[:trunk_rows, cols:],
+                sources[trunk_rows:, :cols],
+                sources[trunk_rows:, cols:],
+                k_own,
+                v_own,
+            )
+        )
+        metas.append(block_meta(parent_of[m, 0], seg_length[m, 0], rows, n_blocks))
+        attn_low, lse = attend_forward(metas[m], part_of(q_low, m), kvs[m])
+        attn_lows.append(attn_low)
+        lses.append(lse)
+        parts.append(right_t(attn_low, wo_t).astype(bf16))
+        if m == 0:
+            first = line_sum(parts[0], 0)
+            w_own = jnp.concatenate([w_gate, w_up, w_down.T], axis=1)
+            w_mlp = gather_rows(after(w_own, sources))
+    proj, _, _, layer_out, _, _, back, _, mlp_grads, gm_grad = feed_forward(
+        jnp.concatenate(parts, axis=0), x, cot, w_mlp, a_gain[None], m_gain[None], first,
+        micros, owners,
+    )
+    units = w_gate.shape[1]
+    ga_grad = 0.0
+    proj_lows, dqs, owns, sums = [], [], [], []
     for m in range(micros):
-        s = saved[m]
-        attn_proj = projs[m]
+        attn_proj = (first if m == 0 else part_of(proj, m)).astype(f32)
         attn_inv = lax.rsqrt(jnp.mean(attn_proj * attn_proj, axis=1, keepdims=True) + norm_eps)
         attn_unit = attn_proj * attn_inv
-        hidden = s["x"].astype(f32) + attn_unit * a_gain
-        hidden_low = hidden.astype(bf16)
-        gate_pre = matmul(hidden_low, wg)
-        up_pre = matmul(hidden_low, wu)
-        sig = jax.nn.sigmoid(gate_pre)
-        inner_low = (gate_pre * sig * up_pre).astype(bf16)
-        s.update(attn_unit=attn_unit, attn_inv=attn_inv, hidden=hidden, hidden_low=hidden_low,
-                 gate_pre=gate_pre.astype(bf16), up_pre=up_pre.astype(bf16), inner_low=inner_low)
-
-    gm_grad = 0.0
-    projs = all_reduce([matmul(s["inner_low"], wd) for s in saved])
-    for m in range(micros):
-        s = saved[m]
-        mlp_proj = projs[m]
-        mlp_inv = lax.rsqrt(jnp.mean(mlp_proj * mlp_proj, axis=1, keepdims=True) + norm_eps)
-        mlp_unit = mlp_proj * mlp_inv
-        outs.append((s["hidden"] + mlp_unit * m_gain).astype(bf16))
-        c = cotangent[m, 0].astype(f32)
-        gm_grad += jnp.sum(c * mlp_unit, axis=0)
-        unit_grad = c * m_gain
-        mlp_low = (
-            mlp_inv * (unit_grad - mlp_unit * jnp.mean(unit_grad * mlp_unit, axis=1, keepdims=True))
-        ).astype(bf16)
-        inner_grad = right_t(mlp_low, wd)
-        gate_pre, up_pre = s["gate_pre"].astype(f32), s["up_pre"].astype(f32)
-        sig = jax.nn.sigmoid(gate_pre)
-        gate_low = (inner_grad * up_pre * sig * (1.0 + gate_pre * (1.0 - sig))).astype(bf16)
-        up_low = (inner_grad * gate_pre * sig).astype(bf16)
-        s.update(c=c, mlp_low=mlp_low, gate_low=gate_low, up_low=up_low)
-
-    def both(name):
-        return jnp.concatenate([s[name] for s in saved], axis=0)
-
-    g_down = scatter_cols(left_t(both("inner_low"), both("mlp_low")))
-    hidden_low = both("hidden_low")
-    g_gate = scatter_rows(left_t(hidden_low, both("gate_low")))
-    g_up = scatter_rows(left_t(hidden_low, both("up_low")))
-
-    ga_grad = 0.0
-    backs = all_reduce([right_t(s["gate_low"], wg) + right_t(s["up_low"], wu) for s in saved])
-    for m in range(micros):
-        s = saved[m]
-        hidden_grad = s["c"] + backs[m]
-        ga_grad += jnp.sum(hidden_grad * s["attn_unit"], axis=0)
+        hidden_grad = part_of(cot, m).astype(f32) + part_of(back, m).astype(f32)
+        ga_grad += jnp.sum(hidden_grad * attn_unit, axis=0)
         unit_grad = hidden_grad * a_gain
         proj_low = (
-            s["attn_inv"]
-            * (unit_grad
-               - s["attn_unit"] * jnp.mean(unit_grad * s["attn_unit"], axis=1, keepdims=True))
+            attn_inv
+            * (unit_grad - attn_unit * jnp.mean(unit_grad * attn_unit, axis=1, keepdims=True))
         ).astype(bf16)
-        attn_grad = right_t(proj_low, wo).astype(bf16)
+        attn_grad = matmul(proj_low, wo_t).astype(bf16)
+        if m > 0:
+            attn_grad = after(attn_grad, sums[-1])
         dq, dko, dvo, dkt, dvt, dkb, dvb = attend_backward(
-            s["meta"], s["q_low"], attn_grad, s["lse"], s["kv"]
-        )
-        returned = return_to_sources(
-            jnp.concatenate(
-                [jnp.concatenate([dkt, dvt], axis=1), jnp.concatenate([dkb, dvb], axis=1)], axis=0
+            metas[m], part_of(q_low, m), attn_grad, lses[m], kvs[m]
+        )
+        sums.append(
+            sum_over_group(
+                jnp.concatenate(
+                    [jnp.concatenate([dkt, dvt], axis=1), jnp.concatenate([dkb, dvb], axis=1)],
+                    axis=0,
+                )
             )
         )
-        cols = dko.shape[1]
-        dk = dko + returned[:, :cols]
-        dv = dvo + returned[:, cols:]
-        s.update(hidden_grad=hidden_grad, proj_low=proj_low, dq=dq, dk=dk, dv=dv)
-
-    qg_grad = kg_grad = 0.0
-    backs = []
+        proj_lows.append(proj_low)
+        dqs.append(dq)
+        owns.append((dko, dvo))
+
+    qkv_lows, lasts = [], []
+    qg_grad = kg_grad = g_qkv = 0.0
     for m in range(micros):
-        s = saved[m]
-        q_unit, k_unit = s["q_unit"], s["k_unit"]
-        qg_grad += jnp.sum(s["dq"] * q_unit, axis=0)
-        kg_grad += jnp.sum(s["dk"] * k_unit, axis=0)
-        q_scaled, k_scaled = s["dq"] * q_gain, s["dk"] * k_gain
-        q_inner, k_inner = lax.psum(
-            (jnp.sum(q_scaled * q_unit, axis=1), jnp.sum(k_scaled * k_unit, axis=1)), "tensor"
-        )
-        qr_low = (s["q_inv"] * (q_scaled - q_unit * (q_inner / full_width)[:, None])).astype(bf16)
-        kr_low = (s["k_inv"] * (k_scaled - k_unit * (k_inner / full_width)[:, None])).astype(bf16)
-        vr_low = s["dv"].astype(bf16)
-        backs.append(right_t(qr_low, wq) + right_t(kr_low, wk) + right_t(vr_low, wv))
-        s.update(qr_low=qr_low, kr_low=kr_low, vr_low=vr_low)
-
-    grads = [s["hidden_grad"] + back for s, back in zip(saved, all_reduce(backs))]
-    x = both("x")
-    g_out = scatter_cols(left_t(both("attn_low"), both("proj_low")))
-    g_query = scatter_rows(left_t(x, both("qr_low")))
-    g_key = scatter_rows(left_t(x, both("kr_low")))
-    g_value = scatter_rows(left_t(x, both("vr_low")))
+        got = return_to_sources(sums[m])
+        if m > 0:
+            got = after(got, lasts[-1])
+        else:
+            got = after(got, dqs[-1])
+            mlp_grads = after(mlp_grads.reshape(-1, mlp_grads.shape[2]), got)
+            mlp_grads = scatter_rows(mlp_grads)
+        dq, dk, dv = dqs[m], owns[m][0] + got[:, :cols], owns[m][1] + got[:, cols:]
+        q_u, k_u = part_of(q_unit, m), part_of(k_unit, m)
+        qg_grad += jnp.sum(dq * q_u, axis=0)
+        kg_grad += jnp.sum(dk * k_u, axis=0)
+        q_scaled, k_scaled = dq * q_gain, dk * k_gain
+        q_inner, k_inner = small_sum(
+            jnp.stack([jnp.sum(q_scaled * q_u, axis=1), jnp.sum(k_scaled * k_u, axis=1)]), 4
+        )
+        q_inner, k_inner = q_inner[:, None] / full_width, k_inner[:, None] / full_width
+        qr_low = (part_of(q_inv, m) * (q_scaled - q_u * q_inner)).astype(bf16)
+        kr_low = (part_of(k_inv, m) * (k_scaled - k_u * k_inner)).astype(bf16)
+        qkv_lows.append(jnp.concatenate([qr_low, kr_low, dv.astype(bf16)], axis=1))
+        part = right_t(qkv_lows[m], w_attn[:, : 3 * cols]).astype(bf16)
+        g_qkv += left_t(part_of(x, m), qkv_lows[m])
+        if m > 0:
+            g_qkv = g_qkv.astype(bf16)
+            part = after(part, g_qkv)
+        lasts.append(line_sum(part, 3))
+    g_qkv = scatter_rows(g_qkv)
+    last = jnp.concatenate(lasts, axis=0)
+
+    def head_grad(value):
+        return jnp.swapaxes(value.reshape(heads, owners, HD // owners), 0, 1).reshape(owners, -1)
+
+    gain_grads = jnp.concatenate(
+        [
+            head_grad(qg_grad),
+            head_grad(kg_grad),
+            ga_grad.reshape(owners, -1),
+            jnp.sum(gm_grad, axis=0).reshape(owners, -1),
+        ],
+        axis=1,
+    )
+    count = gain_grads.shape[1]
+    lines = -(-count // 128)
+    gain_grads = jnp.pad(gain_grads, ((0, 0), (0, lines * 128 - count)))
+    gain_grads = gain_grads.reshape(owners, lines, 128)
+    gain_grads = jnp.pad(gain_grads, ((0, 0), (0, width // owners - lines), (0, 0)))
+    proj_low = after(jnp.concatenate(proj_lows, axis=0), lasts[0])
+    g_out = left_t(proj_low, jnp.concatenate(attn_lows, axis=0))
+    g_out = jnp.concatenate([g_out, gain_grads.reshape(width, 128)], axis=1).astype(bf16)
+    g_out = scatter_rows(after(g_out, mlp_grads))
+    gain_grads = g_out[:lines, cols:].reshape(-1)
+    input_grad = cot.astype(f32) + back.astype(f32) + last.astype(f32)
     return (
-        jnp.stack(outs)[:, None],
-        jnp.stack(grads)[:, None],
-        g_query,
-        g_key,
-        g_value,
-        g_out,
-        g_gate,
-        g_up,
-        g_down,
-        scatter_cols(qg_grad.reshape(heads, HD)),
-        scatter_cols(kg_grad.reshape(heads, HD)),
-        scatter_rows(ga_grad),
-        scatter_rows(gm_grad),
+        layer_out.reshape(tokens.shape),
+        input_grad.reshape(tokens.shape),
+        g_qkv[:, :cols],
+        g_qkv[:, cols : 2 * cols],
+        g_qkv[:, 2 * cols :],
+        g_out[:, :cols].T,
+        mlp_grads[:units].T,
+        mlp_grads[units : 2 * units].T,
+        mlp_grads[2 * units :],
+        gain_grads[:own].reshape(query_gain.shape),
+        gain_grads[own : 2 * own].reshape(key_gain.shape),
+        gain_grads[2 * own : 2 * own + attn_gain.size],
+        gain_grads[2 * own + attn_gain.size : count],
     )
 
 

time: 1550 us -> 1170 us (0.75)
  matrix products: 273 us -> 89.2 us
  blocking collectives: 139 us -> 10.5 us
  waiting for transfers between devices: 182 us -> 90.9 us
  other arithmetic: 197 us -> 113 us
  Pallas kernels: 680 us -> 746 us
  local copies, waits for them, and re-layouts: 44.3 us -> 78.2 us
    pallas_call x0 -> x13, Pallas kernels: none -> 425 us  [the longest x1 404 us: feed_forward(): pl.pallas_call(functools.partial(mlp_kernel, lax.axis_size('tensor'), mic...]
    pallas_call x4 -> x3, Pallas kernels: 611 us -> 252 us  [line_sum(): pl.pallas_call(functools.partial(line_kernel, n, chunks), in_specs=[pl.Bl...]
    all_gather x4 -> x1, blocking collectives: 90.5 us -> 10.5 us  [per_device(): lax.all_gather(jnp.concatenate(gains), ('dp', 'seq'), axis=0, tiled=False)]
    dot_general x14 -> x4, matrix products: 100 us -> 27 us  [right_t(): lax.dot_general(left, right, (((1,), (1,)), ((), ())), preferred_element_...]
    dot_general x14 -> x5, matrix products: 95.7 us -> 34.4 us  [matmul(): return jnp.dot(left, right, preferred_element_type=f32)]
    convert_element_type x25 -> x8, other arithmetic: 86.4 us -> 26.6 us  [the longest x2 8.47 us: sum_over_group(): return total.astype(bf16)]
    ppermute x4, waiting for transfers between devices: 59.2 us -> 7.07 us  [the longest x2 7.06 us: return_to_sources(): got = lax.ppermute(total, 'seq', [(i + half, i) for i in range(half)])]
    reduce_scatter x5 -> x3, waiting for transfers between devices: 51.5 us -> 0.01 us  [scatter_rows(): lax.psum_scatter(item.astype(bf16), ('dp', 'seq'), scatter_dimension=0, t...]
  transfers between devices with their start and end apart: 24 -> 13, of which waited for: 6 -> 4; matrix products, arithmetic and copies ran while one was open for 21% -> 13% of each run, Pallas kernels for 23% -> 27%
where the time goes in v2:
time: 1170 us; the launch traced here: 1160 us
  Pallas kernels  746 us (64%)
  other arithmetic  113 us (10%)
  waiting for transfers between devices  90.9 us (8%)
  matrix products  89.2 us (8%)
  local copies, waits for them, and re-layouts  78.2 us (7%)
  between operations  15.7 us (1%)
  starting transfers between devices  14.2 us (1%)
    pallas_call x1, Pallas kernels, feed_forward(): pl.pallas_call(functools.partial(mlp_kernel, lax.axis_size('tensor'), mic...  404 us
    pallas_call x3, Pallas kernels, line_sum(): pl.pallas_call(functools.partial(line_kernel, n, chunks), in_specs=[pl.Bl...  252 us
    unnamed x244, local copies, waits for them, and re-layouts  55.2 us
    all_gather x2, waiting for transfers between devices, gather_rows(): return lax.all_gather(item, ('dp', 'seq'), axis=0, tiled=True)  51.5 us
    pallas_call x2, Pallas kernels, attend_backward(): pl.pallas_call(functools.partial(attn_bwd_kernel, trunk_rows, n_q), grid_...  44.1 us
    dot_general x5, matrix products, matmul(): return jnp.dot(left, right, preferred_element_type=f32)  34.4 us
    ppermute x2, waiting for transfers between devices, fetch_sources(): got = lax.ppermute(block, 'seq', [(i, i + half) for i in range(half)])  32.2 us
    dot_general x3, matrix products, left_t(): lax.dot_general(left, right, (((0,), (0,)), ((), ())), preferred_element_...  27.7 us
  transfers between devices with their start and end apart: 13, of which 4 were waited for; matrix products, arithmetic and copies ran while one was open for 13% of the time, Pallas kernels for 27%

profile of v2, /device:TPU:0, one launch (start us, length us, event | category | flops | bytes accessed | tf_op | source)
XLA Modules:
  0.0 1157.8 jit_solution(7595877946762368744)
XLA Ops:
  12.9 10.5 all-gather.1
  24.3 47.1 %all-gather.5.cloned.1.call-done = bf16[2048,2048]{0,1:T(8,128)(2,1)} async-done(((bf16[256,2048]{0,1:T(8,128)(2,1)}), bf16[2048,2048]{0,1:T(8,128)(2,1)}) %all-gather.5.cloned.1.call-update) | async-done | bytes 8388624 | tf_op jit(solution)/shard_map/all_gather | solution.py:1047
  71.4 8.5 multiply_reduce_fusion.1
  79.9 8.5 multiply_reduce_fusion
  89.1 7.2 small_sum.3
  100.0 3.5 copy.166
  103.6 5.1 multiply_convert_fusion
  108.8 7.5 fusion.36
  117.9 3.8 collective-permute-start
  121.7 32.2 %collective-permute-done = bf16[768,1024]{1,0:T(8,128)(2,1)} collective-permute-done((bf16[768,1024]{1,0:T(8,128)(2,1)}, bf16[768,1024]{1,0:T(8,128)(2,1)}, u32[]{:S(2)}, u32[]{:S(2)}) %collective-permute-start) | collective-permute-done | bytes 1572896 | tf_op jit(solution)/shard_map/ppermute | solution.py:1006
  157.9 3.1 pad_maximum_fusion.2.refs_0_
  169.8 7.1 collective-permute-start.2
  179.3 12.4 %attend_forward.2 = (bf16[768,512]{1,0:T(8,128)(2,1)S(1)}, f32[768,512]{1,0:T(8,128)S(1)}) custom-call(s32[3,5]{1,0:T(4,128)S(1)} %stack.41.meta, bf16[768,512]{1,0:T(8,128)(2,1)S(1)} %get-tuple-element.185.q, bf16[768,512]{1,0:T(8,128)(2,1)S(1)} %get-tuple-element.180.kt, bf16[768,512]{1,0:T(8,128)(2,1)S(1)} %get-tuple-element.179.vt, ...), custom_call_target="tpu_custom_call" | custom-call | flops 13200000000 | tf_op jit(solution)/shard_map/attend_forward/pallas_call | solution.py:941
  193.0 5.3 convolution_convert_fusion.1.part
  198.3 85.0 %line_sum.3.refs_1_.refs_6_ = bf16[768,2048]{1,0:T(8,128)(2,1)S(1)} custom-call(bf16[768,2048]{1,0:T(8,128)(2,1)} %convolution_convert_fusion.1.part), custom_call_target="tpu_custom_call" | custom-call | flops 93499998208 | tf_op jit(solution)/shard_map/line_sum/pallas_call | solution.py:206
  284.9 3.3 broadcast_select_fusion.4
  297.3 12.4 %attend_forward.3 = (bf16[768,512]{1,0:T(8,128)(2,1)S(1)}, f32[768,512]{1,0:T(8,128)S(1)}) custom-call(s32[3,5]{1,0:T(4,128)S(1)} %stack.45.meta, bf16[768,512]{1,0:T(8,128)(2,1)S(1)} %copy-done.33, bf16[768,512]{1,0:T(8,128)(2,1)S(1)} %get-tuple-element.176.kt, bf16[768,512]{1,0:T(8,128)(2,1)S(1)} %get-tuple-element.175.vt, ...), custom_call_target="tpu_custom_call" | custom-call | flops 13200000000 | tf_op jit(solution)/shard_map/attend_forward/pallas_call | solution.py:941
  311.8 3.5 convolution_convert_fusion
  315.4 3.8 pad_maximum_fusion.refs_0_
  319.2 4.4 all-gather.7.cloned.1.call-done.refs_3_
  323.6 404.3 %feed_forward.1 = (bf16[1536,2048]{1,0:T(8,128)(2,1)}, bf16[1536,2048]{1,0:T(8,128)(2,1)}, bf16[1536,2048]{1,0:T(8,128)(2,1)}, bf16[1536,2048]{1,0:T(8,128)(2,1)...) custom-call(bf16[1536,2048]{1,0:T(8,128)(2,1)} %pad_maximum_fusion.r, ...), custom_call_target="tpu_custom_call" | custom-call | flops 422400000000 | tf_op jit(solution)/shard_map/feed_forward/pallas_call | solution.py:804
  730.8 10.3 fusion.11
  741.7 5.7 fusion.10
  747.5 4.6 convolution_convert_fusion.5.do
  752.2 22.0 %attend_backward.2 = (f32[768,512]{1,0:T(8,128)S(1)}, f32[768,512]{1,0:T(8,128)S(1)}, f32[768,512]{1,0:T(8,128)S(1)}, bf16[768,512]{1,0:T(8,128)(2,1)S(1)}, bf16...) custom-call(s32[3,5]{1,0:T(4,128)S(1)} %stack.41.meta, ...), custom_call_target="tpu_custom_call" | custom-call | flops 24199999488 | tf_op jit(solution)/shard_map/attend_backward/pallas_call | solution.py:967
  777.2 5.4 convolution_convert_fusion.4.refs_0_
  782.6 3.6 add_convert_fusion.2.refs_1_
  794.4 22.0 %attend_backward.3 = (f32[768,512]{1,0:T(8,128)S(1)}, f32[768,512]{1,0:T(8,128)S(1)}, f32[768,512]{1,0:T(8,128)S(1)}, bf16[768,512]{1,0:T(8,128)(2,1)S(1)}, bf16...) custom-call(s32[3,5]{1,0:T(4,128)S(1)} %stack.45.meta, ...), custom_call_target="tpu_custom_call" | custom-call | flops 24199999488 | tf_op jit(solution)/shard_map/attend_backward/pallas_call | solution.py:967
  818.2 7.1 collective-permute-done.5
  825.3 4.2 add_select_fusion.1.refs_0_
  840.7 4.9 add_convert_fusion.1
  846.9 6.9 small_sum.4
  857.7 4.3 multiply_convert_fusion.4
  862.0 9.7 fusion.25.part
  871.7 84.7 %line_sum.4.refs_1_ = bf16[768,2048]{1,0:T(8,128)(2,1)S(1)} custom-call(bf16[768,2048]{1,0:T(8,128)(2,1)} %fusion.25.part), custom_call_target="tpu_custom_call" | custom-call | flops 93499998208 | tf_op jit(solution)/shard_map/line_sum/pallas_call | solution.py:206
  956.4 8.0 fusion.32
  964.5 4.2 add_select_fusion.refs_0_
  973.3 6.8 small_sum.5
  982.7 3.4 multiply_convert_fusion.2
  987.2 11.1 fusion.6.refs_1_
  1000.3 5.6 pad_maximum_fusion.1.refs_0_
  1007.7 8.6 convolution_convert_fusion.2
  1016.6 8.5 fusion.28.refs_0_
  1028.3 5.0 convert_element_type.254.refs_1_
  1033.3 82.6 %line_sum.5 = bf16[768,2048]{1,0:T(8,128)(2,1)S(1)} custom-call(bf16[768,2048]{1,0:T(8,128)(2,1)} %after.14.part), custom_call_target="tpu_custom_call" | custom-call | flops 93499998208 | tf_op jit(solution)/shard_map/line_sum/pallas_call | solution.py:206
  1116.0 11.8 %convert_add_fusion = f32[1536,2048]{1,0:T(8,128)} fusion(bf16[1536,2048]{1,0:T(8,128)(2,1)} %get-tuple-element.39, bf16[768,2048]{1,0:T(8,128)(2,1)S(1)} %line_sum.5, bf16[768,2048]{1,0:T(8,128)(2,1)S(1)} %copy-done.4, bf16[2,1,768,2048]{3,2,1,0:T(8,128)(2,1)S(1)} %bitcast.122), kind=kLoop, calls=%fused_computation | loop fusion | flops 25165824 | bytes 31457280 | tf_op jit(solution)/shard_map/add | solution.py:1236
  1130.1 3.8 slice_bitcast_fusion
  1144.2 6.6 copy.209
  (384 shorter events, 102.3 us)
Async XLA Ops:
  7.2 64.1 %all-gather.5.cloned.1.call-start = ((), (), s32[]{:S(2)}) async-start(), calls=%async_computation.3 | async-start | bytes 9437184 | tf_op jit(solution)/shard_map/all_gather | solution.py:1047
  12.6 311.0 %all-gather.7.cloned.1.call-start = ((), (), s32[]{:S(2)}) async-start(), calls=%async_computation.4 | async-start | bytes 28311552 | tf_op jit(solution)/shard_map/all_gather | solution.py:1047
  24.1 79.5 %copy-start.84 = (f32[512]{0:T(512)}, f32[512]{0:T(512)S(1)}, u32[]{:S(2)}) copy-start(f32[512]{0:T(512)S(1)} %reshape.390) | copy-start | bytes 6148
  24.3 79.3 %copy-start.87 = (f32[512]{0:T(512)}, f32[512]{0:T(512)S(1)}, u32[]{:S(2)}) copy-start(f32[512]{0:T(512)S(1)} %reshape.389) | copy-start | bytes 6148
  108.8 60.8 %copy-start.7 = (bf16[768,512]{1,0:T(8,128)(2,1)}, bf16[768,512]{1,0:T(8,128)(2,1)S(1)}, u32[]{:S(2)}) copy-start(bf16[768,512]{1,0:T(8,128)(2,1)S(1)} %get-tuple-element.182.ko) | copy-start | bytes 2359300
  108.8 70.5 %copy-start.13 = (bf16[768,512]{1,0:T(8,128)(2,1)}, bf16[768,512]{1,0:T(8,128)(2,1)S(1)}, u32[]{:S(2)}) copy-start(bf16[768,512]{1,0:T(8,128)(2,1)S(1)} %get-tuple-element.181.ko) | copy-start | bytes 2359300
  116.4 53.2 %copy-start.10 = (bf16[768,512]{1,0:T(8,128)(2,1)}, bf16[768,512]{1,0:T(8,128)(2,1)S(1)}, u32[]{:S(2)}) copy-start(bf16[768,512]{1,0:T(8,128)(2,1)S(1)} %get-tuple-element.184.vo) | copy-start | bytes 2359300
  116.4 62.9 %copy-start.15 = (bf16[768,512]{1,0:T(8,128)(2,1)}, bf16[768,512]{1,0:T(8,128)(2,1)S(1)}, u32[]{:S(2)}) copy-start(bf16[768,512]{1,0:T(8,128)(2,1)S(1)} %get-tuple-element.183.vo) | copy-start | bytes 2359300
  117.9 36.0 %collective-permute-start = (bf16[768,1024]{1,0:T(8,128)(2,1)}, bf16[768,1024]{1,0:T(8,128)(2,1)}, u32[]{:S(2)}, u32[]{:S(2)}) collective-permute-start(bf16[768,1024]{1,0:T(8,128)(2,1)} %pad_maximum_fusion.7), channel_id=1, source_target_pairs={{0,8},{4,12},{1,9},{5,13},{2,10},{6,14},{3,11},{7,15},{16,24},{20,... | collective-permute-start | bytes 4718600 | tf_op jit(solution)/shard_map/ppermute | solution.py:1006
  155.6 5.4 collective-permute-start.1
  166.8 861.5 %reduce-scatter.6.cloned.1.call-start = ((), (), s32[]{:S(2)}) async-start(), calls=%async_computation.6 | async-start | bytes 28311552 | tf_op jit(solution)/shard_map/reduce_scatter | solution.py:1051
  169.6 7.4 copy-start.75
  169.6 8.3 copy-start.67
  169.8 115.1 %collective-permute-start.2 = (bf16[768,1024]{1,0:T(8,128)(2,1)S(1)}, bf16[768,1024]{1,0:T(8,128)(2,1)}, u32[]{:S(2)}, u32[]{:S(2)}) collective-permute-start(bf16[768,1024]{1,0:T(8,128)(2,1)S(1)} %pad_maximum_fusion.8), channel_id=1, source_target_pairs={{0,8},{4,12},{1,9},{5,13},{2,10},{6,14},{3,11},{7,15},{16,24},{20,... | collective-permute-start | bytes 4718600 | tf_op jit(solution)/shard_map/ppermute | solution.py:1006
  179.2 12.6 %copy-start.37 = (bf16[768,512]{1,0:T(8,128)(2,1)}, bf16[768,512]{1,0:T(8,128)(2,1)S(1)}, u32[]{:S(2)}) copy-start(bf16[768,512]{1,0:T(8,128)(2,1)S(1)} %get-tuple-element.177.vp) | copy-start | bytes 2359300
  179.2 12.6 %copy-start.39 = (bf16[768,512]{1,0:T(8,128)(2,1)}, bf16[768,512]{1,0:T(8,128)(2,1)S(1)}, u32[]{:S(2)}) copy-start(bf16[768,512]{1,0:T(8,128)(2,1)S(1)} %get-tuple-element.178.kp) | copy-start | bytes 2359300
  179.3 12.5 %copy-start.41 = (bf16[768,512]{1,0:T(8,128)(2,1)}, bf16[768,512]{1,0:T(8,128)(2,1)S(1)}, u32[]{:S(2)}) copy-start(bf16[768,512]{1,0:T(8,128)(2,1)S(1)} %get-tuple-element.179.vt) | copy-start | bytes 2359300
  179.3 12.5 %copy-start.43 = (bf16[768,512]{1,0:T(8,128)(2,1)}, bf16[768,512]{1,0:T(8,128)(2,1)S(1)}, u32[]{:S(2)}) copy-start(bf16[768,512]{1,0:T(8,128)(2,1)S(1)} %get-tuple-element.180.kt) | copy-start | bytes 2359300
  288.2 4.2 collective-permute-start.3
  294.7 15.1 %copy-start.45 = (bf16[768,512]{1,0:T(8,128)(2,1)}, bf16[768,512]{1,0:T(8,128)(2,1)S(1)}, u32[]{:S(2)}) copy-start(bf16[768,512]{1,0:T(8,128)(2,1)S(1)} %get-tuple-element.173.vp) | copy-start | bytes 2359300
  294.7 15.1 %copy-start.47 = (bf16[768,512]{1,0:T(8,128)(2,1)}, bf16[768,512]{1,0:T(8,128)(2,1)S(1)}, u32[]{:S(2)}) copy-start(bf16[768,512]{1,0:T(8,128)(2,1)S(1)} %get-tuple-element.174.kp) | copy-start | bytes 2359300
  294.8 14.9 %copy-start.49 = (bf16[768,512]{1,0:T(8,128)(2,1)}, bf16[768,512]{1,0:T(8,128)(2,1)S(1)}, u32[]{:S(2)}) copy-start(bf16[768,512]{1,0:T(8,128)(2,1)S(1)} %get-tuple-element.175.vt) | copy-start | bytes 2359300
  294.8 14.9 %copy-start.51 = (bf16[768,512]{1,0:T(8,128)(2,1)}, bf16[768,512]{1,0:T(8,128)(2,1)S(1)}, u32[]{:S(2)}) copy-start(bf16[768,512]{1,0:T(8,128)(2,1)S(1)} %get-tuple-element.176.kt) | copy-start | bytes 2359300
  730.7 10.4 slice-start
  730.7 10.4 slice-start.4
  730.8 10.3 slice-start.1
  730.8 10.3 slice-start.5
  730.8 10.9 copy-start.63
  777.2 5.4 collective-permute-start.4
  786.2 39.1 %collective-permute-start.5 = (bf16[768,1024]{1,0:T(8,128)(2,1)}, bf16[768,1024]{1,0:T(8,128)(2,1)}, u32[]{:S(2)}, u32[]{:S(2)}) collective-permute-start(bf16[768,1024]{1,0:T(8,128)(2,1)} %add_convert_fusion.2.refs_1_), channel_id=1, source_target_pairs={{8,0},{12,4},{9,1},{13,5},{10,2},{14,6},{11,3},{15,7},{24,16},{28,... | collective-permute-start | bytes 4718600 | tf_op jit(solution)/shard_map/ppermute | solution.py:1041
  818.2 11.3 copy-start.5
  818.2 11.3 copy-start.20
  818.2 11.3 copy-start.24
  818.2 11.3 copy-start.26
  818.2 11.3 copy-start.28
  829.6 298.2 %reduce-scatter.4.cloned.1.call-start = ((), (), s32[]{:S(2)}) async-start(), calls=%async_computation.5 | async-start | bytes 7077888 | tf_op jit(solution)/shard_map/reduce_scatter | solution.py:1051
  833.1 7.6 collective-permute-start.6
  845.6 118.9 %collective-permute-start.7 = (bf16[768,1024]{1,0:T(8,128)(2,1)}, bf16[768,1024]{1,0:T(8,128)(2,1)}, u32[]{:S(2)}, u32[]{:S(2)}) collective-permute-start(bf16[768,1024]{1,0:T(8,128)(2,1)} %add_convert_fusion.1), channel_id=1, source_target_pairs={{8,0},{12,4},{9,1},{13,5},{10,2},{14,6},{11,3},{15,7},{24,16},{28,... | collective-permute-start | bytes 4718600 | tf_op jit(solution)/shard_map/ppermute | solution.py:1041
  862.0 94.4 %slice-start.6 = ((s8[6291456]{0:T(1024)(128)(4,1)}), s8[4194304]{0:T(1024)(128)(4,1)S(1)}, s32[]{:S(2)}) async-start(s8[6291456]{0:T(1024)(128)(4,1)} %bitcast.146), calls=%async_computation.14 | async-start | bytes 8388608
  871.7 84.7 %slice-start.7 = ((s8[6291456]{0:T(1024)(128)(4,1)}), s8[2097152]{0:T(1024)(128)(4,1)S(1)}, s32[]{:S(2)}) async-start(s8[6291456]{0:T(1024)(128)(4,1)} %bitcast.146), calls=%async_computation.15 | async-start | bytes 4194304
  956.4 8.1 copy-start.3
  998.4 141.9 %reduce-scatter.8.cloned.1.call-start = ((), (), s32[]{:S(2)}) async-start(), calls=%async_computation.7 | async-start | bytes 2949120 | tf_op jit(solution)/shard_map/reduce_scatter | solution.py:1051
  1007.6 8.6 copy-start.98
  1007.7 8.9 copy-start.79
  1007.7 8.9 copy-start.81
  1033.3 82.7 %slice-start.2 = ((s8[6291456]{0:T(1024)(128)(4,1)}), s8[2097152]{0:T(1024)(128)(4,1)S(1)}, s32[]{:S(2)}) async-start(s8[6291456]{0:T(1024)(128)(4,1)} %bitcast.121), calls=%async_computation.10 | async-start | bytes 4194304
  1033.3 82.7 %copy-start.4 = (bf16[768,2048]{1,0:T(8,128)(2,1)S(1)}, bf16[768,2048]{1,0:T(8,128)(2,1)}, u32[]{:S(2)}) copy-start(bf16[768,2048]{1,0:T(8,128)(2,1)} %copy-done.3) | copy-start | bytes 9437188
  1033.3 82.7 %slice-start.3 = ((s8[6291456]{0:T(1024)(128)(4,1)}), s8[4194304]{0:T(1024)(128)(4,1)S(1)}, s32[]{:S(2)}) async-start(s8[6291456]{0:T(1024)(128)(4,1)} %bitcast.121), calls=%async_computation.11 | async-start | bytes 8388608
  (78 other events, 206.1 us)
Sparse Core Ops, SparseCore 0:
  12.7 58.6 all-gather.4
  166.9 156.6 all-gather.6
  829.7 166.0 reduce-scatter.5
  999.6 61.7 reduce-scatter.3
  1064.9 43.6 reduce-scatter.7

commit v3 on v2

--- a/solution.py
+++ b/solution.py
@@ -34,6 +34,13 @@
 
 def cost(us):
     return pl.CostEstimate(flops=int(us * 1.1e9), bytes_accessed=0, transcendentals=0)
+
+
+def fold(rows):
+    total = rows[0:8]
+    for j in range(8, rows.shape[0], 8):
+        total += rows[j : j + 8]
+    return total
 
 
 def after(value, *earlier):
@@ -115,14 +122,32 @@
 
         pl.semaphore_wait(barrier, jnp.where(self.relay, 2, 1))
         self.load().wait()
-
+        self.launch(0, self.chunks)
+
+    def launch(self, first, last):
         @pl.when(~self.relay)
         def _():
             def one(c, carry):
                 self.inward_copy(c, self.slot).start()
                 return carry
 
-            lax.fori_loop(0, self.chunks, one, 0)
+            lax.fori_loop(first, last, one, 0)
+
+    def stream(self, job=None):
+        def step(c, carry):
+            if job is not None:
+                job(c)
+            self.reduce(c)
+
+            @pl.when(c > 0)
+            def _():
+                self.spread(c - 1)
+
+            return carry
+
+        lax.fori_loop(0, self.chunks, step, 0)
+        self.spread(self.chunks - 1)
+        self.end()
 
     def reduce(self, c):
         @pl.when(self.relay)
@@ -184,19 +209,7 @@
 def line_kernel(n, chunks, part, out, s, land, res, *sems):
     line = Line(n, chunks, part.shape[0] // chunks, part, out, s, land, res, sems)
     line.begin()
-
-    def step(c, carry):
-        line.reduce(c)
-
-        @pl.when(c > 0)
-        def _():
-            line.spread(c - 1)
-
-        return carry
-
-    lax.fori_loop(0, chunks, step, 0)
-    line.spread(chunks - 1)
-    line.end()
+    line.stream()
 
 
 def line_sum(part, collective_id):
@@ -210,71 +223,451 @@
         out_shape=jax.ShapeDtypeStruct(part.shape, bf16),
         scratch_shapes=line_scratch(rows, width, chunks),
         compiler_params=pltpu.CompilerParams(
-            collective_id=collective_id, has_side_effects=True, vmem_limit_bytes=48 << 20
+            collective_id=collective_id, has_side_effects=True, vmem_limit_bytes=60 << 20
         ),
         cost_estimate=cost(rows // 9),
         name="line_sum",
     )(part)
 
 
-def small_kernel(n, x, out, land, send, recv):
-    me = lax.axis_index("tensor")
-    barrier = pltpu.get_barrier_semaphore()
-    peers = [lax.rem(me + d, n) for d in range(1, n)]
-    for peer in peers:
-        pl.semaphore_signal(barrier, inc=1, device_id={"tensor": peer}, device_id_type=MESH)
-    land[me] = x[...]
-    pl.semaphore_wait(barrier, n - 1)
-    copies = [
-        pltpu.make_async_remote_copy(
-            src_ref=x,
-            dst_ref=land.at[me],
-            send_sem=send.at[d],
-            recv_sem=recv.at[me],
+LANES = 128
+
+
+def diagonal():
+    shape = (LANES, LANES)
+    return lax.broadcasted_iota(jnp.int32, shape, 0) == lax.broadcasted_iota(jnp.int32, shape, 1)
+
+
+def to_line(column):
+    return jnp.sum(jnp.where(diagonal(), column, 0.0), axis=0, keepdims=True)
+
+
+def to_column(line):
+    return jnp.sum(jnp.where(diagonal(), line, 0.0), axis=1, keepdims=True)
+
+
+class Exchange:
+    def __init__(self, n, lines, land, send, recv):
+        self.n, self.lines, self.land, self.send, self.recv = n, lines, land, send, recv
+        self.me = lax.axis_index("tensor")
+        self.peers = [lax.rem(self.me + d, n) for d in range(1, n)]
+
+    def greet(self):
+        barrier = pltpu.get_barrier_semaphore()
+        for peer in self.peers:
+            pl.semaphore_signal(barrier, inc=1, device_id={"tensor": peer}, device_id_type=MESH)
+
+    def met(self):
+        pl.semaphore_wait(pltpu.get_barrier_semaphore(), self.n - 1)
+
+    def copy(self, d, peer, slot):
+        return pltpu.make_async_remote_copy(
+            src_ref=self.lines,
+            dst_ref=self.land.at[slot],
+            send_sem=self.send.at[d],
+            recv_sem=self.recv.at[slot],
             device_id={"tensor": peer},
             device_id_type=MESH,
         )
-        for d, peer in enumerate(peers)
+
+    def total(self):
+        self.land[self.me] = self.lines[...]
+        for d, peer in enumerate(self.peers):
+            self.copy(d, peer, self.me).start()
+        for d, peer in enumerate(self.peers):
+            self.copy(d, peer, peer).wait_recv()
+        total = self.land[0]
+        for place in range(1, self.n):
+            total += self.land[place]
+        for d, peer in enumerate(self.peers):
+            self.copy(d, peer, self.me).wait_send()
+        return total
+
+
+def exchange_scratch(n, lines):
+    dma = pltpu.SemaphoreType.DMA
+    return [
+        pltpu.VMEM((2 * lines, LANES), f32),
+        pltpu.VMEM((n, 2 * lines, LANES), f32),
+        dma((n - 1,)),
+        dma((n,)),
     ]
-    for copy in copies:
-        copy.start()
-    for d, peer in enumerate(peers):
-        pltpu.make_async_remote_copy(
-            src_ref=x,
-            dst_ref=land.at[peer],
-            send_sem=send.at[d],
-            recv_sem=recv.at[peer],
-            device_id={"tensor": peer},
-            device_id_type=MESH,
-        ).wait_recv()
-    total = land[0]
-    for place in range(1, n):
-        total += land[place]
-    out[...] = total
-    for copy in copies:
-        copy.wait_send()
-
-
-def small_sum(x, collective_id):
+
+
+def line_count(rows):
+    return -(-rows // LANES // 8) * 8
+
+
+def qkv_kernel(n, rows, cols, x, w, qg, kg, q_low, kv_low, units, squares, raw, *net):
+    swap = Exchange(n, *net)
+    swap.greet()
+    lines = swap.lines.shape[0] // 2
+    swap.lines[...] = jnp.zeros_like(swap.lines)
+    step = math.gcd(rows, 384)
+    for r in range(0, rows, step):
+        at = slice(r, r + step)
+        for k in range(2):
+            value = matmul(x[at, :], w[:, k * cols : (k + 1) * cols])
+            raw[k, at, :] = value
+            square = jnp.sum(value * value, axis=1, keepdims=True)
+            for j in range(0, step, LANES):
+                spot = k * lines + (r + j) // LANES
+                swap.lines[spot : spot + 1, :] = to_line(square[j : j + LANES])
+    swap.met()
+    for r in range(0, rows, step):
+        at = slice(r, r + step)
+        kv_low[1, at, :] = matmul(x[at, :], w[:, 2 * cols : 3 * cols]).astype(bf16)
+    total = swap.total()
+    squares[...] = total
+    width = n * cols
+    for r in range(0, rows, LANES):
+        at = slice(r, r + LANES)
+        for k, gain in enumerate((qg, kg)):
+            spot = k * lines + r // LANES
+            square = to_column(total[spot : spot + 1, :])
+            unit = raw[k, at, :] * lax.rsqrt(square / width + norm_eps)
+            units[k, at, :] = unit
+            low = (unit * gain[...]).astype(bf16)
+            if k == 0:
+                q_low[at, :] = low
+            else:
+                kv_low[0, at, :] = low
+
+
+def qkv(x, w, qg, kg, m, rows, collective_id):
     n = lax.axis_size("tensor")
-    flat = x.reshape(-1, 128)
-    dma = pltpu.SemaphoreType.DMA
+    width = x.shape[1]
+    cols = qg.shape[1]
+    lines = line_count(rows)
     vmem = pl.BlockSpec(memory_space=pltpu.VMEM)
     return pl.pallas_call(
-        functools.partial(small_kernel, n),
-        in_specs=[vmem],
-        out_specs=vmem,
-        out_shape=jax.ShapeDtypeStruct(flat.shape, f32),
-        scratch_shapes=[pltpu.VMEM((n,) + flat.shape, f32), dma((n - 1,)), dma((n,))],
+        functools.partial(qkv_kernel, n, rows, cols),
+        grid=(1,),
+        in_specs=[
+            pl.BlockSpec((rows, width), lambda i: (m, 0)),
+            pl.BlockSpec((width, 3 * cols), lambda i: (0, 0)),
+            vmem,
+            vmem,
+        ],
+        out_specs=[vmem] * 4,
+        out_shape=[
+            jax.ShapeDtypeStruct((rows, cols), bf16),
+            jax.ShapeDtypeStruct((2, rows, cols), bf16),
+            jax.ShapeDtypeStruct((2, rows, cols), f32),
+            jax.ShapeDtypeStruct((2 * lines, LANES), f32),
+        ],
+        scratch_shapes=[pltpu.VMEM((2, rows, cols), f32)] + exchange_scratch(n, lines),
         compiler_params=pltpu.CompilerParams(
-            collective_id=collective_id, has_side_effects=True
+            collective_id=collective_id, has_side_effects=True, vmem_limit_bytes=60 << 20
         ),
-        cost_estimate=cost(7),
-        name="small_sum",
-    )(flat).reshape(x.shape)
+        cost_estimate=cost(15),
+        name="qkv",
+    )(x, w, qg, kg)
+
+
+def proj_kernel(cot, back, proj, gain, wo_t, layer, *refs):
+    low, grad, gain_grad, layer_out = refs[-4:]
+    layer_out[...] = layer[...]
+
+    @pl.when(pl.program_id(0) == 0)
+    def _():
+        gain_grad[...] = jnp.zeros_like(gain_grad)
+
+    step = ROW_STEP
+
+    def one(r, carry):
+        at = pl.ds(pl.multiple_of(r * step, step), step)
+        value = proj[at, :].astype(f32)
+        inv = lax.rsqrt(jnp.mean(value * value, axis=1, keepdims=True) + norm_eps)
+        unit = value * inv
+        hidden = cot[at, :].astype(f32) + back[at, :].astype(f32)
+        hit = hidden * unit
+        gain_grad[...] += fold(hit)
+        inner = jnp.mean(hit * gain[...], axis=1, keepdims=True)
+        low[at, :] = (inv * (hidden * gain[...] - unit * inner)).astype(bf16)
+        return carry
+
+    lax.fori_loop(0, low.shape[0] // step, one, 0)
+    grad[...] = matmul(low[...], wo_t[...]).astype(bf16)
+
+
+def proj_backward(cot, back, proj, gain, w, layer, layer_out, cols, m, rows, proj_m):
+    width = cot.shape[1]
+    step = BLOCK
+    blocks = rows // step
+
+    earlier = [] if layer_out is None else [layer_out]
+
+    def whole(first):
+        return pl.BlockSpec((step, width), lambda i: (first * blocks + i, 0))
+
+    return pl.pallas_call(
+        proj_kernel,
+        grid=(blocks,),
+        in_specs=[
+            whole(m),
+            whole(m),
+            whole(proj_m),
+            pl.BlockSpec((1, width), lambda i: (0, 0)),
+            pl.BlockSpec((width, cols), lambda i: (0, 3)),
+            whole(m),
+        ]
+        + [pl.BlockSpec(memory_space=pl.ANY)] * len(earlier),
+        out_specs=[
+            whole(0),
+            pl.BlockSpec((step, cols), lambda i: (i, 0)),
+            pl.BlockSpec((8, width), lambda i: (0, 0)),
+            whole(m),
+        ],
+        out_shape=[
+            jax.ShapeDtypeStruct((rows, width), bf16),
+            jax.ShapeDtypeStruct((rows, cols), bf16),
+            jax.ShapeDtypeStruct((8, width), f32),
+            jax.ShapeDtypeStruct(cot.shape, bf16),
+        ],
+        input_output_aliases={6: 3} if earlier else {},
+        compiler_params=pltpu.CompilerParams(vmem_limit_bytes=60 << 20),
+        cost_estimate=cost(10),
+        name="proj_backward",
+    )(cot, back, proj, gain, w, layer, *earlier)
+
+
+class Grads:
+    def __init__(self, to, stage, sem):
+        self.to, self.stage, self.sem = to, stage, sem
+        self.wide = stage.shape[1]
+
+    def at(self, owner):
+        return pl.ds(pl.multiple_of(owner * self.wide, self.wide), self.wide)
+
+    def store(self, owner, slot):
+        width = self.stage.shape[2]
+        return pltpu.make_async_copy(
+            self.stage.at[slot], self.to.at[self.at(owner), pl.ds(0, width)], self.sem.at[slot]
+        )
+
+
+def last_kernel(
+    n, rows, cols, sources, stream, dq, own, mine, got, units, squares, qg, kg, x, proj, attn,
+    before, others, w, low, out, gain_grad, g_attn, *scratch,
+):
+    swap = Exchange(n, *scratch[:4])
+    swap.greet()
+    xin, x_sem, stage, g_sem = scratch[4:8]
+    load_x = pltpu.make_async_copy(x.at[0 if stream else 1], xin, x_sem)
+    load_x.start()
+    grads = Grads(g_attn, stage, g_sem)
+    owners = xin.shape[1] // grads.wide
+    if stream:
+        s, land, res, pin, p_sem = scratch[8:13]
+        loads = [pltpu.make_async_copy(proj[m], pin.at[m], p_sem.at[m]) for m in range(2)]
+        for load in loads:
+            load.start()
+    else:
+        s = out
+        had, b_sem, gains, n_sem = scratch[8:12]
+
+        def load_before(owner, slot):
+            return pltpu.make_async_copy(
+                before.at[grads.at(owner), pl.ds(0, 3 * cols)], had.at[slot], b_sem.at[slot]
+            )
+
+        load_before(0, 0).start()
+    lines = swap.lines.shape[0] // 2
+    swap.lines[...] = jnp.zeros_like(swap.lines)
+    gain_grad[...] = jnp.zeros_like(gain_grad)
+    scale = jnp.where(sources, 1.0, 0.0).astype(f32)
+    width = n * cols
+
+    def gathered(k, at):
+        both = mine[k, at, :].astype(f32) + got[k, at, :].astype(f32)
+        return own[k, at, :] + scale * both
+
+    for r in range(0, rows, LANES):
+        at = slice(r, r + LANES)
+        for k, gain in enumerate((qg, kg)):
+            grad = dq[at, :] if k == 0 else gathered(0, at)
+            hit = grad * units[k, at, :]
+            gain_grad[8 * k : 8 * k + 8, :] += fold(hit)
+            spot = k * lines + r // LANES
+            swap.lines[spot : spot + 1, :] = to_line(
+                jnp.sum(hit * gain[...], axis=1, keepdims=True)
+            )
+    swap.met()
+    total = swap.total()
+    for r in range(0, rows, LANES):
+        at = slice(r, r + LANES)
+        for k, gain in enumerate((qg, kg)):
+            spot = k * lines + r // LANES
+            inner = to_column(total[spot : spot + 1, :]) / width
+            inv = lax.rsqrt(to_column(squares[spot : spot + 1, :]) / width + norm_eps)
+            grad = dq[at, :] if k == 0 else gathered(0, at)
+            value = inv * (grad * gain[...] - units[k, at, :] * inner)
+            low[at, k * cols : (k + 1) * cols] = value.astype(bf16)
+        low[at, 2 * cols :] = gathered(1, at).astype(bf16)
+    if stream:
+        line = Line(n, out.shape[0] // 48, 48, None, out, s, land, res, scratch[13:])
+    step = math.gcd(rows, 384)
+    piece = math.gcd(s.shape[1], 512)
+    for r in range(0, rows, step):
+        at = slice(r, r + step)
+        for c in range(0, s.shape[1], piece):
+            s[at, c : c + piece] = right_t(low[at, :], w[c : c + piece, :]).astype(bf16)
+        if stream:
+            line.launch(r // 48, (r + step) // 48)
+
+    def narrow(array, owner, small):
+        return left_t(array[:, grads.at(owner)], small)
+
+    def drain():
+        for owner in range(max(owners - 2, 0), owners):
+            grads.store(owner, owner % 2).wait()
+
+    if stream:
+
+        def job(owner):
+            slot = lax.rem(owner, 2)
+
+            @pl.when(owner == 0)
+            def _():
+                load_x.wait()
+                for load in loads:
+                    load.wait()
+
+            @pl.when((owner >= 2) & (owner < owners))
+            def _():
+                grads.store(owner - 2, slot).wait()
+
+            @pl.when(owner < owners)
+            def _():
+                stage[slot, :, : 3 * cols] = narrow(xin, owner, low[...]).astype(bf16)
+                stage[slot, :, 3 * cols :] = (
+                    narrow(pin.at[0], owner, attn[0][...])
+                    + narrow(pin.at[1], owner, attn[1][...])
+                ).astype(bf16)
+                grads.store(owner, slot).start()
+
+        assert owners <= rows // 48
+        line.stream(job)
+        drain()
+    else:
+        load_x.wait()
+
+        def one(owner, carry):
+            slot = lax.rem(owner, 2)
+            load_before(owner, slot).wait()
+
+            @pl.when(owner < owners - 1)
+            def _():
+                load_before(owner + 1, 1 - slot).start()
+
+            @pl.when(owner >= 2)
+            def _():
+                grads.store(owner - 2, slot).wait()
+
+            value = narrow(xin, owner, low[...]) + had[slot].astype(f32)
+            stage[slot] = value.astype(bf16)
+            grads.store(owner, slot).start()
+            return carry
+
+        lax.fori_loop(0, owners, one, 0)
+        heads = cols // HD
+        parts = grads.wide // LANES
+        gains[...] = jnp.zeros_like(gains)
+        first = others[0][...]
+        for k in range(2):
+            both = gain_grad[8 * k : 8 * k + 8, :] + first[8 * k : 8 * k + 8, :]
+            total = jnp.sum(both, axis=0, keepdims=True)
+            for owner in range(owners):
+                for h in range(heads):
+                    gains[owner, k * heads + h, :] = total[0, h * HD : (h + 1) * HD]
+        for k, items in enumerate((others[1:3], others[3:])):
+            total = sum(jnp.sum(item[...], axis=0, keepdims=True) for item in items)
+            for owner in range(owners):
+                for j in range(parts):
+                    at = (owner * parts + j) * LANES
+                    gains[owner, 2 * heads + k * parts + j, :] = total[0, at : at + LANES]
+        low_gains, stores = scratch[12], []
+        low_gains[...] = gains[...].astype(bf16)
+        for owner in range(owners):
+            at = pl.ds(owner * grads.wide, low_gains.shape[1])
+            to = g_attn.at[at, pl.ds(4 * cols, LANES)]
+            stores.append(pltpu.make_async_copy(low_gains.at[owner], to, n_sem.at[owner]))
+        for store in stores:
+            store.start()
+        for store in stores:
+            store.wait()
+        drain()
+
+
+def last_sum(
+    dq, own, mine, got, units, squares, qg, kg, x, extra, before, w, owners, collective_id
+):
+    stream = before is None
+    n = lax.axis_size("tensor")
+    rows, cols = dq.shape
+    width = w.shape[0]
+    lines = line_count(rows)
+    vmem = pl.BlockSpec(memory_space=pltpu.VMEM)
+    hbm = pl.BlockSpec(memory_space=pl.ANY)
+    dma = pltpu.SemaphoreType.DMA
+    wide = width // owners
+    weights = pl.BlockSpec((width, 3 * cols), lambda i: (0, 0))
+
+    def kernel(*refs):
+        sources = lax.axis_index("seq") < lax.axis_size("seq") // 2
+        args = [n, rows, cols, sources, stream, *refs[:9]]
+        if stream:
+            args += [refs[9:11], refs[11:13], None, None, *refs[13:]]
+        else:
+            args += [None, None, refs[9], refs[10:14], *refs[14:]]
+        last_kernel(*args)
+
+    if stream:
+        extra_specs = [hbm, hbm, vmem, vmem]
+    else:
+        extra, extra_specs = [before, *extra], [hbm] + [vmem] * 4
+    shapes = [
+        jax.ShapeDtypeStruct((rows, 3 * cols), bf16),
+        jax.ShapeDtypeStruct((rows, width), bf16),
+        jax.ShapeDtypeStruct((16, cols), f32),
+        jax.ShapeDtypeStruct((width, 4 * cols + LANES), bf16),
+    ]
+    scratch = exchange_scratch(n, lines) + [
+        pltpu.VMEM((rows, width), bf16),
+        dma(()),
+        pltpu.VMEM((2, wide, (4 if stream else 3) * cols), bf16),
+        dma((2,)),
+    ]
+    if stream:
+        line = line_scratch(rows, width, rows // 48)
+        scratch += line[:3] + [pltpu.VMEM((2, rows, width), bf16), dma((2,))] + line[3:]
+    else:
+        scratch += [
+            pltpu.VMEM((2, wide, 3 * cols), bf16),
+            dma((2,)),
+            pltpu.VMEM((owners, 16, LANES), f32),
+            dma((owners,)),
+            pltpu.VMEM((owners, 16, LANES), bf16),
+        ]
+    return pl.pallas_call(
+        kernel,
+        grid=(1,),
+        in_specs=[vmem] * 8 + [hbm] + extra_specs + [weights],
+        out_specs=[vmem, hbm if stream else vmem, vmem, hbm],
+        out_shape=shapes,
+        scratch_shapes=scratch,
+        input_output_aliases={} if stream else {9: 3},
+        compiler_params=pltpu.CompilerParams(
+            collective_id=collective_id, has_side_effects=True, vmem_limit_bytes=60 << 20
+        ),
+        cost_estimate=cost(100 if stream else 25),
+        name="last_sum" if stream else "last_part",
+    )(dq, own, mine, got, units, squares, qg, kg, x, *extra, w)
 
 
 LINE_ROWS = 48
+ROW_STEP = 32
 LAG = 3
 TILE = 256
 NAMES = (
@@ -371,7 +764,8 @@
         self.each_chunk(one)
 
     def begin(self):
-        load = pltpu.make_async_copy(self.part, self.s, self.load_sem)
+        others = pl.ds(self.rows, (self.micros - 1) * self.rows)
+        load = pltpu.make_async_copy(self.part, self.s.at[others], self.load_sem)
         load.start()
         rest = self.micro(0)
         done = pltpu.make_async_copy(self.first, self.res.at[rest], self.y_sem)
@@ -485,7 +879,7 @@
         )
 
     def row_groups(self, body):
-        step = 16
+        step = ROW_STEP
 
         def one(r, carry):
             body(pl.ds(pl.multiple_of(r * step, step), step), r * step)
@@ -503,7 +897,7 @@
         gain = self.ga[...]
 
         def one(at, r):
-            total = self.res[pl.ds(pl.multiple_of(base + r, 16), 16), :].astype(f32)
+            total = self.res[pl.ds(pl.multiple_of(base + r, ROW_STEP), ROW_STEP), :].astype(f32)
             inv = lax.rsqrt(jnp.mean(total * total, axis=1, keepdims=True) + norm_eps)
             self.h[at, :] = (self.xin[at, :].astype(f32) + total * inv * gain).astype(bf16)
 
@@ -519,13 +913,13 @@
         gain = self.gm[...]
 
         def one(at, r):
-            total = self.res[pl.ds(pl.multiple_of(base + r, 16), 16), :].astype(f32)
+            total = self.res[pl.ds(pl.multiple_of(base + r, ROW_STEP), ROW_STEP), :].astype(f32)
             inv = lax.rsqrt(jnp.mean(total * total, axis=1, keepdims=True) + norm_eps)
             unit = total * inv
             c = self.cin[at, :].astype(f32)
             self.xin[at, :] = (self.xin[at, :].astype(f32) + unit * gain).astype(bf16)
             hit = c * unit
-            self.gm_grad[...] += hit[0:8, :] + hit[8:16, :]
+            self.gm_grad[...] += fold(hit)
             dy = c * gain
             inner = jnp.mean(hit * gain, axis=1, keepdims=True)
             self.h[at, :] = (inv * (dy - unit * inner)).astype(bf16)
@@ -701,7 +1095,7 @@
         base = m * self.rows
 
         def one(at, r):
-            self.s[pl.ds(pl.multiple_of(base + r, 16), 16), :] = self.acc[at, :].astype(bf16)
+            self.s[pl.ds(pl.multiple_of(base + r, ROW_STEP), ROW_STEP), :] = self.acc[at, :].astype(bf16)
 
         self.row_groups(one)
         self.launch(m)
@@ -868,9 +1262,9 @@
     return st, sp, so
 
 
-def attn_fwd_kernel(trunk_rows, meta, q, kt, vt, kp, vp, ko, vo, out, lse):
+def attn_fwd_kernel(trunk_rows, meta, q, trunk, par, own, out, lse):
     i = pl.program_id(1)
-    st, sp, so = attn_scores(meta, i, trunk_rows, q[...], kt[...], kp[...], ko[...])
+    st, sp, so = attn_scores(meta, i, trunk_rows, q[...], trunk[0], par[0], own[0])
     top = jnp.maximum(
         jnp.max(st, axis=1, keepdims=True),
         jnp.maximum(jnp.max(sp, axis=1, keepdims=True), jnp.max(so, axis=1, keepdims=True)),
@@ -881,62 +1275,58 @@
         + jnp.sum(ep, axis=1, keepdims=True)
         + jnp.sum(eo, axis=1, keepdims=True)
     )
-    acc = matmul(et.astype(bf16), vt[...])
-    acc += matmul(ep.astype(bf16), vp[...])
-    acc += matmul(eo.astype(bf16), vo[...])
+    acc = matmul(et.astype(bf16), trunk[1])
+    acc += matmul(ep.astype(bf16), par[1])
+    acc += matmul(eo.astype(bf16), own[1])
     out[...] = (acc / total).astype(bf16)
     lse[...] = jnp.broadcast_to(top + jnp.log(total), (BLOCK, HD))
 
 
 def attn_bwd_kernel(
-    trunk_rows, n_q, meta, q, do, lse, kt, vt, kp, vp, ko, vo,
-    dq, dko, dvo, dkt, dvt, dkb, dvb, a_kt, a_vt, a_kb, a_vb,
+    trunk_rows, n_q, meta, q, do, lse, trunk, par, own, dq, d_own, d_src, acc,
 ):
     i = pl.program_id(1)
 
     @pl.when(i == 0)
     def _():
-        for acc in (a_kt, a_vt, a_kb, a_vb):
-            acc[...] = jnp.zeros_like(acc)
+        acc[...] = jnp.zeros_like(acc)
 
     scale = HD ** (-0.5)
     qv, dov = q[...], do[...]
-    scores = attn_scores(meta, i, trunk_rows, qv, kt[...], kp[...], ko[...])
+    scores = attn_scores(meta, i, trunk_rows, qv, trunk[0], par[0], own[0])
     top = lse[:, 0:1]
     probs = [jnp.exp(s - top) for s in scores]
-    grads = [right_t(dov, v[...]) for v in (vt, vp, vo)]
+    grads = [right_t(dov, v[1]) for v in (trunk, par, own)]
     inner = sum(jnp.sum(p * g, axis=1, keepdims=True) for p, g in zip(probs, grads))
     low = [(p * (g - inner)).astype(bf16) for p, g in zip(probs, grads)]
     probs = [p.astype(bf16) for p in probs]
     dq[...] = scale * (
-        matmul(low[0], kt[...]) + matmul(low[1], kp[...]) + matmul(low[2], ko[...])
+        matmul(low[0], trunk[0]) + matmul(low[1], par[0]) + matmul(low[2], own[0])
     )
-    a_kt[...] += left_t(low[0], qv)
-    a_vt[...] += left_t(probs[0], dov)
-    dko[...] = scale * left_t(low[2], qv)
-    dvo[...] = left_t(probs[2], dov)
-    at = pl.ds(pl.multiple_of(meta[i, 1] * BLOCK, BLOCK), BLOCK)
-    a_kb[at, :] += left_t(low[1], qv)
-    a_vb[at, :] += left_t(probs[1], dov)
+    d_own[0] = scale * left_t(low[2], qv)
+    d_own[1] = left_t(probs[2], dov)
+    acc[0, :trunk_rows] += left_t(low[0], qv)
+    acc[1, :trunk_rows] += left_t(probs[0], dov)
+    at = pl.ds(pl.multiple_of(trunk_rows + meta[i, 1] * BLOCK, BLOCK), BLOCK)
+    acc[0, at] += left_t(low[1], qv)
+    acc[1, at] += left_t(probs[1], dov)
 
     @pl.when(i == n_q - 1)
     def _():
-        dkt[...] = (scale * a_kt[...]).astype(bf16)
-        dvt[...] = a_vt[...].astype(bf16)
-        dkb[...] = (scale * a_kb[...]).astype(bf16)
-        dvb[...] = a_vb[...].astype(bf16)
+        d_src[0] = (scale * acc[0]).astype(bf16)
+        d_src[1] = acc[1].astype(bf16)
 
 
 def kv_specs(trunk_rows):
-    trunk = pl.BlockSpec((trunk_rows, HD), lambda h, i, meta: (0, h))
-    par = pl.BlockSpec((BLOCK, HD), lambda h, i, meta: (meta[i, 1], h))
-    own = pl.BlockSpec((BLOCK, HD), lambda h, i, meta: (i, h))
-    return [trunk, trunk, par, par, own, own]
-
-
-def attend_forward(meta, q, kv):
+    skip = trunk_rows // BLOCK
+    trunk = pl.BlockSpec((2, trunk_rows, HD), lambda h, i, meta: (0, 0, h))
+    par = pl.BlockSpec((2, BLOCK, HD), lambda h, i, meta: (0, skip + meta[i, 1], h))
+    own = pl.BlockSpec((2, BLOCK, HD), lambda h, i, meta: (0, i, h))
+    return [trunk, par, own]
+
+
+def attend_forward(meta, q, sources, own_kv, trunk_rows):
     rows, width = q.shape
-    trunk_rows = kv[0].shape[0]
     own = pl.BlockSpec((BLOCK, HD), lambda h, i, meta: (i, h))
     return pl.pallas_call(
         functools.partial(attn_fwd_kernel, trunk_rows),
@@ -953,16 +1343,14 @@
         compiler_params=pltpu.CompilerParams(vmem_limit_bytes=32 << 20),
         cost_estimate=cost(12),
         name="attend_forward",
-    )(meta, q, *kv)
-
-
-def attend_backward(meta, q, do, lse, kv):
+    )(meta, q, sources, sources, own_kv)
+
+
+def attend_backward(meta, q, do, lse, sources, own_kv, trunk_rows):
     rows, width = q.shape
-    trunk_rows = kv[0].shape[0]
-    branch_rows = kv[2].shape[0]
     own = pl.BlockSpec((BLOCK, HD), lambda h, i, meta: (i, h))
-    trunk = pl.BlockSpec((trunk_rows, HD), lambda h, i, meta: (0, h))
-    branch = pl.BlockSpec((branch_rows, HD), lambda h, i, meta: (0, h))
+    own_two = pl.BlockSpec((2, BLOCK, HD), lambda h, i, meta: (0, i, h))
+    all_rows = sources.shape[1]
     n_q = rows // BLOCK
     return pl.pallas_call(
         functools.partial(attn_bwd_kernel, trunk_rows, n_q),
@@ -970,27 +1358,22 @@
             num_scalar_prefetch=1,
             grid=(width // HD, n_q),
             in_specs=[own, own, own] + kv_specs(trunk_rows),
-            out_specs=[own, own, own, trunk, trunk, branch, branch],
-            scratch_shapes=[
-                pltpu.VMEM((trunk_rows, HD), f32),
-                pltpu.VMEM((trunk_rows, HD), f32),
-                pltpu.VMEM((branch_rows, HD), f32),
-                pltpu.VMEM((branch_rows, HD), f32),
+            out_specs=[
+                own,
+                own_two,
+                pl.BlockSpec((2, all_rows, HD), lambda h, i, meta: (0, 0, h)),
             ],
+            scratch_shapes=[pltpu.VMEM((2, all_rows, HD), f32)],
         ),
         out_shape=[
             jax.ShapeDtypeStruct((rows, width), f32),
-            jax.ShapeDtypeStruct((rows, width), f32),
-            jax.ShapeDtypeStruct((rows, width), f32),
-            jax.ShapeDtypeStruct((trunk_rows, width), bf16),
-            jax.ShapeDtypeStruct((trunk_rows, width), bf16),
-            jax.ShapeDtypeStruct((branch_rows, width), bf16),
-            jax.ShapeDtypeStruct((branch_rows, width), bf16),
+            jax.ShapeDtypeStruct((2, rows, width), f32),
+            jax.ShapeDtypeStruct(sources.shape, bf16),
         ],
         compiler_params=pltpu.CompilerParams(vmem_limit_bytes=40 << 20),
         cost_estimate=cost(22),
         name="attend_backward",
-    )(meta, q, do, lse, *kv)
+    )(meta, q, do, lse, sources, sources, own_kv)
 
 
 def group_perm(n, k):
@@ -1012,15 +1395,15 @@
         for k in range(1, half):
             pick = jnp.where(lax.rem(spot - k + half, half) == source, parts[k], pick)
         out.append(pick)
-    return jnp.concatenate(out, axis=0)
+    return jnp.concatenate(out, axis=1)
 
 
 def sum_over_group(grads):
     n = lax.axis_size("seq")
     half = n // 2
     spot = lax.rem(lax.axis_index("seq"), half)
-    rows = grads.shape[0] // half
-    pieces = [grads[s * rows : (s + 1) * rows] for s in range(half)]
+    rows = grads.shape[1] // half
+    pieces = [grads[:, s * rows : (s + 1) * rows] for s in range(half)]
 
     def piece(index):
         pick = pieces[0]
@@ -1038,19 +1421,19 @@
 def return_to_sources(total):
     n = lax.axis_size("seq")
     half = n // 2
-    got = lax.ppermute(total, "seq", [(i + half, i) for i in range(half)])
-    both = total.astype(f32) + got.astype(f32)
-    return jnp.where(lax.axis_index("seq") < half, both, 0.0)
+    return lax.ppermute(total, "seq", [(i + half, i) for i in range(half)])
 
 
 def gather_rows(item):
     return lax.all_gather(item, ("dp", "seq"), axis=0, tiled=True)
 
 
+def scatter_low(item):
+    return lax.psum_scatter(item, ("dp", "seq"), scatter_dimension=0, tiled=True)
+
+
 def scatter_rows(item):
-    return lax.psum_scatter(
-        item.astype(bf16), ("dp", "seq"), scatter_dimension=0, tiled=True
-    ).astype(f32)
+    return scatter_low(item).astype(f32)
 
 
 def block_meta(parents, lengths, rows, n_blocks):
@@ -1092,6 +1475,8 @@
     w_attn = gather_rows(jnp.concatenate([w_query, w_key, w_value, w_out.T], axis=1))
     gains = [query_gain.reshape(-1), key_gain.reshape(-1), attn_gain, mlp_gain]
     gains = lax.all_gather(jnp.concatenate(gains), ("dp", "seq"), axis=0, tiled=False)
+    w_own = jnp.concatenate([w_gate, w_up, w_down.T], axis=1)
+    gains = after(gains, w_own)
     own = query_gain.size
 
     def head_gain(block):
@@ -1102,86 +1487,47 @@
     k_gain = head_gain(gains[:, own : 2 * own])
     a_gain = gains[:, 2 * own : 2 * own + attn_gain.size].reshape(-1).astype(f32)
     m_gain = gains[:, 2 * own + attn_gain.size :].reshape(-1).astype(f32)
-    wq, wk, wv = (w_attn[:, k * cols : (k + 1) * cols] for k in range(3))
     wo_t = w_attn[:, 3 * cols :]
-
-    def part_of(array, m):
-        return array[m * rows : (m + 1) * rows]
+    q_gain, k_gain, a_gain = q_gain[None], k_gain[None], a_gain[None]
 
     x = tokens.reshape(micros * rows, width)
     cot = cotangent.reshape(micros * rows, width)
-    q_raw, k_raw, v_raw = matmul(x, wq), matmul(x, wk), matmul(x, wv)
-    q_sq, k_sq = small_sum(
-        jnp.stack([jnp.sum(q_raw * q_raw, axis=1), jnp.sum(k_raw * k_raw, axis=1)]), 2
+    q_lows, kv_lows, units, squares = zip(
+        *(qkv(x, w_attn, q_gain, k_gain, m, rows, 6 + m) for m in range(micros))
     )
-    q_inv = lax.rsqrt(q_sq / full_width + norm_eps)[:, None]
-    k_inv = lax.rsqrt(k_sq / full_width + norm_eps)[:, None]
-    q_unit, k_unit = q_raw * q_inv, k_raw * k_inv
-    q_low = (q_unit * q_gain).astype(bf16)
-    k_low = (k_unit * k_gain).astype(bf16)
-    v_low = v_raw.astype(bf16)
-
-    kvs, metas, attn_lows, lses, parts, first = [], [], [], [], [], None
+    sources, metas, attn_lows, lses, parts, first = [], [], [], [], [], None
     for m in range(micros):
-        k_own, v_own = part_of(k_low, m), part_of(v_low, m)
-        sources = fetch_sources(jnp.concatenate([k_own, v_own], axis=1), first)
-        kvs.append(
-            (
-                sources[:trunk_rows, :cols],
-                sources[:trunk_rows, cols:],
-                sources[trunk_rows:, :cols],
-                sources[trunk_rows:, cols:],
-                k_own,
-                v_own,
-            )
-        )
+        sources.append(fetch_sources(kv_lows[m], q_lows[1] if m == 0 else first))
         metas.append(block_meta(parent_of[m, 0], seg_length[m, 0], rows, n_blocks))
-        attn_low, lse = attend_forward(metas[m], part_of(q_low, m), kvs[m])
+        attn_low, lse = attend_forward(metas[m], q_lows[m], sources[m], kv_lows[m], trunk_rows)
         attn_lows.append(attn_low)
         lses.append(lse)
         parts.append(right_t(attn_low, wo_t).astype(bf16))
         if m == 0:
             first = line_sum(parts[0], 0)
-            w_own = jnp.concatenate([w_gate, w_up, w_down.T], axis=1)
-            w_mlp = gather_rows(after(w_own, sources))
-    proj, _, _, layer_out, _, _, back, _, mlp_grads, gm_grad = feed_forward(
-        jnp.concatenate(parts, axis=0), x, cot, w_mlp, a_gain[None], m_gain[None], first,
+            w_mlp = gather_rows(after(w_own, sources[0]))
+    proj, _, _, layer, _, _, back, _, mlp_grads, gm_grad = feed_forward(
+        parts[1], x, cot, w_mlp, a_gain, m_gain[None], first,
         micros, owners,
     )
-    units = w_gate.shape[1]
-    ga_grad = 0.0
-    proj_lows, dqs, owns, sums = [], [], [], []
+    hidden = w_gate.shape[1]
+    g_attn, qk_grad, ga_grads, layer_out = None, None, [], None
+    proj_lows, dqs, d_owns, sums = [], [], [], []
     for m in range(micros):
-        attn_proj = (first if m == 0 else part_of(proj, m)).astype(f32)
-        attn_inv = lax.rsqrt(jnp.mean(attn_proj * attn_proj, axis=1, keepdims=True) + norm_eps)
-        attn_unit = attn_proj * attn_inv
-        hidden_grad = part_of(cot, m).astype(f32) + part_of(back, m).astype(f32)
-        ga_grad += jnp.sum(hidden_grad * attn_unit, axis=0)
-        unit_grad = hidden_grad * a_gain
-        proj_low = (
-            attn_inv
-            * (unit_grad - attn_unit * jnp.mean(unit_grad * attn_unit, axis=1, keepdims=True))
-        ).astype(bf16)
-        attn_grad = matmul(proj_low, wo_t).astype(bf16)
-        if m > 0:
-            attn_grad = after(attn_grad, sums[-1])
-        dq, dko, dvo, dkt, dvt, dkb, dvb = attend_backward(
-            metas[m], part_of(q_low, m), attn_grad, lses[m], kvs[m]
-        )
-        sums.append(
-            sum_over_group(
-                jnp.concatenate(
-                    [jnp.concatenate([dkt, dvt], axis=1), jnp.concatenate([dkb, dvb], axis=1)],
-                    axis=0,
-                )
-            )
-        )
+        proj_low, attn_grad, grad, layer_out = proj_backward(
+            cot, back, first if m == 0 else proj, after(a_gain, sums[0]) if m else a_gain, w_attn,
+            layer, layer_out, cols, m, rows, m
+        )
+        ga_grads.append(grad)
+        dq, d_own, d_src = attend_backward(
+            metas[m], q_lows[m], attn_grad, lses[m], sources[m], kv_lows[m], trunk_rows
+        )
+        sums.append(sum_over_group(d_src))
         proj_lows.append(proj_low)
         dqs.append(dq)
-        owns.append((dko, dvo))
-
-    qkv_lows, lasts = [], []
-    qg_grad = kg_grad = g_qkv = 0.0
+        d_owns.append(d_own)
+
+    lasts = []
     for m in range(micros):
         got = return_to_sources(sums[m])
         if m > 0:
@@ -1189,65 +1535,37 @@
         else:
             got = after(got, dqs[-1])
             mlp_grads = after(mlp_grads.reshape(-1, mlp_grads.shape[2]), got)
-            mlp_grads = scatter_rows(mlp_grads)
-        dq, dk, dv = dqs[m], owns[m][0] + got[:, :cols], owns[m][1] + got[:, cols:]
-        q_u, k_u = part_of(q_unit, m), part_of(k_unit, m)
-        qg_grad += jnp.sum(dq * q_u, axis=0)
-        kg_grad += jnp.sum(dk * k_u, axis=0)
-        q_scaled, k_scaled = dq * q_gain, dk * k_gain
-        q_inner, k_inner = small_sum(
-            jnp.stack([jnp.sum(q_scaled * q_u, axis=1), jnp.sum(k_scaled * k_u, axis=1)]), 4
-        )
-        q_inner, k_inner = q_inner[:, None] / full_width, k_inner[:, None] / full_width
-        qr_low = (part_of(q_inv, m) * (q_scaled - q_u * q_inner)).astype(bf16)
-        kr_low = (part_of(k_inv, m) * (k_scaled - k_u * k_inner)).astype(bf16)
-        qkv_lows.append(jnp.concatenate([qr_low, kr_low, dv.astype(bf16)], axis=1))
-        part = right_t(qkv_lows[m], w_attn[:, : 3 * cols]).astype(bf16)
-        g_qkv += left_t(part_of(x, m), qkv_lows[m])
-        if m > 0:
-            g_qkv = g_qkv.astype(bf16)
-            part = after(part, g_qkv)
-        lasts.append(line_sum(part, 3))
-    g_qkv = scatter_rows(g_qkv)
+            mlp_grads = scatter_low(mlp_grads)
+        extra = [*proj_lows, *attn_lows] if m == 0 else [qk_grad, *ga_grads, gm_grad]
+        _, last, qk_grad, g_attn = last_sum(
+            dqs[m], d_owns[m], sums[m], got, units[m], squares[m], q_gain, k_gain,
+            x.reshape(micros, rows, width), extra, g_attn, w_attn, owners, 5 if m else 3,
+        )
+        lasts.append(line_sum(last, 4) if m else last)
+    g_attn = scatter_low(after(g_attn, mlp_grads))
+    g_attn = after(g_attn, qk_grad).astype(f32)
     last = jnp.concatenate(lasts, axis=0)
 
-    def head_grad(value):
-        return jnp.swapaxes(value.reshape(heads, owners, HD // owners), 0, 1).reshape(owners, -1)
-
-    gain_grads = jnp.concatenate(
-        [
-            head_grad(qg_grad),
-            head_grad(kg_grad),
-            ga_grad.reshape(owners, -1),
-            jnp.sum(gm_grad, axis=0).reshape(owners, -1),
-        ],
-        axis=1,
-    )
-    count = gain_grads.shape[1]
-    lines = -(-count // 128)
-    gain_grads = jnp.pad(gain_grads, ((0, 0), (0, lines * 128 - count)))
-    gain_grads = gain_grads.reshape(owners, lines, 128)
-    gain_grads = jnp.pad(gain_grads, ((0, 0), (0, width // owners - lines), (0, 0)))
-    proj_low = after(jnp.concatenate(proj_lows, axis=0), lasts[0])
-    g_out = left_t(proj_low, jnp.concatenate(attn_lows, axis=0))
-    g_out = jnp.concatenate([g_out, gain_grads.reshape(width, 128)], axis=1).astype(bf16)
-    g_out = scatter_rows(after(g_out, mlp_grads))
-    gain_grads = g_out[:lines, cols:].reshape(-1)
+    lines = g_attn[:, 4 * cols :]
+    share = HD // owners
+    place = lax.axis_index("dp") * lax.axis_size("seq") + lax.axis_index("seq")
+    head_lines = lax.dynamic_slice_in_dim(lines[: 2 * heads], place * share, share, 1)
+    own_lines = lines[2 * heads : 2 * heads + 2 * attn_gain.size // LANES].reshape(2, -1)
     input_grad = cot.astype(f32) + back.astype(f32) + last.astype(f32)
     return (
         layer_out.reshape(tokens.shape),
         input_grad.reshape(tokens.shape),
-        g_qkv[:, :cols],
-        g_qkv[:, cols : 2 * cols],
-        g_qkv[:, 2 * cols :],
-        g_out[:, :cols].T,
-        mlp_grads[:units].T,
-        mlp_grads[units : 2 * units].T,
-        mlp_grads[2 * units :],
-        gain_grads[:own].reshape(query_gain.shape),
-        gain_grads[own : 2 * own].reshape(key_gain.shape),
-        gain_grads[2 * own : 2 * own + attn_gain.size],
-        gain_grads[2 * own + attn_gain.size : count],
+        g_attn[:, :cols],
+        g_attn[:, cols : 2 * cols],
+        g_attn[:, 2 * cols : 3 * cols],
+        g_attn[:, 3 * cols : 4 * cols].T,
+        mlp_grads[:hidden].astype(f32).T,
+        mlp_grads[hidden : 2 * hidden].astype(f32).T,
+        mlp_grads[2 * hidden :].astype(f32),
+        head_lines[:heads],
+        head_lines[heads:],
+        own_lines[0],
+        own_lines[1],
     )
 
 

time: 1170 us -> 1060 us (0.906)
  matrix products: 89.2 us -> 10.5 us
  other arithmetic: 113 us -> 34.8 us
  Pallas kernels: 746 us -> 820 us
  local copies, waits for them, and re-layouts: 78.2 us -> 45 us
    pallas_call x3 -> x6, Pallas kernels: 20.9 us -> 191 us  [the longest x2 134 us: last_sum(): pl.pallas_call(kernel, grid=(1,), in_specs=[vmem] * 8 + [hbm] + extra_spe...]
    pallas_call x3 -> x2, Pallas kernels: 252 us -> 167 us  [line_sum(): pl.pallas_call(functools.partial(line_kernel, n, chunks), in_specs=[pl.Bl...]
    dot_general x8 -> x0, matrix products: 62.2 us -> none  [the longest x5 34.4 us: matmul(): return jnp.dot(left, right, preferred_element_type=f32)]
    convert_element_type x8 -> x2, other arithmetic: 29.1 us -> 2.69 us  [the longest x1 2.54 us: per_device(): mlp_grads[2 * hidden:].astype(f32)]
    unnamed x244 -> x87, local copies, waits for them, and re-layouts: 55.2 us -> 36.4 us
    reduce_sum x7 -> x0, other arithmetic: 18.7 us -> none  [the longest x1 10.3 us: per_device(): ga_grad += jnp.sum(hidden_grad * attn_unit, axis=0)]
    reduce_scatter x3 -> x2, waiting for transfers between devices: 0.01 us -> 18.1 us  [scatter_low(): lax.psum_scatter(item, ('dp', 'seq'), scatter_dimension=0, tiled=True)]
    dot_general x4 -> x2, matrix products: 27 us -> 10.5 us  [right_t(): lax.dot_general(left, right, (((1,), (1,)), ((), ())), preferred_element_...]
  transfers between devices with their start and end apart: 13 -> 12, of which waited for: 4 -> 8; matrix products, arithmetic and copies ran while one was open for 13% -> 5% of each run, Pallas kernels for 27% -> 36%
where the time goes in v3:
time: 1060 us; the launch traced here: 1050 us
  Pallas kernels  820 us (77%)
  waiting for transfers between devices  100 us (9%)
  local copies, waits for them, and re-layouts  45 us (4%)
  other arithmetic  34.8 us (3%)
  between operations  14.8 us (1%)
  starting transfers between devices  13.5 us (1%)
    pallas_call x1, Pallas kernels, feed_forward(): pl.pallas_call(functools.partial(mlp_kernel, lax.axis_size('tensor'), mic...  393 us
    pallas_call x2, Pallas kernels, line_sum(): pl.pallas_call(functools.partial(line_kernel, n, chunks), in_specs=[pl.Bl...  167 us
    pallas_call x2, Pallas kernels, last_sum(): pl.pallas_call(kernel, grid=(1,), in_specs=[vmem] * 8 + [hbm] + extra_spe...  134 us
    all_gather x2, waiting for transfers between devices, gather_rows(): return lax.all_gather(item, ('dp', 'seq'), axis=0, tiled=True)  50.2 us
    pallas_call x2, Pallas kernels, attend_backward(): pl.pallas_call(functools.partial(attn_bwd_kernel, trunk_rows, n_q), grid_...  44.1 us
    unnamed x87, local copies, waits for them, and re-layouts  36.4 us
    pallas_call x2, Pallas kernels, qkv(): pl.pallas_call(functools.partial(qkv_kernel, n, rows, cols), grid=(1,), i...  31.5 us
    pallas_call x2, Pallas kernels, proj_backward(): pl.pallas_call(proj_kernel, grid=(blocks,), in_specs=[whole(m), whole(m),...  25.1 us
  transfers between devices with their start and end apart: 12, of which 8 were waited for; matrix products, arithmetic and copies ran while one was open for 5% of the time, Pallas kernels for 36%

profile of v3, /device:TPU:0, one launch (start us, length us, event | category | flops | bytes accessed | tf_op | source)
XLA Modules:
  0.0 1049.0 jit_solution(4794408859614707121)
XLA Ops:
  8.5 2.2 pad_maximum_fusion.3
  11.1 10.5 all-gather.1
  22.8 2.9 pad_maximum_fusion.refs_1_.refs_0_
  28.0 40.0 %all-gather.5.cloned.1.call-done.w.wo_t.refs_13_.refs_14_ = bf16[2048,2048]{1,0:T(8,128)(2,1)} async-done(((bf16[256,2048]{1,0:T(8,128)(2,1)}), bf16[2048,2048]{1,0:T(8,128)(2,1)}) %all-gather.5.cloned.1.call-update) | async-done | bytes 8388624 | tf_op jit(solution)/shard_map/all_gather | solution.py:1428
  68.0 16.9 %qkv.3 = (bf16[768,512]{1,0:T(8,128)(2,1)}, bf16[2,768,512]{2,1,0:T(8,128)(2,1)}, f32[2,768,512]{2,1,0:T(8,128)}, f32[16,128]{1,0:T(8,128)}) custom-call(bf16[1536,2048]{1,0:T(8,128)(2,1)} %bitcast.78, bf16[2048,2048]{1,0:T(8,128)(2,1)} %all-gather.5.cloned.1.call-done.w.wo_t.refs_13_.refs_14_, f32[1,512]{1,0:T(1,128)} %reshape.221.qg.refs_6_, ...), custom_call_target="tpu_custom_call" | custom-call | flops 16499999744 | tf_op jit(solution)/shard_map/qkv/pallas_call | solution.py:343
  84.9 3.1 collective-permute-start.1
  88.1 14.6 %qkv.2 = (bf16[768,512]{1,0:T(8,128)(2,1)}, bf16[2,768,512]{2,1,0:T(8,128)(2,1)}, f32[2,768,512]{2,1,0:T(8,128)}, f32[16,128]{1,0:T(8,128)}) custom-call(bf16[1536,2048]{1,0:T(8,128)(2,1)} %bitcast.79, bf16[2048,2048]{1,0:T(8,128)(2,1)} %all-gather.5.cloned.1.call-done.w.wo_t.refs_13_.refs_14_, f32[1,512]{1,0:T(1,128)} %reshape.221.qg.refs_6_, ...), custom_call_target="tpu_custom_call" | custom-call | flops 16499999744 | tf_op jit(solution)/shard_map/qkv/pallas_call | solution.py:343
  102.7 18.8 %collective-permute-done.1.refs_0_ = bf16[2,768,512]{2,1,0:T(8,128)(2,1)S(1)} collective-permute-done((bf16[2,768,512]{2,1,0:T(8,128)(2,1)}, bf16[2,768,512]{2,1,0:T(8,128)(2,1)S(1)}, u32[]{:S(2)}, u32[]{:S(2)}) %collective-permute-start.1) | collective-permute-done | bytes 1572896 | tf_op jit(solution)/shard_map/ppermute | solution.py:1389
  122.9 3.4 collective-permute-done.2
  126.5 1.9 pad_maximum_fusion.1.trunk.par.refs_1_
  131.2 7.3 collective-permute-start
  138.5 1.7 copy-done.5
  141.3 12.4 %attend_forward.2 = (bf16[768,512]{1,0:T(8,128)(2,1)S(1)}, f32[768,512]{1,0:T(8,128)S(1)}) custom-call(s32[3,5]{1,0:T(4,128)S(1)} %stack.5.meta, bf16[768,512]{1,0:T(8,128)(2,1)S(1)} %copy-done.22, bf16[2,1536,512]{2,1,0:T(8,128)(2,1)S(1)} %copy-done, bf16[2,1536,512]{2,1,0:T(8,128)(2,1)S(1)} %copy-done, bf16[2,768,512]{2,1,0:T(8,128)(2,1)S(1)} %copy-done.5), custom_call_target="tpu_custom_call" | custom-call | flops 13200000000 | tf_op jit(solution)/shard_map/attend_forward/pallas_call | solution.py:1331
  155.8 5.1 convolution_convert_fusion.1.part
  160.9 82.5 %line_sum.2.refs_1_.refs_6_.proj = bf16[768,2048]{1,0:T(8,128)(2,1)} custom-call(bf16[768,2048]{1,0:T(8,128)(2,1)} %convolution_convert_fusion.1.part), custom_call_target="tpu_custom_call" | custom-call | flops 93499998208 | tf_op jit(solution)/shard_map/line_sum/pallas_call | solution.py:219
  243.5 1.4 copy-done.2
  247.5 2.6 collective-permute-done.3
  250.2 1.6 broadcast_select_fusion.6
  252.9 12.4 %attend_forward.3 = (bf16[768,512]{1,0:T(8,128)(2,1)S(1)}, f32[768,512]{1,0:T(8,128)S(1)}) custom-call(s32[3,5]{1,0:T(4,128)S(1)} %stack.4.meta, bf16[768,512]{1,0:T(8,128)(2,1)S(1)} %copy-done.8, bf16[2,1536,512]{2,1,0:T(8,128)(2,1)S(1)} %pad_maximum_fusion.2.trunk.par, bf16[2,1536,512]{2,1,0:T(8,128)(2,1)S(1)} %pad_maximum_fusion.2.trunk.par, ...), custom_call_target="tpu_custom_call" | custom-call | flops 13200000000 | tf_op jit(solution)/shard_map/attend_forward/pallas_call | solution.py:1331
  266.5 5.3 convolution_convert_fusion.refs_0_
  271.8 10.2 all-gather.7.cloned.1.call-done.refs_3_
  282.0 393.1 %feed_forward.1 = (bf16[1536,2048]{1,0:T(8,128)(2,1)}, bf16[1536,2048]{1,0:T(8,128)(2,1)}, bf16[1536,2048]{1,0:T(8,128)(2,1)}, bf16[1536,2048]{1,0:T(8,128)(2,1)...) custom-call(bf16[768,2048]{1,0:T(8,128)(2,1)} %convolution_convert_f, ...), custom_call_target="tpu_custom_call" | custom-call | flops 422400000000 | tf_op jit(solution)/shard_map/feed_forward/pallas_call | solution.py:1198
  675.1 12.6 %proj_backward.2 = (bf16[768,2048]{1,0:T(8,128)(2,1)}, bf16[768,512]{1,0:T(8,128)(2,1)}, f32[8,2048]{1,0:T(8,128)}, bf16[1536,2048]{1,0:T(8,128)(2,1)}) custom-call(bf16[1536,2048]{1,0:T(8,128)(2,1)} %bitcast.65, bf16[1536,2048]{1,0:T(8,128)(2,1)} %get-tuple-element.56.back, bf16[768,2048]{1,0:T(8,128)(2,1)} %line_sum.2.refs_1_.refs_6_.proj, ...), custom_call_target="tpu_custom_call" | custom-call | flops 11000000512 | tf_op jit(solution)/shard_map/proj_backward/pallas_call | solution.py:404
  687.7 1.4 copy-done.6
  690.2 1.4 copy-done.17
  692.8 22.2 %attend_backward.2 = (f32[768,512]{1,0:T(8,128)S(1)}, f32[2,768,512]{2,1,0:T(8,128)S(1)}, bf16[2,1536,512]{2,1,0:T(8,128)(2,1)S(1)}) custom-call(s32[3,5]{1,0:T(4,128)S(1)} %stack.5.meta, bf16[768,512]{1,0:T(8,128)(2,1)S(1)} %copy-done.23, bf16[768,512]{1,0:T(8,128)(2,1)S(1)} %copy-done.15, f32[768,512]{1,0:T(8,128)S(1)} %copy-done.17, ...), custom_call_target="tpu_custom_call" | custom-call | flops 24199999488 | tf_op jit(solution)/shard_map/attend_backward/pallas_call | solution.py:1355
  715.0 1.7 copy-done.21
  717.7 1.3 broadcast_select_fusion.1
  719.1 3.7 collective-permute-done.4
  722.8 3.2 add_convert_fusion.1.refs_1_.refs_2_
  726.1 1.3 collective-permute-start.5
  727.4 12.6 %proj_backward.3 = (bf16[768,2048]{1,0:T(8,128)(2,1)}, bf16[768,512]{1,0:T(8,128)(2,1)}, f32[8,2048]{1,0:T(8,128)}, bf16[1536,2048]{1,0:T(8,128)(2,1)}) custom-call(bf16[1536,2048]{1,0:T(8,128)(2,1)} %bitcast.66, bf16[1536,2048]{1,0:T(8,128)(2,1)} %get-tuple-element.56.back, ...), custom_call_target="tpu_custom_call", output_to_operand_aliasing={{3}: (6, {})} | custom-call | flops 11000000512 | tf_op jit(solution)/shard_map/proj_backward/pallas_call | solution.py:404
  739.9 1.4 copy-done.3
  743.6 1.4 copy-done.19
  745.0 21.9 %attend_backward.3 = (f32[768,512]{1,0:T(8,128)S(1)}, f32[2,768,512]{2,1,0:T(8,128)S(1)}, bf16[2,1536,512]{2,1,0:T(8,128)(2,1)S(1)}) custom-call(s32[3,5]{1,0:T(4,128)S(1)} %copy-done.11, bf16[768,512]{1,0:T(8,128)(2,1)S(1)} %copy-done.9, bf16[768,512]{1,0:T(8,128)(2,1)S(1)} %copy-done.12, f32[768,512]{1,0:T(8,128)S(1)} %copy-done.19, ...), custom_call_target="tpu_custom_call" | custom-call | flops 24199999488 | tf_op jit(solution)/shard_map/attend_backward/pallas_call | solution.py:1355
  768.1 1.6 copy-done.20
  770.2 3.3 collective-permute-done.6
  773.4 1.8 add_convert_fusion.refs_2_
  775.3 1.3 collective-permute-start.7
  776.5 104.3 %last_sum.1 = (bf16[768,1536]{1,0:T(8,128)(2,1)}, bf16[768,2048]{1,0:T(8,128)(2,1)}, f32[16,512]{1,0:T(8,128)}, bf16[2048,2176]{1,0:T(8,128)(2,1)}) custom-call(f32[768,512]{1,0:T(8,128)} %copy-done.24, f32[2,768,512]{2,1,0:T(8,128)} %copy-done.21, bf16[2,768,512]{2,1,0:T(8,128)(2,1)} %add_convert_fusion.1.refs_1_.refs_2_, ...), custom_call_target="tpu_custom_call" | custom-call | flops 109999996928 | tf_op jit(solution)/shard_map/last_sum/pallas_call | solution.py:653
  882.0 29.8 %last_part.1 = (bf16[768,1536]{1,0:T(8,128)(2,1)}, bf16[768,2048]{1,0:T(8,128)(2,1)}, f32[16,512]{1,0:T(8,128)}, bf16[2048,2176]{1,0:T(8,128)(2,1)}) custom-call(f32[768,512]{1,0:T(8,128)} %copy-done.7, f32[2,768,512]{2,1,0:T(8,128)} %copy-done.20, bf16[2,768,512]{2,1,0:T(8,128)(2,1)} %add_convert_fusion.refs_2_, ...), custom_call_target="tpu_custom_call", output_to_operand_aliasing={{3}: (9, {})} | custom-call | flops 27499999232 | tf_op jit(solution)/shard_map/last_part/pallas_call | solution.py:653
  911.8 18.1 %reduce-scatter.3.cloned.1.call-done.refs_1_ = bf16[6144,256]{1,0:T(8,128)(2,1)} async-done(((bf16[49152,256]{1,0:T(8,128)(2,1)}), bf16[6144,256]{1,0:T(8,128)(2,1)}) %reduce-scatter.3.cloned.1.call-update) | async-done | bytes 3145744 | tf_op jit(solution)/shard_map/reduce_scatter | solution.py:1432
  929.9 84.6 %line_sum.3 = bf16[768,2048]{1,0:T(8,128)(2,1)} custom-call(bf16[768,2048]{1,0:T(8,128)(2,1)} %get-tuple-element.83.part), custom_call_target="tpu_custom_call" | custom-call | flops 93499998208 | tf_op jit(solution)/shard_map/line_sum/pallas_call | solution.py:219
  1014.5 14.7 %convert_add_fusion = f32[1536,2048]{1,0:T(8,128)} fusion(bf16[1536,2048]{1,0:T(8,128)(2,1)} %get-tuple-element.56.back, bf16[768,2048]{1,0:T(8,128)(2,1)} %line_sum.3, bf16[768,2048]{1,0:T(8,128)(2,1)S(1)} %copy-done.27, bf16[2,1,768,2048]{3,2,1,0:T(8,128)(2,1)} %param.16), kind=kLoop, calls=%fused_computation | loop fusion | flops 25165824 | bytes 31457280 | tf_op jit(solution)/shard_map/add | solution.py:1554
  1029.2 2.5 slice_convert_fusion
  1031.8 2.9 copy.99
  1034.7 1.8 copy.98
  1037.3 2.3 fusion.4
  (145 shorter events, 29.3 us)
Async XLA Ops:
  7.2 3.6 copy-start.37
  7.2 3.7 copy-start.38
  7.2 3.8 copy-start.35
  7.2 3.8 copy-start.36
  7.2 14.9 %copy-start.30 = (bf16[2048,256]{1,0:T(8,128)(2,1)S(1)}, bf16[2048,256]{1,0:T(8,128)(2,1)}, u32[]{:S(2)}) copy-start(bf16[2048,256]{1,0:T(8,128)(2,1)} %param.23) | copy-start | bytes 3145732
  7.2 15.6 %copy-start.31 = (bf16[256,2048]{1,0:T(8,128)(2,1)S(1)}, bf16[256,2048]{1,0:T(8,128)(2,1)}, u32[]{:S(2)}) copy-start(bf16[256,2048]{1,0:T(8,128)(2,1)} %param.22) | copy-start | bytes 3145732
  7.2 60.8 %all-gather.5.cloned.1.call-start = ((), (), s32[]{:S(2)}) async-start(), calls=%async_computation.2 | async-start | bytes 9437184 | tf_op jit(solution)/shard_map/all_gather | solution.py:1428
  10.8 271.3 %all-gather.7.cloned.1.call-start = ((), (), s32[]{:S(2)}) async-start(), calls=%async_computation.3 | async-start | bytes 28311552 | tf_op jit(solution)/shard_map/all_gather | solution.py:1428
  84.9 36.5 %collective-permute-start.1 = (bf16[2,768,512]{2,1,0:T(8,128)(2,1)}, bf16[2,768,512]{2,1,0:T(8,128)(2,1)S(1)}, u32[]{:S(2)}, u32[]{:S(2)}) collective-permute-start(bf16[2,768,512]{2,1,0:T(8,128)(2,1)} %get-tuple-element.53.own), channel_id=1, source_target_pairs={{0,8},{4,12},{1,9},{5,13},{2,10},{6,14},{3,11},{7,15},{16,24},{20,... | collective-permute-start | bytes 4718600 | tf_op jit(solution)/shard_map/ppermute | solution.py:1389
  102.7 20.0 %copy-start.4 = (bf16[2,768,512]{2,1,0:T(8,128)(2,1)S(1)}, bf16[2,768,512]{2,1,0:T(8,128)(2,1)}, u32[]{:S(2)}) copy-start(bf16[2,768,512]{2,1,0:T(8,128)(2,1)} %get-tuple-element.53.own) | copy-start | bytes 4718596
  121.5 1.1 copy-start.28
  122.8 3.5 collective-permute-start.2
  128.4 10.1 copy-start
  128.4 801.4 %reduce-scatter.3.cloned.1.call-start = ((), (), s32[]{:S(2)}) async-start(), calls=%async_computation.4 | async-start | bytes 28311552 | tf_op jit(solution)/shard_map/reduce_scatter | solution.py:1432
  131.2 112.3 %collective-permute-start = (bf16[2,768,512]{2,1,0:T(8,128)(2,1)}, bf16[2,768,512]{2,1,0:T(8,128)(2,1)}, u32[]{:S(2)}, u32[]{:S(2)}) collective-permute-start(bf16[2,768,512]{2,1,0:T(8,128)(2,1)} %get-tuple-element.51.own), channel_id=1, source_target_pairs={{0,8},{4,12},{1,9},{5,13},{2,10},{6,14},{3,11},{7,15},{16,24},{20,... | collective-permute-start | bytes 4718600 | tf_op jit(solution)/shard_map/ppermute | solution.py:1389
  138.5 1.7 copy-start.5
  140.2 1.2 copy-start.22
  153.8 1.1 copy-start.16
  154.9 0.9 copy-start.13
  243.5 1.4 copy-start.2
  245.0 5.1 collective-permute-start.3
  247.5 4.5 copy-start.10
  251.8 1.1 copy-start.8
  252.9 12.4 %copy-start.1 = (bf16[2,1536,512]{2,1,0:T(8,128)(2,1)}, bf16[2,1536,512]{2,1,0:T(8,128)(2,1)S(1)}, u32[]{:S(2)}) copy-start(bf16[2,1536,512]{2,1,0:T(8,128)(2,1)S(1)} %pad_maximum_fusion.2.trunk.par) | copy-start | bytes 9437188
  265.4 1.1 copy-start.18
  266.5 5.3 copy-start.14
  687.7 1.4 copy-start.6
  689.1 1.1 copy-start.15
  690.2 1.4 copy-start.17
  691.7 1.1 copy-start.23
  715.0 1.7 copy-start.21
  716.6 1.1 copy-start.24
  719.1 3.8 collective-permute-start.4
  726.1 43.7 %collective-permute-start.5 = (bf16[2,768,512]{2,1,0:T(8,128)(2,1)}, bf16[2,768,512]{2,1,0:T(8,128)(2,1)}, u32[]{:S(2)}, u32[]{:S(2)}) collective-permute-start(bf16[2,768,512]{2,1,0:T(8,128)(2,1)} %add_convert_fusion.1.refs_1_.refs_2_), channel_id=1, source_target_pairs={{8,0},{12,4},{9,1},{13,5},{10,2},{14,6},{11,3},{15,7},{24,16},{28,... | collective-permute-start | bytes 4718600 | tf_op jit(solution)/shard_map/ppermute | solution.py:1424
  727.3 12.6 %copy-start.11 = (s32[3,5]{1,0:T(4,128)S(1)}, s32[3,5]{1,0:T(4,128)}, u32[]{:S(2)}) copy-start(s32[3,5]{1,0:T(4,128)} %copy-done.10) | copy-start | bytes 184
  739.9 1.4 copy-start.3
  741.3 1.1 copy-start.9
  742.5 1.1 copy-start.12
  743.6 1.4 copy-start.19
  767.0 1.1 copy-start.7
  768.1 1.6 copy-start.20
  769.7 266.7 %reduce-scatter.5.cloned.1.call-start = ((), (), s32[]{:S(2)}) async-start(), calls=%async_computation.5 | async-start | bytes 10027008 | tf_op jit(solution)/shard_map/reduce_scatter | solution.py:1432
  770.0 3.5 collective-permute-start.6
  775.3 105.6 %collective-permute-start.7 = (bf16[2,768,512]{2,1,0:T(8,128)(2,1)}, bf16[2,768,512]{2,1,0:T(8,128)(2,1)S(1)}, u32[]{:S(2)}, u32[]{:S(2)}) collective-permute-start(bf16[2,768,512]{2,1,0:T(8,128)(2,1)} %add_convert_fusion.refs_2_), channel_id=1, source_target_pairs={{8,0},{12,4},{9,1},{13,5},{10,2},{14,6},{11,3},{15,7},{24,16},{28,... | collective-permute-start | bytes 4718600 | tf_op jit(solution)/shard_map/ppermute | solution.py:1424
  880.8 1.1 copy-start.29
  929.9 84.6 %copy-start.27 = (bf16[768,2048]{1,0:T(8,128)(2,1)S(1)}, bf16[768,2048]{1,0:T(8,128)(2,1)}, u32[]{:S(2)}) copy-start(bf16[768,2048]{1,0:T(8,128)(2,1)} %get-tuple-element.73.refs_1_) | copy-start | bytes 9437188
  1014.5 14.8 %copy-start.26 = (bf16[6144,256]{1,0:T(8,128)(2,1)S(1)}, bf16[6144,256]{1,0:T(8,128)(2,1)}, u32[]{:S(2)}) copy-start(bf16[6144,256]{1,0:T(8,128)(2,1)} %reduce-scatter.3.cloned.1.call-done.refs_1_) | copy-start | bytes 9437188
  1036.5 3.1 copy-start.25
  (3 other events, 2.2 us)
Sparse Core Ops, SparseCore 0:
  10.9 57.0 all-gather.4
  128.5 153.4 all-gather.6
  769.9 159.9 reduce-scatter.2
  933.3 73.7 reduce-scatter.4

commit v4 on v3

--- a/solution.py
+++ b/solution.py
@@ -228,6 +228,111 @@
         cost_estimate=cost(rows // 9),
         name="line_sum",
     )(part)
+
+
+def gather_kernel(dps, seqs, own, out, own_sem, recv, send):
+    chips = seqs // 2
+    dp, seq = lax.axis_index("dp"), lax.axis_index("seq")
+    chip, core = seq // 2, lax.rem(seq, 2)
+    rows = own.shape[0]
+    half = rows // 2
+    across = [lax.rem(dp + a, dps) for a in range(1, dps)]
+    along = [lax.rem(chip + b, chips) for b in range(1, chips)]
+    here = lax.axis_index("tensor")
+
+    def device(d, c, k):
+        return {"dp": d, "seq": 2 * c + k, "tensor": here}
+
+    def owner(d, c, k):
+        return d * seqs + 2 * c + k
+
+    other = device(dp, chip, 1 - core)
+    mine = owner(dp, chip, core)
+    by_dp = [device(d, chip, core) for d in across]
+    by_chip = [device(dp, c, core) for c in along]
+    sends = []
+
+    def copy(index, part, target, number, source=None):
+        at = pl.ds(pl.multiple_of(index * rows + part * half, half), half)
+        return pltpu.make_async_remote_copy(
+            src_ref=out.at[at] if source is None else source,
+            dst_ref=out.at[at],
+            send_sem=send.at[number],
+            recv_sem=recv.at[index, part],
+            device_id=target,
+            device_id_type=MESH,
+        )
+
+    def push(index, part, target):
+        source = own.at[pl.ds(part * half, half)] if index is mine else None
+        item = copy(index, part, target, len(sends), source)
+        item.start()
+        sends.append(item)
+
+    def arrived(index, part):
+        copy(index, part, other, 0).wait_recv()
+
+    at = pl.ds(pl.multiple_of(mine * rows, rows), rows)
+    place = pltpu.make_async_copy(own, out.at[at], own_sem)
+    place.start()
+    barrier = pltpu.get_barrier_semaphore()
+    neighbours = by_dp + by_chip + [other]
+    for target in neighbours:
+        pl.semaphore_signal(barrier, inc=1, device_id=target, device_id_type=MESH)
+    pl.semaphore_wait(barrier, len(neighbours))
+    for target in by_dp:
+        push(mine, 0, target)
+    for target in by_chip:
+        push(mine, 1, target)
+    for part in range(2):
+        push(mine, part, other)
+    for target in by_chip:
+        push(mine, 0, target)
+    for target in by_dp:
+        push(mine, 1, target)
+    for d in across:
+        index = owner(d, chip, core)
+        arrived(index, 0)
+        for target in by_chip + [other]:
+            push(index, 0, target)
+    for c in along:
+        index = owner(dp, c, core)
+        arrived(index, 1)
+        for target in by_dp + [other]:
+            push(index, 1, target)
+    late = [(owner(dp, c, core), 0) for c in along] + [(owner(d, chip, core), 1) for d in across]
+    late += [(owner(d, c, core), part) for d in across for c in along for part in range(2)]
+    for index, part in late:
+        arrived(index, part)
+        push(index, part, other)
+    for d in [dp] + across:
+        for c in [chip] + along:
+            for part in range(2):
+                arrived(owner(d, c, 1 - core), part)
+    place.wait()
+    for item in sends:
+        item.wait_send()
+
+
+def gather_shards(own, collective_id):
+    dps, seqs = lax.axis_size("dp"), lax.axis_size("seq")
+    chips = seqs // 2
+    rows, cols = own.shape
+    dma = pltpu.SemaphoreType.DMA
+    hbm = pl.BlockSpec(memory_space=pl.ANY)
+    sends = (dps - 1) * (1 + chips) + (chips - 1) * (1 + dps) + 2 * dps * chips
+    return pl.pallas_call(
+        functools.partial(gather_kernel, dps, seqs),
+        in_specs=[hbm],
+        out_specs=hbm,
+        out_shape=jax.ShapeDtypeStruct((dps * seqs * rows, cols), own.dtype),
+        scratch_shapes=[dma(()), dma((dps * seqs, 2)), dma((sends,))],
+        compiler_params=pltpu.CompilerParams(
+            collective_id=collective_id, has_side_effects=True, vmem_limit_bytes=60 << 20
+        ),
+        cost_estimate=cost(40),
+        name="gather_shards",
+    )(own)
 
 
 LANES = 128
@@ -430,6 +535,30 @@
         cost_estimate=cost(10),
         name="proj_backward",
     )(cot, back, proj, gain, w, layer, *earlier)
+
+
+def add_kernel(cot, back, last, *refs):
+    refs[-1][...] = cot[...].astype(f32) + back[...].astype(f32) + last[...].astype(f32)
+
+
+def add_up(cot, back, last, m, out):
+    rows, width = last.shape
+    step = math.gcd(rows, 128)
+    blocks = rows // step
+    earlier = [] if out is None else [out]
+    whole = pl.BlockSpec((step, width), lambda i: (m * blocks + i, 0))
+    return pl.pallas_call(
+        add_kernel,
+        grid=(blocks,),
+        in_specs=[whole, whole, pl.BlockSpec((step, width), lambda i: (i, 0))]
+        + [pl.BlockSpec(memory_space=pl.ANY)] * len(earlier),
+        out_specs=whole,
+        out_shape=jax.ShapeDtypeStruct(cot.shape, f32),
+        input_output_aliases={3: 0} if earlier else {},
+        compiler_params=pltpu.CompilerParams(vmem_limit_bytes=60 << 20),
+        cost_estimate=cost(6),
+        name="add_up",
+    )(cot, back, last, *earlier)
 
 
 class Grads:
@@ -1387,7 +1516,8 @@
     place = lax.axis_index("seq")
     spot = lax.rem(place, half)
     got = lax.ppermute(block, "seq", [(i, i + half) for i in range(half)])
-    mine = jnp.where(place < half, block, got if hold is None else after(got, hold))
+    got = after(got, *hold)
+    mine = jnp.where(place < half, block, got)
     parts = [mine] + [lax.ppermute(mine, "seq", group_perm(n, k)) for k in range(1, half)]
     out = []
     for source in range(half):
@@ -1395,7 +1525,7 @@
         for k in range(1, half):
             pick = jnp.where(lax.rem(spot - k + half, half) == source, parts[k], pick)
         out.append(pick)
-    return jnp.concatenate(out, axis=1)
+    return jnp.concatenate(out, axis=1), got
 
 
 def sum_over_group(grads):
@@ -1472,11 +1602,18 @@
 
     cols = w_query.shape[1]
     owners = lax.axis_size("dp") * lax.axis_size("seq")
-    w_attn = gather_rows(jnp.concatenate([w_query, w_key, w_value, w_out.T], axis=1))
     gains = [query_gain.reshape(-1), key_gain.reshape(-1), attn_gain, mlp_gain]
-    gains = lax.all_gather(jnp.concatenate(gains), ("dp", "seq"), axis=0, tiled=False)
+    gains = jnp.concatenate(gains)
+    count = gains.shape[0]
+    lines = -(-count // LANES)
+    gains = jnp.pad(gains, (0, lines * LANES - count)).reshape(lines, LANES)
+    gains = jnp.pad(gains, ((0, width // owners - lines), (0, 0)))
+    w_attn = gather_shards(
+        jnp.concatenate([w_query, w_key, w_value, w_out.T, gains], axis=1), 9
+    )
     w_own = jnp.concatenate([w_gate, w_up, w_down.T], axis=1)
-    gains = after(gains, w_own)
+    gains = w_attn[:, 4 * cols :].reshape(owners, -1, LANES)[:, :lines]
+    gains = gains.reshape(owners, lines * LANES)
     own = query_gain.size
 
     def head_gain(block):
@@ -1486,8 +1623,8 @@
     q_gain = head_gain(gains[:, :own])
     k_gain = head_gain(gains[:, own : 2 * own])
     a_gain = gains[:, 2 * own : 2 * own + attn_gain.size].reshape(-1).astype(f32)
-    m_gain = gains[:, 2 * own + attn_gain.size :].reshape(-1).astype(f32)
-    wo_t = w_attn[:, 3 * cols :]
+    m_gain = gains[:, 2 * own + attn_gain.size : count].reshape(-1).astype(f32)
+    wo_t = w_attn[:, 3 * cols : 4 * cols]
     q_gain, k_gain, a_gain = q_gain[None], k_gain[None], a_gain[None]
 
     x = tokens.reshape(micros * rows, width)
@@ -1497,7 +1634,9 @@
     )
     sources, metas, attn_lows, lses, parts, first = [], [], [], [], [], None
     for m in range(micros):
-        sources.append(fetch_sources(kv_lows[m], q_lows[1] if m == 0 else first))
+        block = kv_lows[m] if m == 0 else after(kv_lows[m], attn_lows[0])
+        source, got = fetch_sources(block, (q_lows[1], w_own) if m == 0 else (first,))
+        sources.append(source)
         metas.append(block_meta(parent_of[m, 0], seg_length[m, 0], rows, n_blocks))
         attn_low, lse = attend_forward(metas[m], q_lows[m], sources[m], kv_lows[m], trunk_rows)
         attn_lows.append(attn_low)
@@ -1505,7 +1644,7 @@
         parts.append(right_t(attn_low, wo_t).astype(bf16))
         if m == 0:
             first = line_sum(parts[0], 0)
-            w_mlp = gather_rows(after(w_own, sources[0]))
+            w_mlp = gather_rows(after(w_own, got))
     proj, _, _, layer, _, _, back, _, mlp_grads, gm_grad = feed_forward(
         parts[1], x, cot, w_mlp, a_gain, m_gain[None], first,
         micros, owners,
@@ -1531,7 +1670,8 @@
     for m in range(micros):
         got = return_to_sources(sums[m])
         if m > 0:
-            got = after(got, lasts[-1])
+            input_grad = add_up(cot, back, lasts[0], 0, None)
+            got = after(got, input_grad)
         else:
             got = after(got, dqs[-1])
             mlp_grads = after(mlp_grads.reshape(-1, mlp_grads.shape[2]), got)
@@ -1544,14 +1684,13 @@
         lasts.append(line_sum(last, 4) if m else last)
     g_attn = scatter_low(after(g_attn, mlp_grads))
     g_attn = after(g_attn, qk_grad).astype(f32)
-    last = jnp.concatenate(lasts, axis=0)
 
     lines = g_attn[:, 4 * cols :]
     share = HD // owners
     place = lax.axis_index("dp") * lax.axis_size("seq") + lax.axis_index("seq")
     head_lines = lax.dynamic_slice_in_dim(lines[: 2 * heads], place * share, share, 1)
     own_lines = lines[2 * heads : 2 * heads + 2 * attn_gain.size // LANES].reshape(2, -1)
-    input_grad = cot.astype(f32) + back.astype(f32) + last.astype(f32)
+    input_grad = add_up(cot, back, lasts[1], 1, input_grad)
     return (
         layer_out.reshape(tokens.shape),
         input_grad.reshape(tokens.shape),

time: 1060 us -> 1040 us (0.981)
  waiting for transfers between devices: 100 us -> 33.6 us
  Pallas kernels: 820 us -> 879 us
  other arithmetic: 34.8 us -> 21.7 us
    pallas_call x0 -> x3, Pallas kernels: none -> 59.7 us  [the longest x1 44 us: gather_shards(): pl.pallas_call(functools.partial(gather_kernel, dps, seqs), in_specs=[hbm...]
    all_gather x2 -> x1, waiting for transfers between devices: 50.2 us -> 0.01 us  [gather_rows(): return lax.all_gather(item, ('dp', 'seq'), axis=0, tiled=True)]
    add x1 -> x0, other arithmetic: 14.7 us -> none  [per_device(): input_grad = cot.astype(f32) + back.astype(f32) + last.astype(f32)]
    ppermute x2, starting transfers between devices: 10.4 us -> 21.1 us  [fetch_sources(): got = lax.ppermute(block, 'seq', [(i, i + half) for i in range(half)])]
    unnamed x87 -> x89, local copies, waits for them, and re-layouts: 36.4 us -> 40.8 us
  transfers between devices with their start and end apart: 12 -> 11, of which waited for: 8 -> 6; matrix products, arithmetic and copies ran while one was open for 5% -> 4% of each run, Pallas kernels for 36% -> 38%
where the time goes in v4:
time: 1040 us; the launch traced here: 1030 us
  Pallas kernels  879 us (85%)
  local copies, waits for them, and re-layouts  51.9 us (5%)
  waiting for transfers between devices  33.6 us (3%)
  starting transfers between devices  24 us (2%)
  other arithmetic  21.7 us (2%)
  between operations  14.5 us (1%)
    pallas_call x1, Pallas kernels, feed_forward(): pl.pallas_call(functools.partial(mlp_kernel, lax.axis_size('tensor'), mic...  393 us
    pallas_call x2, Pallas kernels, line_sum(): pl.pallas_call(functools.partial(line_kernel, n, chunks), in_specs=[pl.Bl...  167 us
    pallas_call x2, Pallas kernels, last_sum(): pl.pallas_call(kernel, grid=(1,), in_specs=[vmem] * 8 + [hbm] + extra_spe...  134 us
    pallas_call x2, Pallas kernels, attend_backward(): pl.pallas_call(functools.partial(attn_bwd_kernel, trunk_rows, n_q), grid_...  44.3 us
    pallas_call x1, Pallas kernels, gather_shards(): pl.pallas_call(functools.partial(gather_kernel, dps, seqs), in_specs=[hbm...  44 us
    unnamed x89, local copies, waits for them, and re-layouts  40.8 us
    pallas_call x2, Pallas kernels, qkv(): pl.pallas_call(functools.partial(qkv_kernel, n, rows, cols), grid=(1,), i...  31.6 us
    pallas_call x2, Pallas kernels, proj_backward(): pl.pallas_call(proj_kernel, grid=(blocks,), in_specs=[whole(m), whole(m),...  25.1 us
  transfers between devices with their start and end apart: 11, of which 6 were waited for; matrix products, arithmetic and copies ran while one was open for 4% of the time, Pallas kernels for 38%

profile of v4, /device:TPU:0, one launch (start us, length us, event | category | flops | bytes accessed | tf_op | source)
XLA Modules:
  0.0 1034.7 jit_solution(227110368708932205)
XLA Ops:
  13.9 44.0 %gather_shards.1.w.wo_t.refs_13_.refs_14_ = bf16[2048,2176]{1,0:T(8,128)(2,1)} custom-call(bf16[256,2176]{1,0:T(8,128)(2,1)} %copy-done.31), custom_call_target="tpu_custom_call" | custom-call | flops 44000002048 | tf_op jit(solution)/shard_map/gather_shards/pallas_call | solution.py:324
  61.1 17.1 %qkv.3 = (bf16[768,512]{1,0:T(8,128)(2,1)}, bf16[2,768,512]{2,1,0:T(8,128)(2,1)}, f32[2,768,512]{2,1,0:T(8,128)}, f32[16,128]{1,0:T(8,128)}) custom-call(bf16[1536,2048]{1,0:T(8,128)(2,1)} %bitcast.80, bf16[2048,2176]{1,0:T(8,128)(2,1)} %gather_shards.1.w.wo_t.refs_13_.refs_14_, f32[1,512]{1,0:T(1,128)} %reshape.233.qg.refs_6_, f32[1,512]{1,0:T(1,128)} %reshape.234.kg.refs_7_), custom_call_target="tpu_custom_call" | custom-call | flops 16499999744 | tf_op jit(solution)/shard_map/qkv/pallas_call | solution.py:448
  78.2 2.5 collective-permute-start
  80.8 1.5 copy.80
  82.3 3.0 pad_maximum_fusion.refs_2_.refs_0_
  85.3 14.5 %qkv.2 = (bf16[768,512]{1,0:T(8,128)(2,1)}, bf16[2,768,512]{2,1,0:T(8,128)(2,1)}, f32[2,768,512]{2,1,0:T(8,128)}, f32[16,128]{1,0:T(8,128)}) custom-call(bf16[1536,2048]{1,0:T(8,128)(2,1)} %bitcast.81, bf16[2048,2176]{1,0:T(8,128)(2,1)} %gather_shards.1.w.wo_t.refs_13_.refs_14_, f32[1,512]{1,0:T(1,128)} %reshape.233.qg.refs_6_, f32[1,512]{1,0:T(1,128)} %reshape.234.kg.refs_7_), custom_call_target="tpu_custom_call" | custom-call | flops 16499999744 | tf_op jit(solution)/shard_map/qkv/pallas_call | solution.py:448
  99.8 14.5 %collective-permute-done.refs_0_ = bf16[2,768,512]{2,1,0:T(8,128)(2,1)S(1)} collective-permute-done((bf16[2,768,512]{2,1,0:T(8,128)(2,1)}, bf16[2,768,512]{2,1,0:T(8,128)(2,1)S(1)}, u32[]{:S(2)}, u32[]{:S(2)}) %collective-permute-start) | collective-permute-done | bytes 1572896 | tf_op jit(solution)/shard_map/ppermute | solution.py:1518
  115.6 1.3 copy-done.2
  116.9 1.3 broadcast_select_fusion.5
  122.0 2.8 broadcast_select_fusion.7
  125.0 1.2 copy-done.22
  126.3 12.4 %attend_forward.2 = (bf16[768,512]{1,0:T(8,128)(2,1)S(1)}, f32[768,512]{1,0:T(8,128)S(1)}) custom-call(s32[3,5]{1,0:T(4,128)S(1)} %stack.5.meta, bf16[768,512]{1,0:T(8,128)(2,1)S(1)} %copy-done.22, bf16[2,1536,512]{2,1,0:T(8,128)(2,1)S(1)} %pad_maximum_fusion.1.trunk.par, bf16[2,1536,512]{2,1,0:T(8,128)(2,1)S(1)} %pad_maximum_fusion.1.trunk.par, ...), custom_call_target="tpu_custom_call" | custom-call | flops 13200000000 | tf_op jit(solution)/shard_map/attend_forward/pallas_call | solution.py:1460
  140.8 18.6 %collective-permute-start.2 = (bf16[2,768,512]{2,1,0:T(8,128)(2,1)}, bf16[2,768,512]{2,1,0:T(8,128)(2,1)}, u32[]{:S(2)}, u32[]{:S(2)}) collective-permute-start(bf16[2,768,512]{2,1,0:T(8,128)(2,1)} %after.11), channel_id=1, source_target_pairs={{0,8},{4,12},{1,9},{5,13},{2,10},{6,14},{3,11},{7,15},{16,24},{20,... | collective-permute-start | bytes 4718600 | tf_op jit(solution)/shard_map/ppermute | solution.py:1518
  159.4 5.1 convolution_convert_fusion.1.part
  164.5 82.3 %line_sum.2.refs_1_.refs_6_.proj = bf16[768,2048]{1,0:T(8,128)(2,1)} custom-call(bf16[768,2048]{1,0:T(8,128)(2,1)} %convolution_convert_fusion.1.part), custom_call_target="tpu_custom_call" | custom-call | flops 93499998208 | tf_op jit(solution)/shard_map/line_sum/pallas_call | solution.py:219
  246.8 1.4 copy-done.25
  248.2 1.3 broadcast_select_fusion.4
  251.8 1.5 collective-permute-done.3
  253.3 2.4 broadcast_select_fusion.6
  256.8 12.4 %attend_forward.3 = (bf16[768,512]{1,0:T(8,128)(2,1)S(1)}, f32[768,512]{1,0:T(8,128)S(1)}) custom-call(s32[3,5]{1,0:T(4,128)S(1)} %stack.4.meta, bf16[768,512]{1,0:T(8,128)(2,1)S(1)} %copy-done.7, bf16[2,1536,512]{2,1,0:T(8,128)(2,1)S(1)} %pad_maximum_fusion.2.trunk.par, bf16[2,1536,512]{2,1,0:T(8,128)(2,1)S(1)} %pad_maximum_fusion.2.trunk.par, ...), custom_call_target="tpu_custom_call" | custom-call | flops 13200000000 | tf_op jit(solution)/shard_map/attend_forward/pallas_call | solution.py:1460
  271.3 5.1 convolution_convert_fusion.refs_0_
  276.4 392.6 %feed_forward.1 = (bf16[1536,2048]{1,0:T(8,128)(2,1)}, bf16[1536,2048]{1,0:T(8,128)(2,1)}, bf16[1536,2048]{1,0:T(8,128)(2,1)}, bf16[1536,2048]{1,0:T(8,128)(2,1)...) custom-call(bf16[768,2048]{1,0:T(8,128)(2,1)} %convolution_convert_f, ...), custom_call_target="tpu_custom_call" | custom-call | flops 422400000000 | tf_op jit(solution)/shard_map/feed_forward/pallas_call | solution.py:1327
  669.0 12.5 %proj_backward.2 = (bf16[768,2048]{1,0:T(8,128)(2,1)}, bf16[768,512]{1,0:T(8,128)(2,1)}, f32[8,2048]{1,0:T(8,128)}, bf16[1536,2048]{1,0:T(8,128)(2,1)}) custom-call(bf16[1536,2048]{1,0:T(8,128)(2,1)} %bitcast.64, bf16[1536,2048]{1,0:T(8,128)(2,1)} %get-tuple-element.56.back, bf16[768,2048]{1,0:T(8,128)(2,1)} %line_sum.2.refs_1_.refs_6_.proj, ...), custom_call_target="tpu_custom_call" | custom-call | flops 11000000512 | tf_op jit(solution)/shard_map/proj_backward/pallas_call | solution.py:509
  681.5 1.4 copy-done.3
  684.0 1.4 copy-done.17
  686.6 22.4 %attend_backward.2 = (f32[768,512]{1,0:T(8,128)S(1)}, f32[2,768,512]{2,1,0:T(8,128)S(1)}, bf16[2,1536,512]{2,1,0:T(8,128)(2,1)S(1)}) custom-call(s32[3,5]{1,0:T(4,128)S(1)} %stack.5.meta, bf16[768,512]{1,0:T(8,128)(2,1)S(1)} %copy-done.23, bf16[768,512]{1,0:T(8,128)(2,1)S(1)} %copy-done.15, f32[768,512]{1,0:T(8,128)S(1)} %copy-done.17, ...), custom_call_target="tpu_custom_call" | custom-call | flops 24199999488 | tf_op jit(solution)/shard_map/attend_backward/pallas_call | solution.py:1484
  709.0 1.4 broadcast_select_fusion.1
  711.6 3.7 collective-permute-done.4
  715.4 3.2 add_convert_fusion.1.refs_1_.refs_2_
  718.6 1.3 collective-permute-start.7
  719.9 12.6 %proj_backward.3 = (bf16[768,2048]{1,0:T(8,128)(2,1)}, bf16[768,512]{1,0:T(8,128)(2,1)}, f32[8,2048]{1,0:T(8,128)}, bf16[1536,2048]{1,0:T(8,128)(2,1)}) custom-call(bf16[1536,2048]{1,0:T(8,128)(2,1)} %bitcast.65, bf16[1536,2048]{1,0:T(8,128)(2,1)} %get-tuple-element.56.back, ...), custom_call_target="tpu_custom_call", output_to_operand_aliasing={{3}: (6, {})} | custom-call | flops 11000000512 | tf_op jit(solution)/shard_map/proj_backward/pallas_call | solution.py:509
  732.4 1.4 copy-done.5
  736.1 1.4 copy-done.19
  737.5 22.0 %attend_backward.3 = (f32[768,512]{1,0:T(8,128)S(1)}, f32[2,768,512]{2,1,0:T(8,128)S(1)}, bf16[2,1536,512]{2,1,0:T(8,128)(2,1)S(1)}) custom-call(s32[3,5]{1,0:T(4,128)S(1)} %copy-done.12, bf16[768,512]{1,0:T(8,128)(2,1)S(1)} %copy-done.8, bf16[768,512]{1,0:T(8,128)(2,1)S(1)} %copy-done.13, f32[768,512]{1,0:T(8,128)S(1)} %copy-done.19, ...), custom_call_target="tpu_custom_call" | custom-call | flops 24199999488 | tf_op jit(solution)/shard_map/attend_backward/pallas_call | solution.py:1484
  760.6 1.8 copy-done.20
  762.9 3.3 collective-permute-done.5
  766.2 1.8 add_convert_fusion.refs_2_
  768.0 1.3 collective-permute-start.6
  769.2 103.3 %last_sum.1 = (bf16[768,1536]{1,0:T(8,128)(2,1)}, bf16[768,2048]{1,0:T(8,128)(2,1)}, f32[16,512]{1,0:T(8,128)}, bf16[2048,2176]{1,0:T(8,128)(2,1)}) custom-call(f32[768,512]{1,0:T(8,128)} %copy-done.24, f32[2,768,512]{2,1,0:T(8,128)} %copy-done.21, bf16[2,768,512]{2,1,0:T(8,128)(2,1)} %add_convert_fusion.1.refs_1_.refs_2_, ...), custom_call_target="tpu_custom_call" | custom-call | flops 109999996928 | tf_op jit(solution)/shard_map/last_sum/pallas_call | solution.py:782
  872.5 7.7 add_up.2.refs_1_.refs_0_
  881.4 30.7 %last_part.1 = (bf16[768,1536]{1,0:T(8,128)(2,1)}, bf16[768,2048]{1,0:T(8,128)(2,1)}, f32[16,512]{1,0:T(8,128)}, bf16[2048,2176]{1,0:T(8,128)(2,1)}) custom-call(f32[768,512]{1,0:T(8,128)} %copy-done.6, f32[2,768,512]{2,1,0:T(8,128)} %copy-done.20, bf16[2,768,512]{2,1,0:T(8,128)(2,1)} %add_convert_fusion.refs_2_, ...), custom_call_target="tpu_custom_call", output_to_operand_aliasing={{3}: (9, {})} | custom-call | flops 27499999232 | tf_op jit(solution)/shard_map/last_part/pallas_call | solution.py:782
  912.1 10.2 reduce-scatter.3.cloned.1.call-done.refs_1_
  922.3 84.4 %line_sum.3.last = bf16[768,2048]{1,0:T(8,128)(2,1)} custom-call(bf16[768,2048]{1,0:T(8,128)(2,1)} %get-tuple-element.83.part), custom_call_target="tpu_custom_call" | custom-call | flops 93499998208 | tf_op jit(solution)/shard_map/line_sum/pallas_call | solution.py:219
  1006.7 8.0 add_up.3
  1014.8 2.9 slice_convert_fusion
  1017.6 3.0 copy.85
  1020.7 1.8 copy.84
  1023.3 2.3 fusion.4
  (147 shorter events, 34.2 us)
Async XLA Ops:
  7.2 5.6 copy-start.36
  7.2 5.6 copy-start.37
  7.2 269.2 %all-gather.2.cloned.1.call-start = ((), (), s32[]{:S(2)}) async-start(), calls=%async_computation.2 | async-start | bytes 28311552 | tf_op jit(solution)/shard_map/all_gather | solution.py:1558
  12.9 1.0 copy-start.31
  78.2 36.1 %collective-permute-start = (bf16[2,768,512]{2,1,0:T(8,128)(2,1)}, bf16[2,768,512]{2,1,0:T(8,128)(2,1)S(1)}, u32[]{:S(2)}, u32[]{:S(2)}) collective-permute-start(bf16[2,768,512]{2,1,0:T(8,128)(2,1)} %get-tuple-element.53.own), channel_id=1, source_target_pairs={{0,8},{4,12},{1,9},{5,13},{2,10},{6,14},{3,11},{7,15},{16,24},{20,... | collective-permute-start | bytes 4718600 | tf_op jit(solution)/shard_map/ppermute | solution.py:1518
  114.3 1.1 copy-start.26
  115.5 1.4 copy-start.2
  115.5 806.7 %reduce-scatter.3.cloned.1.call-start = ((), (), s32[]{:S(2)}) async-start(), calls=%async_computation.3 | async-start | bytes 28311552 | tf_op jit(solution)/shard_map/reduce_scatter | solution.py:1562
  116.9 1.3 copy-start.35
  116.9 1.5 copy-start.34
  116.9 2.2 copy-start.4
  118.2 3.8 collective-permute-start.1
  124.8 1.5 copy-start.22
  125.0 13.7 %copy-start = (bf16[2,1536,512]{2,1,0:T(8,128)(2,1)}, bf16[2,1536,512]{2,1,0:T(8,128)(2,1)S(1)}, u32[]{:S(2)}) copy-start(bf16[2,1536,512]{2,1,0:T(8,128)(2,1)S(1)} %pad_maximum_fusion.1.trunk.par) | copy-start | bytes 9437188
  138.7 0.9 copy-start.9
  139.6 1.1 copy-start.16
  140.8 18.6 %copy-start.10 = (bf16[768,512]{1,0:T(8,128)(2,1)S(1)}, bf16[768,512]{1,0:T(8,128)(2,1)}, u32[]{:S(2)}) copy-start(bf16[768,512]{1,0:T(8,128)(2,1)} %copy-done.9) | copy-start | bytes 2359300
  140.8 106.1 %collective-permute-start.2 = (bf16[2,768,512]{2,1,0:T(8,128)(2,1)}, bf16[2,768,512]{2,1,0:T(8,128)(2,1)}, u32[]{:S(2)}, u32[]{:S(2)}) collective-permute-start(bf16[2,768,512]{2,1,0:T(8,128)(2,1)} %after.11), channel_id=1, source_target_pairs={{0,8},{4,12},{1,9},{5,13},{2,10},{6,14},{3,11},{7,15},{16,24},{20,... | collective-permute-start | bytes 4718600 | tf_op jit(solution)/shard_map/ppermute | solution.py:1518
  246.8 1.4 copy-start.25
  248.2 1.6 copy-start.33
  249.5 3.8 collective-permute-start.3
  251.8 4.1 copy-start.11
  255.7 1.1 copy-start.7
  256.8 12.4 %copy-start.1 = (bf16[2,1536,512]{2,1,0:T(8,128)(2,1)}, bf16[2,1536,512]{2,1,0:T(8,128)(2,1)S(1)}, u32[]{:S(2)}) copy-start(bf16[2,1536,512]{2,1,0:T(8,128)(2,1)S(1)} %pad_maximum_fusion.2.trunk.par) | copy-start | bytes 9437188
  269.2 1.1 copy-start.18
  270.4 0.9 copy-start.14
  681.5 1.4 copy-start.3
  682.9 1.1 copy-start.15
  684.0 1.4 copy-start.17
  685.4 1.1 copy-start.23
  708.9 2.1 copy-start.21
  708.9 2.7 copy-start.24
  711.6 3.8 collective-permute-start.4
  718.6 43.9 %collective-permute-start.7 = (bf16[2,768,512]{2,1,0:T(8,128)(2,1)}, bf16[2,768,512]{2,1,0:T(8,128)(2,1)}, u32[]{:S(2)}, u32[]{:S(2)}) collective-permute-start(bf16[2,768,512]{2,1,0:T(8,128)(2,1)} %add_convert_fusion.1.refs_1_.refs_2_), channel_id=1, source_target_pairs={{8,0},{12,4},{9,1},{13,5},{10,2},{14,6},{11,3},{15,7},{24,16},{28,... | collective-permute-start | bytes 4718600 | tf_op jit(solution)/shard_map/ppermute | solution.py:1554
  719.8 12.6 %copy-start.12 = (s32[3,5]{1,0:T(4,128)S(1)}, s32[3,5]{1,0:T(4,128)}, u32[]{:S(2)}) copy-start(s32[3,5]{1,0:T(4,128)} %copy-done.11) | copy-start | bytes 184
  732.4 1.4 copy-start.5
  733.8 1.1 copy-start.8
  735.0 1.1 copy-start.13
  736.1 1.4 copy-start.19
  759.5 1.1 copy-start.6
  760.6 1.8 copy-start.20
  762.5 260.0 %reduce-scatter.5.cloned.1.call-start = ((), (), s32[]{:S(2)}) async-start(), calls=%async_computation.4 | async-start | bytes 10027008 | tf_op jit(solution)/shard_map/reduce_scatter | solution.py:1562
  762.7 3.5 collective-permute-start.5
  768.0 112.3 %collective-permute-start.6 = (bf16[2,768,512]{2,1,0:T(8,128)(2,1)}, bf16[2,768,512]{2,1,0:T(8,128)(2,1)S(1)}, u32[]{:S(2)}, u32[]{:S(2)}) collective-permute-start(bf16[2,768,512]{2,1,0:T(8,128)(2,1)} %add_convert_fusion.refs_2_), channel_id=1, source_target_pairs={{8,0},{12,4},{9,1},{13,5},{10,2},{14,6},{11,3},{15,7},{24,16},{28,... | collective-permute-start | bytes 4718600 | tf_op jit(solution)/shard_map/ppermute | solution.py:1554
  880.3 1.1 copy-start.30
  1006.7 8.0 copy-start.28
  1017.6 3.0 copy-start.29
  1022.5 3.1 copy-start.27
  (1 other events, 0.6 us)
Sparse Core Ops, SparseCore 0:
  115.6 145.6 all-gather.1
  762.6 159.6 reduce-scatter.2
  925.8 73.7 reduce-scatter.4

commit v5 on v4

--- a/solution.py
+++ b/solution.py
@@ -798,10 +798,11 @@
 LINE_ROWS = 48
 ROW_STEP = 32
 LAG = 3
+PARTS = 3
 TILE = 256
 NAMES = (
     "part", "x", "cot", "w", "ga", "gm", "first", "proj", "hidden", "inner", "layer", "low",
-    "gu", "back", "pre", "grads", "gm_grad", "s", "land", "swap", "res", "acc", "h", "xin", "cin",
+    "gu", "back", "pre", "grads", "grads_down", "gm_grad", "s", "land", "swap", "res", "acc", "h", "xin", "cin",
     "wgt", "wut", "wdt", "gt", "ut", "it", "jt", "stage", "load_sem", "in_send", "in_recv", "swap_recv",
     "out_send", "out_recv", "store_sem", "w_sem", "x_sem", "c_sem", "h_sem", "y_sem", "t_sem",
     "r_sem", "g_sem",
@@ -1075,7 +1076,7 @@
         def _():
             self.acc[:, at] += value
 
-    def forward_tile(self, m, t):
+    def forward_gate(self, m, t):
         slot = lax.rem(t, 2)
         self.tile_weights(t, slot, False)
 
@@ -1084,13 +1085,19 @@
             for copy in self.store_pre(m, t - 2, slot):
                 copy.wait()
 
-        gate = matmul(self.h[...], self.wgt[slot])
+        self.gt[slot] = matmul(self.h[...], self.wgt[slot]).astype(bf16)
+
+    def forward_up(self, m, t):
+        slot = lax.rem(t, 2)
         up = matmul(self.h[...], self.wut[slot])
-        self.gt[slot] = gate.astype(bf16)
+        gate = self.gt[slot].astype(f32)
         self.ut[slot] = up.astype(bf16)
         self.it[slot] = (gate * jax.nn.sigmoid(gate) * up).astype(bf16)
         for copy in self.store_pre(m, t, slot):
             copy.start()
+
+    def forward_down(self, m, t):
+        slot = lax.rem(t, 2)
         wide = self.acc.shape[1]
         step = math.gcd(wide, 512)
         for k in range(0, wide, step):
@@ -1105,7 +1112,7 @@
             self.store_h(m, self.hidden).wait()
             self.finish(m, m > 0)
 
-    def backward_tile(self, m, t, last):
+    def backward_low(self, m, t, last):
         slot = lax.rem(t, 2)
         self.tile_weights(t, slot, last & (t == self.tiles - 1))
         for copy in self.load_pre(m, t, slot):
@@ -1131,9 +1138,12 @@
         ).astype(bf16)
         for copy in self.store_low(m, t, slot):
             copy.start()
-        wide = self.acc.shape[1]
-        step = math.gcd(wide, 512)
-        for k in range(0, wide, step):
+
+    def backward_add(self, t, second):
+        slot = lax.rem(t, 2)
+        half = self.acc.shape[1] // 2
+        step = math.gcd(half, 512)
+        for k in range(second * half, (second + 1) * half, step):
             self.add(
                 t,
                 slice(k, k + step),
@@ -1141,6 +1151,7 @@
                 + right_t(self.jt[slot], self.wut[slot, k : k + step, :]),
             )
 
+    def backward_end(self, m, t):
         @pl.when(t == self.tiles - 1)
         def _():
             for back in range(min(2, self.tiles)):
@@ -1151,6 +1162,29 @@
             self.store_layer(m).wait()
             self.finish(m, True)
 
+    def piece(self, m, forward, last, unit):
+        t, which = unit // 3, lax.rem(unit, 3)
+
+        def when(ahead, number, body):
+            @pl.when((forward if ahead else jnp.logical_not(forward)) & (which == number))
+            def _():
+                body()
+
+        when(True, 0, lambda: self.forward_gate(m, t))
+        when(True, 1, lambda: self.forward_up(m, t))
+        when(True, 2, lambda: self.forward_down(m, t))
+        when(False, 0, lambda: self.backward_low(m, t, last))
+        when(False, 1, lambda: self.backward_add(t, 0))
+
+        def rest():
+            self.backward_add(t, 1)
+            self.backward_end(m, t)
+
+        when(False, 2, rest)
+
+    def parts_by(self, step):
+        return jnp.minimum(PARTS * (step - 1), 3 * self.tiles)
+
     def load_bigs(self, source):
         return (
             pltpu.make_async_copy(source.at[self.micro(0)], self.xin, self.x_sem),
@@ -1183,6 +1217,11 @@
             self.stage.at[slot], self.grads.at[:, self.cols(w), :], self.g_sem.at[slot]
         )
 
+    def store_down(self, t, slot):
+        return pltpu.make_async_copy(
+            self.stage.at[slot], self.grads_down.at[:, self.cols(t), :], self.g_sem.at[slot]
+        )
+
     def grad_tile(self, w):
         slot = lax.rem(w, 2)
         split = 2 * self.tiles
@@ -1198,13 +1237,20 @@
 
         @pl.when(w >= 2)
         def _():
-            self.store_grads(w - 2, slot).wait()
+            self.store_grads(0, slot).wait()
 
         value = left_t(self.gt[slot], self.xin[...]) + left_t(self.ut[slot], self.cin[...])
         owners, _, wide = self.stage.shape[1:]
         for owner in range(owners):
             self.stage[slot, owner] = value[:, owner * wide : (owner + 1) * wide].astype(bf16)
-        self.store_grads(w, slot).start()
+
+        @pl.when(w < split)
+        def _():
+            self.store_grads(w, slot).start()
+
+        @pl.when(w >= split)
+        def _():
+            self.store_down(w - split, slot).start()
 
         @pl.when(w == split - 1)
         def _():
@@ -1213,8 +1259,8 @@
 
         @pl.when(w == 3 * self.tiles - 1)
         def _():
-            self.store_grads(w - 1, 1 - slot).wait()
-            self.store_grads(w, slot).wait()
+            self.store_down(0, 1 - slot).wait()
+            self.store_down(0, slot).wait()
 
     def finish(self, m, sent):
         @pl.when(sent)
@@ -1243,17 +1289,17 @@
         def _():
             self.backward_start(m)
 
-        tiled = (step >= 1) & (step <= self.tiles)
-
-        @pl.when(forward & tiled)
-        def _():
-            self.forward_tile(m, step - 1)
-
-        @pl.when(jnp.logical_not(forward) & tiled)
-        def _():
-            self.backward_tile(m, step - 1, last)
-
-        done = step == self.tiles
+        first, after_last = self.parts_by(step), self.parts_by(step + 1)
+
+        def one(unit, carry):
+            self.piece(m, forward, last, unit)
+            return carry
+
+        @pl.when(step >= 1)
+        def _():
+            lax.fori_loop(first, after_last, one, 0)
+
+        done = (first < 3 * self.tiles) & (after_last == 3 * self.tiles)
 
         @pl.when(done & (index < micros - 1))
         def _():
@@ -1273,6 +1319,7 @@
     def run(self):
         n, micros = self.chunks, self.micros
         total = 3 * micros * n
+        clocks = 1 + -(-3 * self.tiles // PARTS)
         self.begin()
 
         def clock(k, carry):
@@ -1293,7 +1340,7 @@
             def _():
                 self.job(turn // n, lax.rem(turn, n))
 
-            turn = turn - 2 * micros * n + n - self.tiles - 1
+            turn = turn - 2 * micros * n + n - clocks
 
             @pl.when((turn >= 0) & (turn < 3 * self.tiles))
             def _():
@@ -1301,7 +1348,7 @@
 
             return carry
 
-        grads_at = 2 * micros * n + LAG + self.tiles + 1
+        grads_at = 2 * micros * n + LAG + clocks
         lax.fori_loop(n, max(total + LAG, grads_at + 3 * self.tiles), clock, 0)
         for m in range(micros):
             self.settle(m)
@@ -1327,9 +1374,9 @@
     return pl.pallas_call(
         functools.partial(mlp_kernel, lax.axis_size("tensor"), micros, rows),
         in_specs=[hbm] * 4 + [vmem] * 2 + [hbm],
-        out_specs=[hbm] * 9 + [vmem],
+        out_specs=[hbm] * 10 + [vmem],
         out_shape=[wide, wide, unit, wide, wide, two, wide, two]
-        + [jax.ShapeDtypeStruct((owners, 3 * hidden, width // owners), bf16)]
+        + [jax.ShapeDtypeStruct((owners, k * hidden, width // owners), bf16) for k in (2, 1)]
         + [jax.ShapeDtypeStruct((8, width), f32)],
         scratch_shapes=[
             pltpu.VMEM((both, width), bf16),
@@ -1645,12 +1692,13 @@
         if m == 0:
             first = line_sum(parts[0], 0)
             w_mlp = gather_rows(after(w_own, got))
-    proj, _, _, layer, _, _, back, _, mlp_grads, gm_grad = feed_forward(
+    proj, _, _, layer, _, _, back, _, gu_grads, down_grads, gm_grad = feed_forward(
         parts[1], x, cot, w_mlp, a_gain, m_gain[None], first,
         micros, owners,
     )
     hidden = w_gate.shape[1]
     g_attn, qk_grad, ga_grads, layer_out = None, None, [], None
+    wide = width // owners
     proj_lows, dqs, d_owns, sums = [], [], [], []
     for m in range(micros):
         proj_low, attn_grad, grad, layer_out = proj_backward(
@@ -1674,15 +1722,16 @@
             got = after(got, input_grad)
         else:
             got = after(got, dqs[-1])
-            mlp_grads = after(mlp_grads.reshape(-1, mlp_grads.shape[2]), got)
-            mlp_grads = scatter_low(mlp_grads)
+            g_down = scatter_low(down_grads.reshape(-1, wide))
+            gu_grads = after(gu_grads.reshape(-1, wide), got, g_down)
+            gu_grads = scatter_low(gu_grads)
         extra = [*proj_lows, *attn_lows] if m == 0 else [qk_grad, *ga_grads, gm_grad]
         _, last, qk_grad, g_attn = last_sum(
             dqs[m], d_owns[m], sums[m], got, units[m], squares[m], q_gain, k_gain,
             x.reshape(micros, rows, width), extra, g_attn, w_attn, owners, 5 if m else 3,
         )
         lasts.append(line_sum(last, 4) if m else last)
-    g_attn = scatter_low(after(g_attn, mlp_grads))
+    g_attn = scatter_low(after(g_attn, gu_grads))
     g_attn = after(g_attn, qk_grad).astype(f32)
 
     lines = g_attn[:, 4 * cols :]
@@ -1698,9 +1747,9 @@
         g_attn[:, cols : 2 * cols],
         g_attn[:, 2 * cols : 3 * cols],
         g_attn[:, 3 * cols : 4 * cols].T,
-        mlp_grads[:hidden].astype(f32).T,
-        mlp_grads[hidden : 2 * hidden].astype(f32).T,
-        mlp_grads[2 * hidden :].astype(f32),
+        gu_grads[:hidden].astype(f32).T,
+        gu_grads[hidden:].astype(f32).T,
+        g_down.astype(f32),
         head_lines[:heads],
         head_lines[heads:],
         own_lines[0],

time: 1040 us -> 1010 us (0.971)
  Pallas kernels: 879 us -> 858 us
  starting transfers between devices: 24 us -> 12.9 us
    pallas_call x1, Pallas kernels: 393 us -> 374 us  [feed_forward(): pl.pallas_call(functools.partial(mlp_kernel, lax.axis_size('tensor'), mic...]
    ppermute x2, starting transfers between devices: 21.1 us -> 9.88 us  [fetch_sources(): got = lax.ppermute(block, 'seq', [(i, i + half) for i in range(half)])]
  transfers between devices with their start and end apart: 11 -> 12, of which waited for: 6 -> 6; matrix products, arithmetic and copies ran while one was open for 4% -> 4% of each run, Pallas kernels for 38% -> 42%
where the time goes in v5:
time: 1010 us; the launch traced here: 999 us
  Pallas kernels  858 us (85%)
  local copies, waits for them, and re-layouts  53.1 us (5%)
  waiting for transfers between devices  28.8 us (3%)
  other arithmetic  21.7 us (2%)
  between operations  14.6 us (1%)
  starting transfers between devices  12.9 us (1%)
  matrix products  10.2 us (1%)
    pallas_call x1, Pallas kernels, feed_forward(): pl.pallas_call(functools.partial(mlp_kernel, lax.axis_size('tensor'), mic...  374 us
    pallas_call x2, Pallas kernels, line_sum(): pl.pallas_call(functools.partial(line_kernel, n, chunks), in_specs=[pl.Bl...  164 us
    pallas_call x2, Pallas kernels, last_sum(): pl.pallas_call(kernel, grid=(1,), in_specs=[vmem] * 8 + [hbm] + extra_spe...  133 us
    pallas_call x1, Pallas kernels, gather_shards(): pl.pallas_call(functools.partial(gather_kernel, dps, seqs), in_specs=[hbm...  44 us
    pallas_call x2, Pallas kernels, attend_backward(): pl.pallas_call(functools.partial(attn_bwd_kernel, trunk_rows, n_q), grid_...  43.9 us
    unnamed x89, local copies, waits for them, and re-layouts  42.1 us
    pallas_call x2, Pallas kernels, qkv(): pl.pallas_call(functools.partial(qkv_kernel, n, rows, cols), grid=(1,), i...  31.6 us
    pallas_call x2, Pallas kernels, proj_backward(): pl.pallas_call(proj_kernel, grid=(blocks,), in_specs=[whole(m), whole(m),...  26.7 us
  transfers between devices with their start and end apart: 12, of which 6 were waited for; matrix products, arithmetic and copies ran while one was open for 4% of the time, Pallas kernels for 42%

profile of v5, /device:TPU:0, one launch (start us, length us, event | category | flops | bytes accessed | tf_op | source)
XLA Modules:
  0.0 999.0 jit_solution(11150084244935999148)
XLA Ops:
  13.9 44.0 %gather_shards.1.w.wo_t.refs_13_.refs_14_ = bf16[2048,2176]{1,0:T(8,128)(2,1)} custom-call(bf16[256,2176]{1,0:T(8,128)(2,1)} %copy-done.31), custom_call_target="tpu_custom_call" | custom-call | flops 44000002048 | tf_op jit(solution)/shard_map/gather_shards/pallas_call | solution.py:324
  61.1 17.1 %qkv.3 = (bf16[768,512]{1,0:T(8,128)(2,1)}, bf16[2,768,512]{2,1,0:T(8,128)(2,1)}, f32[2,768,512]{2,1,0:T(8,128)}, f32[16,128]{1,0:T(8,128)}) custom-call(bf16[1536,2048]{1,0:T(8,128)(2,1)} %bitcast.82, bf16[2048,2176]{1,0:T(8,128)(2,1)} %gather_shards.1.w.wo_t.refs_13_.refs_14_, f32[1,512]{1,0:T(1,128)} %reshape.237.qg.refs_6_, f32[1,512]{1,0:T(1,128)} %reshape.238.kg.refs_7_), custom_call_target="tpu_custom_call" | custom-call | flops 16499999744 | tf_op jit(solution)/shard_map/qkv/pallas_call | solution.py:448
  78.2 2.5 collective-permute-start
  80.8 1.5 copy.80
  82.3 3.0 pad_maximum_fusion.refs_2_.refs_0_
  85.3 14.5 %qkv.2 = (bf16[768,512]{1,0:T(8,128)(2,1)}, bf16[2,768,512]{2,1,0:T(8,128)(2,1)}, f32[2,768,512]{2,1,0:T(8,128)}, f32[16,128]{1,0:T(8,128)}) custom-call(bf16[1536,2048]{1,0:T(8,128)(2,1)} %bitcast.83, bf16[2048,2176]{1,0:T(8,128)(2,1)} %gather_shards.1.w.wo_t.refs_13_.refs_14_, f32[1,512]{1,0:T(1,128)} %reshape.237.qg.refs_6_, f32[1,512]{1,0:T(1,128)} %reshape.238.kg.refs_7_), custom_call_target="tpu_custom_call" | custom-call | flops 16499999744 | tf_op jit(solution)/shard_map/qkv/pallas_call | solution.py:448
  99.9 14.5 %collective-permute-done.refs_0_ = bf16[2,768,512]{2,1,0:T(8,128)(2,1)S(1)} collective-permute-done((bf16[2,768,512]{2,1,0:T(8,128)(2,1)}, bf16[2,768,512]{2,1,0:T(8,128)(2,1)S(1)}, u32[]{:S(2)}, u32[]{:S(2)}) %collective-permute-start) | collective-permute-done | bytes 1572896 | tf_op jit(solution)/shard_map/ppermute | solution.py:1565
  115.6 1.3 copy-done.2
  116.9 1.3 broadcast_select_fusion.5
  122.0 2.8 broadcast_select_fusion.7
  126.3 12.4 %attend_forward.2 = (bf16[768,512]{1,0:T(8,128)(2,1)S(1)}, f32[768,512]{1,0:T(8,128)S(1)}) custom-call(s32[3,5]{1,0:T(4,128)S(1)} %stack.5.meta, bf16[768,512]{1,0:T(8,128)(2,1)S(1)} %copy-done.22, bf16[2,1536,512]{2,1,0:T(8,128)(2,1)S(1)} %pad_maximum_fusion.1.trunk.par, bf16[2,1536,512]{2,1,0:T(8,128)(2,1)S(1)} %pad_maximum_fusion.1.trunk.par, ...), custom_call_target="tpu_custom_call" | custom-call | flops 13200000000 | tf_op jit(solution)/shard_map/attend_forward/pallas_call | solution.py:1507
  140.8 7.3 collective-permute-start.2
  148.1 5.1 convolution_convert_fusion.1.part
  153.2 82.6 %line_sum.2.refs_1_.refs_6_.proj = bf16[768,2048]{1,0:T(8,128)(2,1)} custom-call(bf16[768,2048]{1,0:T(8,128)(2,1)} %convolution_convert_fusion.1.part), custom_call_target="tpu_custom_call" | custom-call | flops 93499998208 | tf_op jit(solution)/shard_map/line_sum/pallas_call | solution.py:219
  235.8 1.4 copy-done.25
  237.2 1.3 broadcast_select_fusion.4
  240.8 1.5 collective-permute-done.3
  242.3 2.1 broadcast_select_fusion.6
  245.5 12.4 %attend_forward.3 = (bf16[768,512]{1,0:T(8,128)(2,1)S(1)}, f32[768,512]{1,0:T(8,128)S(1)}) custom-call(s32[3,5]{1,0:T(4,128)S(1)} %stack.4.meta, bf16[768,512]{1,0:T(8,128)(2,1)S(1)} %copy-done.7, bf16[2,1536,512]{2,1,0:T(8,128)(2,1)S(1)} %pad_maximum_fusion.2.trunk.par, bf16[2,1536,512]{2,1,0:T(8,128)(2,1)S(1)} %pad_maximum_fusion.2.trunk.par, ...), custom_call_target="tpu_custom_call" | custom-call | flops 13200000000 | tf_op jit(solution)/shard_map/attend_forward/pallas_call | solution.py:1507
  260.0 5.1 convolution_convert_fusion.refs_0_
  265.1 374.4 %feed_forward.1 = (bf16[1536,2048]{1,0:T(8,128)(2,1)}, bf16[1536,2048]{1,0:T(8,128)(2,1)}, bf16[1536,2048]{1,0:T(8,128)(2,1)}, bf16[1536,2048]{1,0:T(8,128)(2,1)...) custom-call(bf16[768,2048]{1,0:T(8,128)(2,1)} %convolution_convert_f, ...), custom_call_target="tpu_custom_call" | custom-call | flops 422400000000 | tf_op jit(solution)/shard_map/feed_forward/pallas_call | solution.py:1374
  639.7 13.2 %proj_backward.2 = (bf16[768,2048]{1,0:T(8,128)(2,1)}, bf16[768,512]{1,0:T(8,128)(2,1)}, f32[8,2048]{1,0:T(8,128)}, bf16[1536,2048]{1,0:T(8,128)(2,1)}) custom-call(bf16[1536,2048]{1,0:T(8,128)(2,1)} %bitcast.65, bf16[1536,2048]{1,0:T(8,128)(2,1)} %get-tuple-element.57.back, bf16[768,2048]{1,0:T(8,128)(2,1)} %line_sum.2.refs_1_.refs_6_.proj, ...), custom_call_target="tpu_custom_call" | custom-call | flops 11000000512 | tf_op jit(solution)/shard_map/proj_backward/pallas_call | solution.py:509
  652.9 1.7 copy-done.3
  654.6 1.3 copy-done.15
  655.9 1.6 copy-done.17
  658.7 21.9 %attend_backward.2 = (f32[768,512]{1,0:T(8,128)S(1)}, f32[2,768,512]{2,1,0:T(8,128)S(1)}, bf16[2,1536,512]{2,1,0:T(8,128)(2,1)S(1)}) custom-call(s32[3,5]{1,0:T(4,128)S(1)} %stack.5.meta, bf16[768,512]{1,0:T(8,128)(2,1)S(1)} %copy-done.23, bf16[768,512]{1,0:T(8,128)(2,1)S(1)} %copy-done.15, f32[768,512]{1,0:T(8,128)S(1)} %copy-done.17, ...), custom_call_target="tpu_custom_call" | custom-call | flops 24199999488 | tf_op jit(solution)/shard_map/attend_backward/pallas_call | solution.py:1531
  680.7 1.5 broadcast_select_fusion.1
  683.4 3.7 collective-permute-done.4
  687.1 3.2 add_convert_fusion.1.refs_1_.refs_2_
  690.3 1.3 collective-permute-start.7
  691.6 13.5 %proj_backward.3 = (bf16[768,2048]{1,0:T(8,128)(2,1)}, bf16[768,512]{1,0:T(8,128)(2,1)}, f32[8,2048]{1,0:T(8,128)}, bf16[1536,2048]{1,0:T(8,128)(2,1)}) custom-call(bf16[1536,2048]{1,0:T(8,128)(2,1)} %bitcast.66, bf16[1536,2048]{1,0:T(8,128)(2,1)} %get-tuple-element.57.back, ...), custom_call_target="tpu_custom_call", output_to_operand_aliasing={{3}: (6, {})} | custom-call | flops 11000000512 | tf_op jit(solution)/shard_map/proj_backward/pallas_call | solution.py:509
  705.1 1.4 copy-done.5
  708.8 1.4 copy-done.19
  710.2 21.9 %attend_backward.3 = (f32[768,512]{1,0:T(8,128)S(1)}, f32[2,768,512]{2,1,0:T(8,128)S(1)}, bf16[2,1536,512]{2,1,0:T(8,128)(2,1)S(1)}) custom-call(s32[3,5]{1,0:T(4,128)S(1)} %copy-done.12, bf16[768,512]{1,0:T(8,128)(2,1)S(1)} %copy-done.8, bf16[768,512]{1,0:T(8,128)(2,1)S(1)} %copy-done.13, f32[768,512]{1,0:T(8,128)S(1)} %copy-done.19, ...), custom_call_target="tpu_custom_call" | custom-call | flops 24199999488 | tf_op jit(solution)/shard_map/attend_backward/pallas_call | solution.py:1531
  733.3 1.7 copy-done.20
  735.0 5.2 collective-permute-done.7.refs_0_
  740.5 3.4 collective-permute-done.5
  743.9 1.8 add_convert_fusion.refs_2_
  747.0 103.2 %last_sum.1 = (bf16[768,1536]{1,0:T(8,128)(2,1)}, bf16[768,2048]{1,0:T(8,128)(2,1)}, f32[16,512]{1,0:T(8,128)}, bf16[2048,2176]{1,0:T(8,128)(2,1)}) custom-call(f32[768,512]{1,0:T(8,128)} %copy-done.24, f32[2,768,512]{2,1,0:T(8,128)} %copy-done.21, bf16[2,768,512]{2,1,0:T(8,128)(2,1)} %add_convert_fusion.1.refs_1_.refs_2_, ...), custom_call_target="tpu_custom_call" | custom-call | flops 109999996928 | tf_op jit(solution)/shard_map/last_sum/pallas_call | solution.py:782
  850.2 7.9 add_up.2.refs_1_.refs_0_
  859.3 29.7 %last_part.1 = (bf16[768,1536]{1,0:T(8,128)(2,1)}, bf16[768,2048]{1,0:T(8,128)(2,1)}, f32[16,512]{1,0:T(8,128)}, bf16[2048,2176]{1,0:T(8,128)(2,1)}) custom-call(f32[768,512]{1,0:T(8,128)} %copy-done.6, f32[2,768,512]{2,1,0:T(8,128)} %copy-done.20, bf16[2,768,512]{2,1,0:T(8,128)(2,1)} %add_convert_fusion.refs_2_, ...), custom_call_target="tpu_custom_call", output_to_operand_aliasing={{3}: (9, {})} | custom-call | flops 27499999232 | tf_op jit(solution)/shard_map/last_part/pallas_call | solution.py:782
  889.1 81.1 %line_sum.3.last = bf16[768,2048]{1,0:T(8,128)(2,1)} custom-call(bf16[768,2048]{1,0:T(8,128)(2,1)} %get-tuple-element.84.part), custom_call_target="tpu_custom_call" | custom-call | flops 93499998208 | tf_op jit(solution)/shard_map/line_sum/pallas_call | solution.py:219
  970.2 7.8 add_up.3
  978.0 1.5 convert_element_type.119
  980.4 1.6 convert_bitcast_fusion
  982.0 2.9 copy.85
  984.9 1.8 copy.84
  987.5 2.3 fusion.4
  (151 shorter events, 36.6 us)
Async XLA Ops:
  7.2 5.6 copy-start.36
  7.2 5.6 copy-start.37
  7.2 257.9 %all-gather.2.cloned.1.call-start = ((), (), s32[]{:S(2)}) async-start(), calls=%async_computation.3 | async-start | bytes 28311552 | tf_op jit(solution)/shard_map/all_gather | solution.py:1605
  12.9 1.0 copy-start.31
  78.2 36.1 %collective-permute-start = (bf16[2,768,512]{2,1,0:T(8,128)(2,1)}, bf16[2,768,512]{2,1,0:T(8,128)(2,1)S(1)}, u32[]{:S(2)}, u32[]{:S(2)}) collective-permute-start(bf16[2,768,512]{2,1,0:T(8,128)(2,1)} %get-tuple-element.54.own), channel_id=1, source_target_pairs={{0,8},{4,12},{1,9},{5,13},{2,10},{6,14},{3,11},{7,15},{16,24},{20,... | collective-permute-start | bytes 4718600 | tf_op jit(solution)/shard_map/ppermute | solution.py:1565
  114.3 1.1 copy-start.26
  115.5 1.4 copy-start.2
  115.5 624.7 %reduce-scatter.4.cloned.1.call-start = ((), (), s32[]{:S(2)}) async-start(), calls=%async_computation.4 | async-start | bytes 9437184 | tf_op jit(solution)/shard_map/reduce_scatter | solution.py:1609
  116.9 1.3 copy-start.35
  116.9 1.5 copy-start.34
  116.9 2.2 copy-start.4
  118.2 3.8 collective-permute-start.1
  124.8 1.5 copy-start.22
  125.0 13.7 %copy-start = (bf16[2,1536,512]{2,1,0:T(8,128)(2,1)}, bf16[2,1536,512]{2,1,0:T(8,128)(2,1)S(1)}, u32[]{:S(2)}) copy-start(bf16[2,1536,512]{2,1,0:T(8,128)(2,1)S(1)} %pad_maximum_fusion.1.trunk.par) | copy-start | bytes 9437188
  138.7 0.9 copy-start.9
  139.6 1.1 copy-start.16
  140.8 7.4 copy-start.10
  140.8 95.0 %collective-permute-start.2 = (bf16[2,768,512]{2,1,0:T(8,128)(2,1)}, bf16[2,768,512]{2,1,0:T(8,128)(2,1)}, u32[]{:S(2)}, u32[]{:S(2)}) collective-permute-start(bf16[2,768,512]{2,1,0:T(8,128)(2,1)} %after.11), channel_id=1, source_target_pairs={{0,8},{4,12},{1,9},{5,13},{2,10},{6,14},{3,11},{7,15},{16,24},{20,... | collective-permute-start | bytes 4718600 | tf_op jit(solution)/shard_map/ppermute | solution.py:1565
  235.8 1.4 copy-start.25
  237.2 1.6 copy-start.33
  238.5 3.8 collective-permute-start.3
  240.8 3.8 copy-start.11
  244.4 1.1 copy-start.7
  245.5 12.4 %copy-start.1 = (bf16[2,1536,512]{2,1,0:T(8,128)(2,1)}, bf16[2,1536,512]{2,1,0:T(8,128)(2,1)S(1)}, u32[]{:S(2)}) copy-start(bf16[2,1536,512]{2,1,0:T(8,128)(2,1)S(1)} %pad_maximum_fusion.2.trunk.par) | copy-start | bytes 9437188
  257.9 1.1 copy-start.18
  639.5 249.5 %reduce-scatter.6.cloned.1.call-start = ((), (), s32[]{:S(2)}) async-start(), calls=%async_computation.5 | async-start | bytes 18874368 | tf_op jit(solution)/shard_map/reduce_scatter | solution.py:1609
  652.9 1.7 copy-start.3
  654.6 1.3 copy-start.15
  655.9 1.6 copy-start.17
  657.5 1.2 copy-start.23
  680.6 2.2 copy-start.21
  680.6 2.7 copy-start.24
  683.4 3.8 collective-permute-start.4
  690.3 49.9 %collective-permute-start.7 = (bf16[2,768,512]{2,1,0:T(8,128)(2,1)}, bf16[2,768,512]{2,1,0:T(8,128)(2,1)}, u32[]{:S(2)}, u32[]{:S(2)}) collective-permute-start(bf16[2,768,512]{2,1,0:T(8,128)(2,1)} %add_convert_fusion.1.refs_1_.refs_2_), channel_id=1, source_target_pairs={{8,0},{12,4},{9,1},{13,5},{10,2},{14,6},{11,3},{15,7},{24,16},{28,... | collective-permute-start | bytes 4718600 | tf_op jit(solution)/shard_map/ppermute | solution.py:1601
  691.6 13.5 %copy-start.12 = (s32[3,5]{1,0:T(4,128)S(1)}, s32[3,5]{1,0:T(4,128)}, u32[]{:S(2)}) copy-start(s32[3,5]{1,0:T(4,128)} %copy-done.11) | copy-start | bytes 184
  705.1 1.4 copy-start.5
  706.5 1.1 copy-start.8
  707.7 1.2 copy-start.13
  708.8 1.4 copy-start.19
  732.2 1.1 copy-start.6
  733.3 1.7 copy-start.20
  740.2 246.5 %reduce-scatter.8.cloned.1.call-start = ((), (), s32[]{:S(2)}) async-start(), calls=%async_computation.6 | async-start | bytes 10027008 | tf_op jit(solution)/shard_map/reduce_scatter | solution.py:1609
  740.4 3.5 collective-permute-start.5
  745.7 112.5 %collective-permute-start.6 = (bf16[2,768,512]{2,1,0:T(8,128)(2,1)}, bf16[2,768,512]{2,1,0:T(8,128)(2,1)S(1)}, u32[]{:S(2)}, u32[]{:S(2)}) collective-permute-start(bf16[2,768,512]{2,1,0:T(8,128)(2,1)} %add_convert_fusion.refs_2_), channel_id=1, source_target_pairs={{8,0},{12,4},{9,1},{13,5},{10,2},{14,6},{11,3},{15,7},{24,16},{28,... | collective-permute-start | bytes 4718600 | tf_op jit(solution)/shard_map/ppermute | solution.py:1601
  858.2 1.1 copy-start.30
  970.2 7.8 copy-start.29
  978.0 2.3 copy-start.28
  986.7 3.1 copy-start.27
  (2 other events, 1.5 us)
Sparse Core Ops, SparseCore 0:
  115.6 145.6 all-gather.1
  639.6 85.6 reduce-scatter.3
  740.3 121.8 reduce-scatter.5
  889.2 74.9 reduce-scatter.7

commit v6 on v5

--- a/solution.py
+++ b/solution.py
@@ -531,7 +531,7 @@
             jax.ShapeDtypeStruct(cot.shape, bf16),
         ],
         input_output_aliases={6: 3} if earlier else {},
-        compiler_params=pltpu.CompilerParams(vmem_limit_bytes=60 << 20),
+        compiler_params=pltpu.CompilerParams(vmem_limit_bytes=40 << 20),
         cost_estimate=cost(10),
         name="proj_backward",
     )(cot, back, proj, gain, w, layer, *earlier)

time: 1010 us -> 1010 us (level); the launches traced: 999 us -> 1010 us
    unnamed x89 -> x109, local copies, waits for them, and re-layouts: 42.1 us -> 43.6 us
where the time goes in v6:
time: 1010 us
  Pallas kernels  857 us (85%)
  local copies, waits for them, and re-layouts  54.7 us (5%)
  waiting for transfers between devices  30 us (3%)
  starting transfers between devices  22.4 us (2%)
  other arithmetic  21.2 us (2%)
  between operations  14.6 us (1%)
  matrix products  10.2 us (1%)
    pallas_call x1, Pallas kernels, feed_forward(): pl.pallas_call(functools.partial(mlp_kernel, lax.axis_size('tensor'), mic...  374 us
    pallas_call x2, Pallas kernels, line_sum(): pl.pallas_call(functools.partial(line_kernel, n, chunks), in_specs=[pl.Bl...  165 us
    pallas_call x2, Pallas kernels, last_sum(): pl.pallas_call(kernel, grid=(1,), in_specs=[vmem] * 8 + [hbm] + extra_spe...  135 us
    pallas_call x1, Pallas kernels, gather_shards(): pl.pallas_call(functools.partial(gather_kernel, dps, seqs), in_specs=[hbm...  44 us
    pallas_call x2, Pallas kernels, attend_backward(): pl.pallas_call(functools.partial(attn_bwd_kernel, trunk_rows, n_q), grid_...  43.9 us
    unnamed x109, local copies, waits for them, and re-layouts  43.6 us
    pallas_call x2, Pallas kernels, qkv(): pl.pallas_call(functools.partial(qkv_kernel, n, rows, cols), grid=(1,), i...  31.5 us
    pallas_call x2, Pallas kernels, attend_forward(): pl.pallas_call(functools.partial(attn_fwd_kernel, trunk_rows), grid_spec=...  24.8 us
  transfers between devices with their start and end apart: 12, of which 6 were waited for; matrix products, arithmetic and copies ran while one was open for 4% of the time, Pallas kernels for 42%

profile of v6, /device:TPU:0, one launch (start us, length us, event | category | flops | bytes accessed | tf_op | source)
XLA Modules:
  0.0 1010.1 jit_solution(1314772449858324639)
XLA Ops:
  13.9 44.0 %gather_shards.1.w.wo_t.refs_13_.refs_14_ = bf16[2048,2176]{1,0:T(8,128)(2,1)} custom-call(bf16[256,2176]{1,0:T(8,128)(2,1)} %copy-done.41), custom_call_target="tpu_custom_call" | custom-call | flops 44000002048 | tf_op jit(solution)/shard_map/gather_shards/pallas_call | solution.py:324
  61.1 17.1 %qkv.3 = (bf16[768,512]{1,0:T(8,128)(2,1)}, bf16[2,768,512]{2,1,0:T(8,128)(2,1)}, f32[2,768,512]{2,1,0:T(8,128)}, f32[16,128]{1,0:T(8,128)}) custom-call(bf16[1536,2048]{1,0:T(8,128)(2,1)} %bitcast.82, bf16[2048,2176]{1,0:T(8,128)(2,1)} %gather_shards.1.w.wo_t.refs_13_.refs_14_, f32[1,512]{1,0:T(1,128)} %reshape.237.qg.refs_6_, f32[1,512]{1,0:T(1,128)} %reshape.238.kg.refs_7_), custom_call_target="tpu_custom_call" | custom-call | flops 16499999744 | tf_op jit(solution)/shard_map/qkv/pallas_call | solution.py:448
  78.2 2.5 collective-permute-start
  80.8 1.5 copy.80
  82.3 3.0 pad_maximum_fusion.refs_2_.refs_0_
  85.3 14.4 %qkv.2 = (bf16[768,512]{1,0:T(8,128)(2,1)}, bf16[2,768,512]{2,1,0:T(8,128)(2,1)}, f32[2,768,512]{2,1,0:T(8,128)}, f32[16,128]{1,0:T(8,128)}) custom-call(bf16[1536,2048]{1,0:T(8,128)(2,1)} %bitcast.83, bf16[2048,2176]{1,0:T(8,128)(2,1)} %gather_shards.1.w.wo_t.refs_13_.refs_14_, f32[1,512]{1,0:T(1,128)} %reshape.237.qg.refs_6_, f32[1,512]{1,0:T(1,128)} %reshape.238.kg.refs_7_), custom_call_target="tpu_custom_call" | custom-call | flops 16499999744 | tf_op jit(solution)/shard_map/qkv/pallas_call | solution.py:448
  99.7 14.6 %collective-permute-done.refs_0_ = bf16[2,768,512]{2,1,0:T(8,128)(2,1)S(1)} collective-permute-done((bf16[2,768,512]{2,1,0:T(8,128)(2,1)}, bf16[2,768,512]{2,1,0:T(8,128)(2,1)S(1)}, u32[]{:S(2)}, u32[]{:S(2)}) %collective-permute-start) | collective-permute-done | bytes 1572896 | tf_op jit(solution)/shard_map/ppermute | solution.py:1565
  115.6 1.3 copy-done.5
  116.9 1.3 broadcast_select_fusion.5
  122.0 2.8 broadcast_select_fusion.7
  126.3 12.4 %attend_forward.2 = (bf16[768,512]{1,0:T(8,128)(2,1)S(1)}, f32[768,512]{1,0:T(8,128)S(1)}) custom-call(s32[3,5]{1,0:T(4,128)S(1)} %stack.5.meta, bf16[768,512]{1,0:T(8,128)(2,1)S(1)} %copy-done.31, bf16[2,1536,512]{2,1,0:T(8,128)(2,1)S(1)} %pad_maximum_fusion.1.trunk.par, bf16[2,1536,512]{2,1,0:T(8,128)(2,1)S(1)} %pad_maximum_fusion.1.trunk.par, ...), custom_call_target="tpu_custom_call" | custom-call | flops 13200000000 | tf_op jit(solution)/shard_map/attend_forward/pallas_call | solution.py:1507
  140.8 16.7 %collective-permute-start.2 = (bf16[2,768,512]{2,1,0:T(8,128)(2,1)}, bf16[2,768,512]{2,1,0:T(8,128)(2,1)}, u32[]{:S(2)}, u32[]{:S(2)}) collective-permute-start(bf16[2,768,512]{2,1,0:T(8,128)(2,1)} %after.11), channel_id=1, source_target_pairs={{0,8},{4,12},{1,9},{5,13},{2,10},{6,14},{3,11},{7,15},{16,24},{20,... | collective-permute-start | bytes 4718600 | tf_op jit(solution)/shard_map/ppermute | solution.py:1565
  157.5 5.1 convolution_convert_fusion.1.part
  162.6 82.7 %line_sum.2.refs_1_.refs_6_.proj = bf16[768,2048]{1,0:T(8,128)(2,1)} custom-call(bf16[768,2048]{1,0:T(8,128)(2,1)} %convolution_convert_fusion.1.part), custom_call_target="tpu_custom_call" | custom-call | flops 93499998208 | tf_op jit(solution)/shard_map/line_sum/pallas_call | solution.py:219
  245.3 1.4 copy-done.34
  246.7 1.3 broadcast_select_fusion.4
  250.3 1.4 collective-permute-done.3
  251.6 1.6 broadcast_select_fusion.6
  254.6 12.4 %attend_forward.3 = (bf16[768,512]{1,0:T(8,128)(2,1)S(1)}, f32[768,512]{1,0:T(8,128)S(1)}) custom-call(s32[3,5]{1,0:T(4,128)S(1)} %stack.4.meta, bf16[768,512]{1,0:T(8,128)(2,1)S(1)} %copy-done.10, bf16[2,1536,512]{2,1,0:T(8,128)(2,1)S(1)} %pad_maximum_fusion.2.trunk.par, bf16[2,1536,512]{2,1,0:T(8,128)(2,1)S(1)} %pad_maximum_fusion.2.trunk.par, ...), custom_call_target="tpu_custom_call" | custom-call | flops 13200000000 | tf_op jit(solution)/shard_map/attend_forward/pallas_call | solution.py:1507
  269.1 5.1 convolution_convert_fusion.refs_0_
  274.2 374.1 %feed_forward.1 = (bf16[1536,2048]{1,0:T(8,128)(2,1)}, bf16[1536,2048]{1,0:T(8,128)(2,1)}, bf16[1536,2048]{1,0:T(8,128)(2,1)}, bf16[1536,2048]{1,0:T(8,128)(2,1)...) custom-call(bf16[768,2048]{1,0:T(8,128)(2,1)} %convolution_convert_f, ...), custom_call_target="tpu_custom_call" | custom-call | flops 422400000000 | tf_op jit(solution)/shard_map/feed_forward/pallas_call | solution.py:1374
  648.9 1.4 copy-done.3
  650.3 2.8 copy-done
  653.1 11.4 %proj_backward.2 = (bf16[768,2048]{1,0:T(8,128)(2,1)S(1)}, bf16[768,512]{1,0:T(8,128)(2,1)S(1)}, f32[8,2048]{1,0:T(8,128)S(1)}, bf16[1536,2048]{1,0:T(8,128)(2,1)}) custom-call(bf16[1536,2048]{1,0:T(8,128)(2,1)S(1)} %bitcast.65, bf16[1536,2048]{1,0:T(8,128)(2,1)} %get-tuple-element.57.back, bf16[768,2048]{1,0:T(8,128)(2,1)S(1)} %copy-done.3, ...), custom_call_target="tpu_custom_call" | custom-call | flops 11000000512 | tf_op jit(solution)/shard_map/proj_backward/pallas_call | solution.py:509
  664.5 1.6 copy-done.23
  666.1 22.0 %attend_backward.2 = (f32[768,512]{1,0:T(8,128)S(1)}, f32[2,768,512]{2,1,0:T(8,128)S(1)}, bf16[2,1536,512]{2,1,0:T(8,128)(2,1)S(1)}) custom-call(s32[3,5]{1,0:T(4,128)S(1)} %copy-done.17, bf16[768,512]{1,0:T(8,128)(2,1)S(1)} %copy-done.32, bf16[768,512]{1,0:T(8,128)(2,1)S(1)} %get-tuple-element.60.do, f32[768,512]{1,0:T(8,128)S(1)} %copy-done.25, ...), custom_call_target="tpu_custom_call" | custom-call | flops 24199999488 | tf_op jit(solution)/shard_map/attend_backward/pallas_call | solution.py:1531
  688.1 1.5 broadcast_select_fusion.1
  690.8 3.7 collective-permute-done.4
  694.5 3.2 add_convert_fusion.1.refs_1_.refs_2_
  697.7 1.3 collective-permute-start.7
  699.0 2.8 copy-done.1
  702.5 12.2 %proj_backward.3 = (bf16[768,2048]{1,0:T(8,128)(2,1)S(1)}, bf16[768,512]{1,0:T(8,128)(2,1)S(1)}, f32[8,2048]{1,0:T(8,128)S(1)}, bf16[1536,2048]{1,0:T(8,128)(2,1)}) custom-call(bf16[1536,2048]{1,0:T(8,128)(2,1)S(1)} %bitcast.66, bf16[1536,2048]{1,0:T(8,128)(2,1)} %get-tuple-element.57.back, ...), custom_call_target="tpu_custom_call", output_to_operand_aliasing={{3}: (6, {})} | custom-call | flops 11000000512 | tf_op jit(solution)/shard_map/proj_backward/pallas_call | solution.py:509
  714.7 1.7 copy-done.20
  716.3 22.0 %attend_backward.3 = (f32[768,512]{1,0:T(8,128)S(1)}, f32[2,768,512]{2,1,0:T(8,128)S(1)}, bf16[2,1536,512]{2,1,0:T(8,128)(2,1)S(1)}) custom-call(s32[3,5]{1,0:T(4,128)S(1)} %copy-done.19, bf16[768,512]{1,0:T(8,128)(2,1)S(1)} %copy-done.11, bf16[768,512]{1,0:T(8,128)(2,1)S(1)} %get-tuple-element.65.do, f32[768,512]{1,0:T(8,128)S(1)} %copy-done.27, ...), custom_call_target="tpu_custom_call" | custom-call | flops 24199999488 | tf_op jit(solution)/shard_map/attend_backward/pallas_call | solution.py:1531
  739.5 1.7 copy-done.28
  741.1 6.3 collective-permute-done.7.refs_0_
  749.0 3.4 collective-permute-done.5
  752.4 1.8 add_convert_fusion.refs_2_
  755.5 105.4 %last_sum.1 = (bf16[768,1536]{1,0:T(8,128)(2,1)}, bf16[768,2048]{1,0:T(8,128)(2,1)}, f32[16,512]{1,0:T(8,128)}, bf16[2048,2176]{1,0:T(8,128)(2,1)}) custom-call(f32[768,512]{1,0:T(8,128)} %copy-done.33, f32[2,768,512]{2,1,0:T(8,128)} %copy-done.30, bf16[2,768,512]{2,1,0:T(8,128)(2,1)} %add_convert_fusion.1.refs_1_.refs_2_, ...), custom_call_target="tpu_custom_call" | custom-call | flops 109999996928 | tf_op jit(solution)/shard_map/last_sum/pallas_call | solution.py:782
  860.9 7.7 add_up.2.refs_1_.refs_0_
  869.7 29.5 %last_part.1 = (bf16[768,1536]{1,0:T(8,128)(2,1)}, bf16[768,2048]{1,0:T(8,128)(2,1)}, f32[16,512]{1,0:T(8,128)}, bf16[2048,2176]{1,0:T(8,128)(2,1)}) custom-call(f32[768,512]{1,0:T(8,128)} %copy-done.9, f32[2,768,512]{2,1,0:T(8,128)} %copy-done.28, bf16[2,768,512]{2,1,0:T(8,128)(2,1)} %add_convert_fusion.refs_2_, ...), custom_call_target="tpu_custom_call", output_to_operand_aliasing={{3}: (9, {})} | custom-call | flops 27499999232 | tf_op jit(solution)/shard_map/last_part/pallas_call | solution.py:782
  899.3 82.1 %line_sum.3.last = bf16[768,2048]{1,0:T(8,128)(2,1)} custom-call(bf16[768,2048]{1,0:T(8,128)(2,1)} %get-tuple-element.84.part), custom_call_target="tpu_custom_call" | custom-call | flops 93499998208 | tf_op jit(solution)/shard_map/line_sum/pallas_call | solution.py:219
  981.4 7.8 add_up.3
  989.2 1.5 convert_element_type.119
  991.5 1.6 convert_bitcast_fusion
  993.2 2.9 copy.85
  996.0 1.8 copy.84
  998.6 2.3 fusion.4
  (171 shorter events, 35.5 us)
Async XLA Ops:
  7.2 5.6 copy-start.46
  7.2 5.6 copy-start.47
  7.2 267.0 %all-gather.2.cloned.1.call-start = ((), (), s32[]{:S(2)}) async-start(), calls=%async_computation.3 | async-start | bytes 28311552 | tf_op jit(solution)/shard_map/all_gather | solution.py:1605
  78.2 36.1 %collective-permute-start = (bf16[2,768,512]{2,1,0:T(8,128)(2,1)}, bf16[2,768,512]{2,1,0:T(8,128)(2,1)S(1)}, u32[]{:S(2)}, u32[]{:S(2)}) collective-permute-start(bf16[2,768,512]{2,1,0:T(8,128)(2,1)} %get-tuple-element.54.own), channel_id=1, source_target_pairs={{0,8},{4,12},{1,9},{5,13},{2,10},{6,14},{3,11},{7,15},{16,24},{20,... | collective-permute-start | bytes 4718600 | tf_op jit(solution)/shard_map/ppermute | solution.py:1565
  115.5 1.4 copy-start.5
  115.5 633.1 %reduce-scatter.4.cloned.1.call-start = ((), (), s32[]{:S(2)}) async-start(), calls=%async_computation.4 | async-start | bytes 9437184 | tf_op jit(solution)/shard_map/reduce_scatter | solution.py:1609
  116.9 1.5 copy-start.44
  116.9 2.2 copy-start.7
  118.2 3.8 collective-permute-start.1
  121.6 3.5 copy-start.16
  124.8 1.5 copy-start.31
  125.0 13.7 %copy-start.2 = (bf16[2,1536,512]{2,1,0:T(8,128)(2,1)}, bf16[2,1536,512]{2,1,0:T(8,128)(2,1)S(1)}, u32[]{:S(2)}) copy-start(bf16[2,1536,512]{2,1,0:T(8,128)(2,1)S(1)} %pad_maximum_fusion.1.trunk.par) | copy-start | bytes 9437188
  140.8 16.7 %copy-start.13 = (bf16[768,512]{1,0:T(8,128)(2,1)S(1)}, bf16[768,512]{1,0:T(8,128)(2,1)}, u32[]{:S(2)}) copy-start(bf16[768,512]{1,0:T(8,128)(2,1)} %copy-done.12) | copy-start | bytes 2359300
  140.8 104.5 %collective-permute-start.2 = (bf16[2,768,512]{2,1,0:T(8,128)(2,1)}, bf16[2,768,512]{2,1,0:T(8,128)(2,1)}, u32[]{:S(2)}, u32[]{:S(2)}) collective-permute-start(bf16[2,768,512]{2,1,0:T(8,128)(2,1)} %after.11), channel_id=1, source_target_pairs={{0,8},{4,12},{1,9},{5,13},{2,10},{6,14},{3,11},{7,15},{16,24},{20,... | collective-permute-start | bytes 4718600 | tf_op jit(solution)/shard_map/ppermute | solution.py:1565
  245.2 1.4 copy-start.34
  246.7 1.6 copy-start.43
  248.0 3.6 collective-permute-start.3
  250.3 3.2 copy-start.18
  253.2 1.4 copy-start.10
  254.6 12.4 %copy-start.4 = (bf16[2,1536,512]{2,1,0:T(8,128)(2,1)}, bf16[2,1536,512]{2,1,0:T(8,128)(2,1)S(1)}, u32[]{:S(2)}) copy-start(bf16[2,1536,512]{2,1,0:T(8,128)(2,1)S(1)} %pad_maximum_fusion.2.trunk.par) | copy-start | bytes 9437188
  648.4 1.9 copy-start.3
  648.4 1.9 copy-start.14
  648.4 250.8 %reduce-scatter.6.cloned.1.call-start = ((), (), s32[]{:S(2)}) async-start(), calls=%async_computation.5 | async-start | bytes 18874368 | tf_op jit(solution)/shard_map/reduce_scatter | solution.py:1609
  650.3 2.8 copy-start
  653.0 13.1 %copy-start.6 = (bf16[2,768,512]{2,1,0:T(8,128)(2,1)S(1)}, bf16[2,768,512]{2,1,0:T(8,128)(2,1)}, u32[]{:S(2)}) copy-start(bf16[2,768,512]{2,1,0:T(8,128)(2,1)} %get-tuple-element.54.own) | copy-start | bytes 4718596
  653.1 13.1 %copy-start.17 = (s32[3,5]{1,0:T(4,128)S(1)}, s32[3,5]{1,0:T(4,128)}, u32[]{:S(2)}) copy-start(s32[3,5]{1,0:T(4,128)} %copy-done.16) | copy-start | bytes 184
  653.1 13.1 %copy-start.25 = (f32[768,512]{1,0:T(8,128)S(1)}, f32[768,512]{1,0:T(8,128)}, u32[]{:S(2)}) copy-start(f32[768,512]{1,0:T(8,128)} %copy-done.24) | copy-start | bytes 4718596
  653.1 13.1 %copy-start.32 = (bf16[768,512]{1,0:T(8,128)(2,1)S(1)}, bf16[768,512]{1,0:T(8,128)(2,1)}, u32[]{:S(2)}) copy-start(bf16[768,512]{1,0:T(8,128)(2,1)} %get-tuple-element.53.q) | copy-start | bytes 2359300
  664.5 1.6 copy-start.23
  666.1 22.0 %copy-start.29 = (f32[8,2048]{1,0:T(8,128)}, f32[8,2048]{1,0:T(8,128)S(1)}, u32[]{:S(2)}) copy-start(f32[8,2048]{1,0:T(8,128)S(1)} %get-tuple-element.81.refs_11_) | copy-start | bytes 196612
  688.1 2.1 copy-start.30
  688.1 2.6 copy-start.33
  690.8 3.8 collective-permute-start.4
  697.7 49.8 %collective-permute-start.7 = (bf16[2,768,512]{2,1,0:T(8,128)(2,1)}, bf16[2,768,512]{2,1,0:T(8,128)(2,1)S(1)}, u32[]{:S(2)}, u32[]{:S(2)}) collective-permute-start(bf16[2,768,512]{2,1,0:T(8,128)(2,1)} %add_convert_fusion.1.refs_1_.refs_2_), channel_id=1, source_target_pairs={{8,0},{12,4},{9,1},{13,5},{10,2},{14,6},{11,3},{15,7},{24,16},{28,... | collective-permute-start | bytes 4718600 | tf_op jit(solution)/shard_map/ppermute | solution.py:1601
  699.0 2.8 copy-start.1
  702.5 13.9 %copy-start.8 = (bf16[2,768,512]{2,1,0:T(8,128)(2,1)S(1)}, bf16[2,768,512]{2,1,0:T(8,128)(2,1)}, u32[]{:S(2)}) copy-start(bf16[2,768,512]{2,1,0:T(8,128)(2,1)} %get-tuple-element.52.own) | copy-start | bytes 4718596
  702.5 13.9 %copy-start.11 = (bf16[768,512]{1,0:T(8,128)(2,1)S(1)}, bf16[768,512]{1,0:T(8,128)(2,1)}, u32[]{:S(2)}) copy-start(bf16[768,512]{1,0:T(8,128)(2,1)} %get-tuple-element.51.refs_1_.q) | copy-start | bytes 2359300
  702.5 13.9 %copy-start.19 = (s32[3,5]{1,0:T(4,128)S(1)}, s32[3,5]{1,0:T(4,128)}, u32[]{:S(2)}) copy-start(s32[3,5]{1,0:T(4,128)} %copy-done.18) | copy-start | bytes 184
  702.5 13.9 %copy-start.27 = (f32[768,512]{1,0:T(8,128)S(1)}, f32[768,512]{1,0:T(8,128)}, u32[]{:S(2)}) copy-start(f32[768,512]{1,0:T(8,128)} %copy-done.26) | copy-start | bytes 4718596
  714.7 1.7 copy-start.20
  716.3 22.0 %copy-start.21 = (f32[8,2048]{1,0:T(8,128)}, f32[8,2048]{1,0:T(8,128)S(1)}, u32[]{:S(2)}) copy-start(f32[8,2048]{1,0:T(8,128)S(1)} %get-tuple-element.82.refs_12_) | copy-start | bytes 196612
  739.5 1.7 copy-start.28
  748.7 249.2 %reduce-scatter.8.cloned.1.call-start = ((), (), s32[]{:S(2)}) async-start(), calls=%async_computation.6 | async-start | bytes 10027008 | tf_op jit(solution)/shard_map/reduce_scatter | solution.py:1609
  748.9 3.5 collective-permute-start.5
  754.2 114.4 %collective-permute-start.6 = (bf16[2,768,512]{2,1,0:T(8,128)(2,1)}, bf16[2,768,512]{2,1,0:T(8,128)(2,1)S(1)}, u32[]{:S(2)}, u32[]{:S(2)}) collective-permute-start(bf16[2,768,512]{2,1,0:T(8,128)(2,1)} %add_convert_fusion.refs_2_), channel_id=1, source_target_pairs={{8,0},{12,4},{9,1},{13,5},{10,2},{14,6},{11,3},{15,7},{24,16},{28,... | collective-permute-start | bytes 4718600 | tf_op jit(solution)/shard_map/ppermute | solution.py:1601
  981.4 7.8 copy-start.39
  989.2 2.3 copy-start.37
  997.9 3.1 copy-start.36
  (12 other events, 12.4 us)
Sparse Core Ops, SparseCore 0:
  115.6 145.6 all-gather.1
  648.5 87.0 reduce-scatter.3
  748.8 122.1 reduce-scatter.5
  899.4 73.5 reduce-scatter.7
